TPU v7x, 32 devices: a whole 2x2x4 slice. The times are simulated.
32 devices in a mesh: fsdp: 2 (over x), ctx: 8 (over z, core), tp: 2 (over y).
Axes of the slice: x: 2, y: 2, z: 4, core: 2. Of those that a mesh axis runs over, the one named last changes fastest.
Arguments:
- tokens: bfloat16 [8192, 1024], P(('fsdp', 'ctx')), may hold values from -6 to 6
- cotangent: bfloat16 [8192, 1024], P(('fsdp', 'ctx')), may hold values from -6 to 6
- lengths: int32 [2, 4], P('fsdp'), may hold values from 512 to 2048, as said below
- order: int32 [2, 4], P('fsdp'), may hold values from 0 to 3, each once within a row
- qkv_weight: float32 [1024, 3, 1024], P('fsdp', None, 'tp'), may hold values from -0.1875 to 0.1875
- attn_weight: float32 [1024, 1024], P('tp', 'fsdp'), may hold values from -4 to 4
- wide_weight: float32 [1024, 2, 2624], P('fsdp', None, 'tp'), may hold values from -0.1875 to 0.1875
- down_weight: float32 [2624, 1024], P('tp', 'fsdp'), may hold values from -0.125 to 0.125
- norm_gains: float32 [2, 1024], P(None, 'fsdp'), may hold values from 0.5 to 1.5
- qkv_mean: float32 [1024, 3, 1024], P('fsdp', None, 'tp'), may hold values from -40 to 40
- attn_mean: float32 [1024, 1024], P('tp', 'fsdp'), may hold values from -4 to 4
- wide_mean: float32 [1024, 2, 2624], P('fsdp', None, 'tp'), may hold values from -16 to 16
- down_mean: float32 [2624, 1024], P('tp', 'fsdp'), may hold values from -32 to 32
- gains_mean: float32 [2, 1024], P(None, 'fsdp'), may hold values from -40 to 40
- qkv_square: float32 [1024, 3, 1024], P('fsdp', None, 'tp'), may hold values from 40.96 to 655.36
- attn_square: float32 [1024, 1024], P('tp', 'fsdp'), may hold values from 0.18 to 2.94
- wide_square: float32 [1024, 2, 2624], P('fsdp', None, 'tp'), may hold values from 7.3728 to 120.4224
- down_square: float32 [2624, 1024], P('tp', 'fsdp'), may hold values from 24.576 to 401.408
- gains_square: float32 [2, 1024], P(None, 'fsdp'), may hold values from 40.96 to 655.36
Outputs:
- output: bfloat16 [8192, 1024], P(('fsdp', 'ctx'))
- input_grad: bfloat16 [8192, 1024], P(('fsdp', 'ctx'))
- qkv_new: float32 [1024, 3, 1024], P('fsdp', None, 'tp')
- qkv_first: float32 [1024, 3, 1024], P('fsdp', None, 'tp')
- qkv_second: float32 [1024, 3, 1024], P('fsdp', None, 'tp')
- attn_new: float32 [1024, 1024], P('tp', 'fsdp')
- attn_first: float32 [1024, 1024], P('tp', 'fsdp')
- attn_second: float32 [1024, 1024], P('tp', 'fsdp')
- wide_new: float32 [1024, 2, 2624], P('fsdp', None, 'tp')
- wide_first: float32 [1024, 2, 2624], P('fsdp', None, 'tp')
- wide_second: float32 [1024, 2, 2624], P('fsdp', None, 'tp')
- down_new: float32 [2624, 1024], P('tp', 'fsdp')
- down_first: float32 [2624, 1024], P('tp', 'fsdp')
- down_second: float32 [2624, 1024], P('tp', 'fsdp')
- gains_new: float32 [2, 1024], P(None, 'fsdp')
- gains_first: float32 [2, 1024], P(None, 'fsdp')
- gains_second: float32 [2, 1024], P(None, 'fsdp')
Inputs may be any that keep to these rules, and one draw needn't show every extreme that they name: Each row lists the lengths of one group's 4 sequences; they sum to 4096, and the largest is exactly 2048.
All inputs are finite; a program needn't handle non-finite values.
Results may differ from a plain program's by a relative error of at most 0.03.
Values may be sent and summed in bfloat16 or wider, within the bound.
A program may use at most 192 MiB of HBM per device.

v0:
```python
import jax
import jax.numpy as jnp
from jax import lax
from jax.sharding import PartitionSpec as P

D = 1024
HD = 64
FF = 2624
STEP = 10


NORM_EPS = 1e-05
ROPE_BASE = 160000.0
BETA_FIRST = 0.9
BETA_SECOND = 0.98
ADAM_EPS = 1e-06
DECAY = 0.01
RATE_ATTN = 0.5
RATE_GAIN = 0.8
MASKED = -1e30


def normalize(values):
    centered = values - jnp.mean(values, axis=1, keepdims=True)
    scaling = lax.rsqrt(jnp.mean(centered * centered, axis=1, keepdims=True) + NORM_EPS)
    return (centered * scaling, scaling)


def norm_back(grad_hat, normed, scaling):
    return scaling * (
        grad_hat
        - jnp.mean(grad_hat, axis=1, keepdims=True)
        - normed * jnp.mean(grad_hat * normed, axis=1, keepdims=True)
    )


def packed_place(local_row, device, devices, block_size):
    return (local_row // block_size * devices + device) * block_size + local_row % block_size


def sequence_of(lengths_row, order_row, places):
    count_seqs = lengths_row.shape[0]
    chosen = (order_row[:, None] == jnp.arange(count_seqs, dtype=jnp.int32)[None, :]).astype(
        jnp.int32
    )
    in_order = jnp.sum(chosen * lengths_row[None, :], axis=1)
    endings = jnp.cumsum(in_order)
    passed = (endings[None, :] <= places[:, None]).astype(jnp.int32)
    segment = jnp.sum(passed, axis=1)
    offset = jnp.sum(passed * in_order[None, :], axis=1)
    return (segment, places - offset)


def rope_tables(position, half_size):
    frequency = ROPE_BASE ** (-(2.0 * jnp.arange(half_size, dtype=jnp.float32)) / (2.0 * half_size))
    angles = position.astype(jnp.float32)[:, None] * frequency[None, :]
    return (jnp.cos(angles), jnp.sin(angles))


def rotate(values, cosine, sines):
    half_size = values.shape[-1] // 2
    first_half = values[..., :half_size]
    second_half = values[..., half_size:]
    cos_wide = cosine[:, None, :]
    sin_wide = sines[:, None, :]
    return jnp.concatenate(
        [
            first_half * cos_wide - second_half * sin_wide,
            second_half * cos_wide + first_half * sin_wide,
        ],
        axis=-1,
    )


def exact_gelu(values):
    return jax.nn.gelu(values, approximate=False)


def adam_step(weight, gradient, moment, squared, rate_now):
    first = BETA_FIRST * moment + (1.0 - BETA_FIRST) * gradient
    second = BETA_SECOND * squared + (1.0 - BETA_SECOND) * gradient * gradient
    corrected = first / (1.0 - BETA_FIRST**STEP)
    spread = jnp.sqrt(second / (1.0 - BETA_SECOND**STEP))
    return (weight - rate_now * (corrected / (spread + ADAM_EPS) + DECAY * weight), first, second)


def update_all(weights, gradients, moments, squares, rates):
    results = []
    for weight, gradient, moment, squared, rate_now in zip(
        weights, gradients, moments, squares, rates
    ):
        results.extend(adam_step(weight, gradient, moment, squared, rate_now))
    return results


def on_device(
    tokens,
    cotangent,
    lengths,
    order,
    qkv_weight,
    attn_weight,
    wide_weight,
    down_weight,
    norm_gains,
    qkv_mean,
    attn_mean,
    wide_mean,
    down_mean,
    gains_mean,
    qkv_square,
    attn_square,
    wide_square,
    down_square,
    gains_square,
):
    local_rows = tokens.shape[0]
    ctx_count = lax.axis_size("ctx")
    ctx_index = lax.axis_index("ctx")
    group_rows = local_rows * ctx_count
    block_size = local_rows // 8
    heads_here = qkv_weight.shape[2] // HD
    head_width = heads_here * HD
    scaling = HD ** (-0.5)
    lengths_row = lengths[0]
    order_row = order[0]
    local_ids = jnp.arange(local_rows, dtype=jnp.int32)
    query_seg, query_pos = sequence_of(
        lengths_row, order_row, packed_place(local_ids, ctx_index, ctx_count, block_size)
    )
    group_ids = jnp.arange(group_rows, dtype=jnp.int32)
    key_seg, key_pos = sequence_of(
        lengths_row,
        order_row,
        packed_place(group_ids % local_rows, group_ids // local_rows, ctx_count, block_size),
    )
    cosine, sines = rope_tables(query_pos, HD // 2)
    qkv_low, attn_low, wide_low, down_low, gains_low = (
        lax.all_gather(qkv_weight.astype(jnp.bfloat16), "fsdp", axis=0, tiled=True),
        lax.all_gather(attn_weight.astype(jnp.bfloat16), "fsdp", axis=1, tiled=True),
        lax.all_gather(wide_weight.astype(jnp.bfloat16), "fsdp", axis=0, tiled=True),
        lax.all_gather(down_weight.astype(jnp.bfloat16), "fsdp", axis=1, tiled=True),
        lax.all_gather(norm_gains.astype(jnp.bfloat16), "fsdp", axis=1, tiled=True),
    )
    gains = gains_low.astype(jnp.float32)
    inputs = tokens.astype(jnp.float32)
    normed_one, scaling_one = normalize(inputs)
    entry_one = (normed_one * gains[0][None, :]).astype(jnp.bfloat16)
    projected = jnp.einsum("td,dkf->tkf", entry_one, qkv_low, preferred_element_type=jnp.float32)
    shaped = projected.reshape(local_rows, 3, heads_here, HD)
    query_low = rotate(shaped[:, 0], cosine, sines).astype(jnp.bfloat16)
    key_low = rotate(shaped[:, 1], cosine, sines).astype(jnp.bfloat16)
    value_low = shaped[:, 2].astype(jnp.bfloat16)
    all_keys, all_values = (
        lax.all_gather(key_low.reshape(local_rows, head_width), "ctx", axis=0, tiled=True),
        lax.all_gather(value_low.reshape(local_rows, head_width), "ctx", axis=0, tiled=True),
    )
    key_rows = min(512, group_rows)
    key_blocks = group_rows // key_rows
    seg_blocks = key_seg.reshape(key_blocks, key_rows)

    def blocked(flat):
        return flat.reshape(key_blocks, key_rows, heads_here, HD)

    def block_scores(key_block, seg_block):
        scores = (
            jnp.einsum("qhd,khd->hqk", query_low, key_block, preferred_element_type=jnp.float32)
            * scaling
        )
        allowed = (query_seg[:, None] == seg_block[None, :])[None]
        return (jnp.where(allowed, scores, MASKED), allowed)

    def max_step(carried, block_args):
        running, summed = carried
        key_block, seg_block = block_args
        scores, allowed = block_scores(key_block, seg_block)
        highest_now = jnp.maximum(running, jnp.max(scores, axis=-1))
        summed = summed * jnp.exp(running - highest_now) + jnp.sum(
            jnp.where(allowed, jnp.exp(scores - highest_now[..., None]), 0.0), axis=-1
        )
        return ((highest_now, summed), None)

    initial = (
        jnp.full((heads_here, local_rows), MASKED, jnp.float32),
        jnp.zeros((heads_here, local_rows), jnp.float32),
    )
    (running, summed), nothing = lax.scan(max_step, initial, (blocked(all_keys), seg_blocks))
    log_total = running + jnp.log(summed)

    def value_step(accumulated, block_args):
        key_block, value_block, seg_block = block_args
        scores, allowed = block_scores(key_block, seg_block)
        weights = jnp.where(allowed, jnp.exp(scores - log_total[..., None]), 0.0).astype(
            jnp.bfloat16
        )
        return (
            accumulated
            + jnp.einsum("hqk,khd->qhd", weights, value_block, preferred_element_type=jnp.float32),
            None,
        )

    attended, nothing = lax.scan(
        value_step,
        jnp.zeros((local_rows, heads_here, HD), jnp.float32),
        (blocked(all_keys), blocked(all_values), seg_blocks),
    )
    attended_low = attended.reshape(local_rows, head_width).astype(jnp.bfloat16)
    mixed_sum = lax.psum(
        jnp.dot(attended_low, attn_low, preferred_element_type=jnp.float32).astype(jnp.bfloat16),
        "tp",
    ).astype(jnp.float32)
    middle = inputs + mixed_sum
    normed_two, scaling_two = normalize(middle)
    entry_two = (normed_two * gains[1][None, :]).astype(jnp.bfloat16)
    gate_up = jnp.einsum("td,dkf->tkf", entry_two, wide_low, preferred_element_type=jnp.float32)
    activated, gelu_pull = jax.vjp(exact_gelu, gate_up[:, 0])
    hidden_low = (activated * gate_up[:, 1]).astype(jnp.bfloat16)
    branch = lax.psum(
        jnp.dot(hidden_low, down_low, preferred_element_type=jnp.float32).astype(jnp.bfloat16), "tp"
    ).astype(jnp.float32)
    output = (middle + branch).astype(jnp.bfloat16)
    grad_out = cotangent.astype(jnp.float32)
    down_grad = jnp.einsum("tf,td->fd", hidden_low, cotangent, preferred_element_type=jnp.float32)
    hidden_grad = jnp.einsum("td,fd->tf", cotangent, down_low, preferred_element_type=jnp.float32)
    act_grad = gelu_pull(hidden_grad * gate_up[:, 1])[0]
    gate_grad = hidden_grad * activated
    gated_grad = jnp.stack([act_grad, gate_grad], axis=1).astype(jnp.bfloat16)
    wide_grad = jnp.einsum("td,tkf->dkf", entry_two, gated_grad, preferred_element_type=jnp.float32)
    back_two = lax.psum(
        jnp.einsum("tkf,dkf->td", gated_grad, wide_low, preferred_element_type=jnp.float32).astype(
            jnp.bfloat16
        ),
        "tp",
    ).astype(jnp.float32)
    gain_second = jnp.sum(back_two * normed_two, axis=0)
    middle_grad = grad_out + norm_back(back_two * gains[1][None, :], normed_two, scaling_two)
    middle_low = middle_grad.astype(jnp.bfloat16)
    attn_grad = jnp.einsum(
        "tf,td->fd", attended_low, middle_low, preferred_element_type=jnp.float32
    )
    attended_grad = (
        jnp.einsum("td,fd->tf", middle_low, attn_low, preferred_element_type=jnp.float32)
        .astype(jnp.bfloat16)
        .reshape(local_rows, heads_here, HD)
    )
    balance = jnp.sum(attended_grad.astype(jnp.float32) * attended, axis=-1).T
    back_keys, back_values = (
        lax.all_gather(key_low.reshape(local_rows, head_width), "ctx", axis=0, tiled=True),
        lax.all_gather(value_low.reshape(local_rows, head_width), "ctx", axis=0, tiled=True),
    )

    def grad_step(query_grad, block_args):
        key_block, value_block, seg_block = block_args
        scores, allowed = block_scores(key_block, seg_block)
        chances = jnp.where(allowed, jnp.exp(scores - log_total[..., None]), 0.0)
        chances_low = chances.astype(jnp.bfloat16)
        value_grad = jnp.einsum(
            "hqk,qhd->khd", chances_low, attended_grad, preferred_element_type=jnp.float32
        )
        chance_grad = jnp.einsum(
            "qhd,khd->hqk", attended_grad, value_block, preferred_element_type=jnp.float32
        )
        score_low = (chances * (chance_grad - balance[..., None])).astype(jnp.bfloat16)
        query_grad = query_grad + jnp.einsum(
            "hqk,khd->qhd", score_low, key_block, preferred_element_type=jnp.float32
        )
        key_grad = jnp.einsum(
            "hqk,qhd->khd", score_low, query_low, preferred_element_type=jnp.float32
        )
        return (query_grad, (key_grad, value_grad))

    query_grad, (key_terms, value_terms) = lax.scan(
        grad_step,
        jnp.zeros((local_rows, heads_here, HD), jnp.float32),
        (blocked(back_keys), blocked(back_values), seg_blocks),
    )
    key_grad, value_grad = (
        lax.psum_scatter(
            key_terms.reshape(group_rows, head_width).astype(jnp.bfloat16),
            "ctx",
            scatter_dimension=0,
            tiled=True,
        ).astype(jnp.float32),
        lax.psum_scatter(
            value_terms.reshape(group_rows, head_width).astype(jnp.bfloat16),
            "ctx",
            scatter_dimension=0,
            tiled=True,
        ).astype(jnp.float32),
    )
    query_raw = rotate(query_grad * scaling, cosine, -sines)
    key_raw = rotate(key_grad.reshape(local_rows, heads_here, HD) * scaling, cosine, -sines)
    projected_grad = (
        jnp.stack([query_raw, key_raw, value_grad.reshape(local_rows, heads_here, HD)], axis=1)
        .reshape(local_rows, 3, head_width)
        .astype(jnp.bfloat16)
    )
    qkv_grad = jnp.einsum(
        "td,tkf->dkf", entry_one, projected_grad, preferred_element_type=jnp.float32
    )
    back_one = lax.psum(
        jnp.einsum(
            "tkf,dkf->td", projected_grad, qkv_low, preferred_element_type=jnp.float32
        ).astype(jnp.bfloat16),
        "tp",
    ).astype(jnp.float32)
    gain_first = jnp.sum(back_one * normed_one, axis=0)
    input_grad = (
        middle_grad + norm_back(back_one * gains[0][None, :], normed_one, scaling_one)
    ).astype(jnp.bfloat16)
    gains_grad = jnp.stack([gain_first, gain_second])
    rates = (D ** (-0.5), RATE_ATTN, D ** (-0.5), FF ** (-0.5), RATE_GAIN)
    shards = (
        lax.psum_scatter(
            qkv_grad.astype(jnp.bfloat16), "fsdp", scatter_dimension=0, tiled=True
        ).astype(jnp.float32),
        lax.psum_scatter(
            attn_grad.astype(jnp.bfloat16), "fsdp", scatter_dimension=1, tiled=True
        ).astype(jnp.float32),
        lax.psum_scatter(
            wide_grad.astype(jnp.bfloat16), "fsdp", scatter_dimension=0, tiled=True
        ).astype(jnp.float32),
        lax.psum_scatter(
            down_grad.astype(jnp.bfloat16), "fsdp", scatter_dimension=1, tiled=True
        ).astype(jnp.float32),
        lax.psum_scatter(
            gains_grad.astype(jnp.bfloat16), "fsdp", scatter_dimension=1, tiled=True
        ).astype(jnp.float32),
    )
    shards = (
        lax.psum(shards[0].astype(jnp.bfloat16), "ctx").astype(jnp.float32),
        lax.psum(shards[1].astype(jnp.bfloat16), "ctx").astype(jnp.float32),
        lax.psum(shards[2].astype(jnp.bfloat16), "ctx").astype(jnp.float32),
        lax.psum(shards[3].astype(jnp.bfloat16), "ctx").astype(jnp.float32),
        lax.psum(shards[4].astype(jnp.bfloat16), "ctx").astype(jnp.float32),
    )
    final = update_all(
        (qkv_weight, attn_weight, wide_weight, down_weight, norm_gains),
        shards,
        (qkv_mean, attn_mean, wide_mean, down_mean, gains_mean),
        (qkv_square, attn_square, wide_square, down_square, gains_square),
        rates,
    )
    return (output, input_grad) + tuple(final)


def solution(mesh):
    return jax.shard_map(
        on_device,
        mesh=mesh,
        in_specs=(
            P(("fsdp", "ctx"), None),
            P(("fsdp", "ctx"), None),
            P("fsdp", None),
            P("fsdp", None),
            P("fsdp", None, "tp"),
            P("tp", "fsdp"),
            P("fsdp", None, "tp"),
            P("tp", "fsdp"),
            P(None, "fsdp"),
            P("fsdp", None, "tp"),
            P("tp", "fsdp"),
            P("fsdp", None, "tp"),
            P("tp", "fsdp"),
            P(None, "fsdp"),
            P("fsdp", None, "tp"),
            P("tp", "fsdp"),
            P("fsdp", None, "tp"),
            P("tp", "fsdp"),
            P(None, "fsdp"),
        ),
        out_specs=(
            P(("fsdp", "ctx"), None),
            P(("fsdp", "ctx"), None),
            P("fsdp", None, "tp"),
            P("fsdp", None, "tp"),
            P("fsdp", None, "tp"),
            P("tp", "fsdp"),
            P("tp", "fsdp"),
            P("tp", "fsdp"),
            P("fsdp", None, "tp"),
            P("fsdp", None, "tp"),
            P("fsdp", None, "tp"),
            P("tp", "fsdp"),
            P("tp", "fsdp"),
            P("tp", "fsdp"),
            P(None, "fsdp"),
            P(None, "fsdp"),
            P(None, "fsdp"),
        ),
        check_vma=False,
    )
```

profile of v0, /device:TPU:0, one launch (start us, length us, event | category | flops | bytes accessed | tf_op | source)
XLA Modules:
  0.0 1158.6 jit_solution(12870898784141633112)
XLA Ops:
  10.5 5.2 all_gather.23
  16.4 41.8 %all-gather.7.cloned.1.call-done = bf16[1024,3,512]{0,2,1:T(8,128)(2,1)} async-done(((bf16[512,3,512]{0,2,1:T(8,128)(2,1)}), bf16[1024,3,512]{0,2,1:T(8,128)(2,1)}) %all-gather.7.cloned.1.call-update) | async-done | bytes 3145744 | tf_op jit(solution)/shard_map/all_gather | solution.py:139
  73.9 38.1 %all-gather.9.cloned.1.call-done = bf16[4096,512]{0,1:T(8,128)(2,1)} async-done(((bf16[512,512]{0,1:T(8,128)(2,1)}), bf16[4096,512]{0,1:T(8,128)(2,1)}) %all-gather.9.cloned.1.call-update) | async-done | bytes 4194320 | tf_op jit(solution)/shard_map/all_gather | solution.py:156
  112.0 4.4 copy.109
  119.9 40.2 %all-gather.11.cloned.1.call-done = bf16[4096,512]{0,1:T(8,128)(2,1)} async-done(((bf16[512,512]{0,1:T(8,128)(2,1)}), bf16[4096,512]{0,1:T(8,128)(2,1)}) %all-gather.11.cloned.1.call-update) | async-done | bytes 4194320 | tf_op jit(solution)/shard_map/all_gather | solution.py:155
  160.1 4.4 copy.110
  168.0 84.8 %while.39 = (s32[]{:T(128)}, f32[8,512]{1,0:T(8,128)S(1)}, f32[8,512]{1,0:T(8,128)S(1)}, s32[512]{0:T(512)S(1)}, s32[8,512]{1,0:T(8,128)S(1)}, /*index=5*/bf16[8...) while((s32[]{:T(128)}, f32[8,512]{1,0:T(8,128)S(1)}, ...), condition=%wide.region_10.11_spmd.clone, body=%wide.region_7.10_spmd.clone.sunk | while | flops 285495296 | bytes 18833528 | solution.py:187
  168.4 5.8 fusion.223
  174.3 4.5 select_reduce_fusion.3
  179.0 5.8 fusion.223
  184.8 4.5 select_reduce_fusion.3
  189.6 5.8 fusion.223
  195.5 4.5 select_reduce_fusion.3
  200.2 5.8 fusion.223
  206.0 4.5 select_reduce_fusion.3
  210.8 5.8 fusion.223
  216.6 4.5 select_reduce_fusion.3
  221.3 5.8 fusion.223
  227.1 4.5 select_reduce_fusion.3
  231.9 5.8 fusion.223
  237.7 4.5 select_reduce_fusion.3
  242.5 5.8 fusion.223
  248.3 4.5 select_reduce_fusion.3
  252.8 36.6 %while.40 = (s32[]{:T(128)}, f32[512,8,64]{0,2,1:T(8,128)S(1)}, bf16[8,512,8,64]{1,3,2,0:T(8,128)(2,1)}, s32[512]{0:T(512)S(1)}, s32[8,512]{1,0:T(8,128)S(1)}, /...) while((s32[]{:T(128)}, f32[512,8,64]{0,2,1:T(8,128)S(1)}, ...), condition=%wide.region_12.13_spmd.clone, body=%wide.region_11.12_spmd.clone.sunk | while | flops 548143104 | bytes 4220538 | solution.py:202
  253.1 4.3 fusion.229
  257.6 4.3 fusion.229
  262.2 4.3 fusion.229
  293.0 4.4 convert_element_type.185
  298.7 4.9 fusion.176
  303.6 28.9 %all-reduce.7.cloned.1.call-done = bf16[512,1024]{1,0:T(8,128)(2,1)} async-done(((bf16[512,1024]{1,0:T(8,128)(2,1)}), bf16[512,1024]{1,0:T(8,128)(2,1)}) %all-reduce.7.cloned.1.call-update) | async-done | bytes 1048592 | tf_op jit(solution)/shard_map/psum | solution.py:208
  334.6 70.1 %all-gather.15.cloned.1.call-done = bf16[1024,2,1312]{0,2,1:T(8,128)(2,1)} async-done(((bf16[512,2,1312]{0,2,1:T(8,128)(2,1)}), bf16[1024,2,1312]{0,2,1:T(8,128)(2,1)}) %all-gather.15.cloned.1.call-update) | async-done | bytes 5373968 | tf_op jit(solution)/shard_map/all_gather | solution.py:141
  404.7 6.0 fusion.124
  410.7 6.4 fusion.113
  425.1 40.1 %all-reduce.9.cloned.1.call-done = bf16[512,1024]{1,0:T(8,128)(2,1)} async-done(((bf16[512,1024]{1,0:T(8,128)(2,1)}), bf16[512,1024]{1,0:T(8,128)(2,1)}) %all-reduce.9.cloned.1.call-update) | async-done | bytes 1048592 | tf_op jit(solution)/shard_map/psum | solution.py:229
  471.1 143.1 %while.41 = (s32[]{:T(128)}, f32[512,8,64]{0,2,1:T(8,128)S(1)}, bf16[8,512,8,64]{1,3,2,0:T(8,128)(2,1)}, bf16[8,512,8,64]{1,3,2,0:T(8,128)(2,1)}, bf16[8,512,8,6...) while((s32[]{:T(128)}, f32[512,8,64]{0,2,1:T(8,128)S(1)}, ...), condition=%wide.region_22.23_spmd.clone, body=%wide.region_21.22_spmd.clone.sunk | while | flops 1368129536 | bytes 130343176 | solution.py:272
  473.9 6.0 fusion.241
  491.8 6.0 fusion.241
  509.7 6.0 fusion.241
  527.5 6.0 fusion.241
  545.4 6.0 fusion.241
  563.2 6.0 fusion.241
  581.1 6.0 fusion.241
  598.9 6.0 fusion.241
  614.2 4.7 copy.91
  623.3 10.5 copy.104
  633.7 11.8 %reshape.407 = bf16[4096,512]{1,0:T(8,128)(2,1)} reshape(bf16[8,512,8,64]{3,2,1,0:T(8,128)(2,1)} %copy.104) | data formatting | bytes 8388608 | tf_op jit(solution)/shard_map/convert_element_type | solution.py:285
  645.6 5.0 convolution_convert_fusion.3
  651.7 21.7 %reduce-scatter.10.cloned.1.call-done = bf16[512,512]{0,1:T(8,128)(2,1)} async-done(((bf16[4096,512]{0,1:T(8,128)(2,1)}), bf16[512,512]{0,1:T(8,128)(2,1)}) %reduce-scatter.10.cloned.1.call-update) | async-done | bytes 524304 | tf_op jit(solution)/shard_map/reduce_scatter | solution.py:278
  676.7 47.6 %reduce-scatter.12.cloned.1.call-done = bf16[512,512]{1,0:T(8,128)(2,1)} async-done(((bf16[4096,512]{1,0:T(8,128)(2,1)}), bf16[512,512]{1,0:T(8,128)(2,1)}) %reduce-scatter.12.cloned.1.call-update) | async-done | bytes 524304 | tf_op jit(solution)/shard_map/reduce_scatter | solution.py:284
  724.3 4.8 bitcast_convert_fusion
  733.5 4.7 convolution_convert_fusion.1
  738.3 7.6 convolution_convert_fusion
  746.6 5.0 convolution_convert_fusion.2
  751.8 38.8 %all-reduce.13.cloned.1.call-done = (bf16[512,1024]{1,0:T(8,128)(2,1)}, bf16[512,1024]{1,0:T(8,128)(2,1)}) async-done(((bf16[512,1024]{1,0:T(8,128)(2,1)}, bf16[512,1024]{1,0:T(8,128)(2,1)}), (bf16[512,1024]{1,0:T(8,128)(2,1)}, bf16[512,1024]{1,0:T(8,128)(2,1)})) %all-reduce.13.cloned.1.call-update) | async-done | bytes 2097168 | tf_op jit(solution)/shard_map/psum | solution.py:218
  793.7 19.9 %reduce-scatter.16.cloned.1.call-done = bf16[512,512]{1,0:T(8,128)(2,1)} async-done(((bf16[512,1024]{1,0:T(8,128)(2,1)}), bf16[512,512]{1,0:T(8,128)(2,1)}) %reduce-scatter.16.cloned.1.call-update) | async-done | bytes 524304 | tf_op jit(solution)/shard_map/reduce_scatter | solution.py:317
  813.7 41.2 %reduce-scatter.20.cloned.1.call-done = bf16[1312,512]{1,0:T(8,128)(2,1)} async-done(((bf16[1312,1024]{1,0:T(8,128)(2,1)}), bf16[1312,512]{1,0:T(8,128)(2,1)}) %reduce-scatter.20.cloned.1.call-update) | async-done | bytes 1343504 | tf_op jit(solution)/shard_map/reduce_scatter | solution.py:323
  854.8 70.0 %reduce-scatter.18.cloned.1.call-done = bf16[512,2,1312]{0,2,1:T(8,128)(2,1)} async-done(((bf16[1024,2,1312]{0,2,1:T(8,128)(2,1)}), bf16[512,2,1312]{0,2,1:T(8,128)(2,1)}) %reduce-scatter.18.cloned.1.call-update) | async-done | bytes 2686992 | tf_op jit(solution)/shard_map/reduce_scatter | solution.py:320
  924.8 46.0 %reduce-scatter.14.cloned.1.call-done = bf16[512,3,512]{2,0,1:T(8,128)(2,1)} async-done(((bf16[1024,3,512]{2,0,1:T(8,128)(2,1)}), bf16[512,3,512]{2,0,1:T(8,128)(2,1)}) %reduce-scatter.14.cloned.1.call-update) | async-done | bytes 1572880 | tf_op jit(solution)/shard_map/reduce_scatter | solution.py:314
  975.1 10.2 reduce-scatter.22.cloned.1.call-done
  986.3 16.7 %psum.71 = bf16[2,512]{1,0:T(2,128)(2,1)S(1)} all-reduce(bf16[2,512]{1,0:T(2,128)(2,1)S(1)} %copy.107), channel_id=1, replica_groups=mesh['fsdp'=2,'ctx'=8,'tp'=2] {'ctx'}, use_global_device_ids=true, to_apply=%region_39.40 | all-reduce | flops 1024 | bytes 4096 | tf_op jit(solution)/shard_map/psum | solution.py:335
  1003.6 118.8 %all-reduce.11.cloned.1.call-done = (bf16[512,3,512]{2,0,1:T(8,128)(2,1)}, bf16[512,512]{1,0:T(8,128)(2,1)}, bf16[512,2,1312]{0,2,1:T(8,128)(2,1)}, bf16[1312,512]{1,0:T(8,128)(2,1)}) async-done(((bf16[512,3,512]{2,0,1:T(8,128)(2,1)}, bf16[512,512]{1,0:T(8,128)(2,1)}, bf16[512,2,1312]{0,2,1:T(8,128)(2,1)}, bf16[1312,512]{1,0:T(8,128)(2,1)}), (bf16[512,3,512]{2,0,1:T(8,128)(2,1)}, ...) | async-done | bytes 6127632 | tf_op jit(solution)/shard_map/psum | solution.py:331
  1122.4 7.7 multiply_subtract_fusion.1
  1132.9 12.4 %multiply_subtract_fusion = (f32[512,2,1312]{0,2,1:T(8,128)}, f32[512,2,1312]{0,2,1:T(8,128)}, f32[512,2,1312]{0,2,1:T(8,128)}) fusion(f32[512,2,1312]{0,2,1:T(8,128)} %param.31, bf16[512,2,1312]{0,2,1:T(8,128)(2,1)S(1)} %copy-done.15, f32[512,2,1312]{0,2,1:T(8,128)} %param.36, f32[512,2,1312]{0,2,1:T(8,128)} %param.41), kind=kLoop, calls=%fused_computation.66 | loop fusion | flops 21495808 | bytes 34930688 | tf_op jit(solution)/shard_map/sub | solution.py:84
  1146.8 4.8 multiply_subtract_fusion.2
  (350 shorter events, 194.3 us)
Async XLA Ops:
  7.2 8.5 copy-start.3
  7.2 51.0 %all-gather.7.cloned.1.call-start = ((), (), s32[]{:S(2)}) async-start(), calls=%async_computation.7 | async-start | bytes 4718592 | tf_op jit(solution)/shard_map/all_gather | solution.py:139
  10.4 101.6 %all-gather.9.cloned.1.call-start = ((), (), s32[]{:S(2)}) async-start(), calls=%async_computation.8 | async-start | bytes 4718592 | tf_op jit(solution)/shard_map/all_gather | solution.py:156
  15.9 46.2 %copy-start.36 = (f32[512]{0:T(512)}, f32[512]{0:T(512)S(1)}, u32[]{:S(2)}) copy-start(f32[512]{0:T(512)S(1)} %broadcast_multiply_fusion.6) | copy-start | bytes 6148
  16.4 45.8 %copy-start.38 = (f32[512]{0:T(512)}, f32[512]{0:T(512)S(1)}, u32[]{:S(2)}) copy-start(f32[512]{0:T(512)S(1)} %add_rsqrt_fusion.1) | copy-start | bytes 6148
  16.4 45.7 %copy-start.34 = (f32[1,1024]{1,0:T(1,128)}, f32[1,1024]{1,0:T(1,128)S(1)}, u32[]{:S(2)}) copy-start(f32[1,1024]{1,0:T(1,128)S(1)} %get-tuple-element.451) | copy-start | bytes 12292
  58.2 6.6 copy-start.44
  58.2 6.6 copy-start.45
  64.7 95.4 %all-gather.11.cloned.1.call-start = ((), (), s32[]{:S(2)}) async-start(), calls=%async_computation.9 | async-start | bytes 4718592 | tf_op jit(solution)/shard_map/all_gather | solution.py:155
  69.3 220.3 %all-gather.13.cloned.1.call-start = ((), (), s32[]{:S(2)}) async-start(), calls=%async_computation.10 | async-start | bytes 1572864 | tf_op jit(solution)/shard_map/all_gather | solution.py:140
  70.2 227.3 %all-gather.17.cloned.1.call-start = ((), (), s32[]{:S(2)}) async-start(), calls=%async_computation.13 | async-start | bytes 4030464 | tf_op jit(solution)/shard_map/all_gather | solution.py:142
  73.4 259.0 %all-reduce.7.cloned.1.call-start = ((), (), s32[]{:S(2)}) async-start(), calls=%async_computation.11 | async-start | bytes 2097152 | tf_op jit(solution)/shard_map/psum | solution.py:208
  289.5 7.9 copy-start.19
  292.9 111.8 %all-gather.15.cloned.1.call-start = ((), (), s32[]{:S(2)}) async-start(), calls=%async_computation.12 | async-start | bytes 8060928 | tf_op jit(solution)/shard_map/all_gather | solution.py:141
  297.4 167.8 %all-reduce.9.cloned.1.call-start = ((), (), s32[]{:S(2)}) async-start(), calls=%async_computation.14 | async-start | bytes 2097152 | tf_op jit(solution)/shard_map/psum | solution.py:229
  404.7 6.0 copy-start.8
  410.7 10.1 slice-start
  417.2 3.6 slice-start.1
  425.0 248.4 %reduce-scatter.10.cloned.1.call-start = ((), (), s32[]{:S(2)}) async-start(), calls=%async_computation.15 | async-start | bytes 4718592 | tf_op jit(solution)/shard_map/reduce_scatter | solution.py:278
  473.7 6.2 copy-start.1
  479.9 3.6 copy-start
  479.9 6.2 copy-start.2
  491.6 6.2 copy-start.1
  497.8 3.6 copy-start
  497.8 6.2 copy-start.2
  509.4 6.2 copy-start.1
  515.6 3.6 copy-start
  515.6 6.2 copy-start.2
  527.3 6.2 copy-start.1
  533.5 3.6 copy-start
  533.5 6.2 copy-start.2
  545.1 6.2 copy-start.1
  551.3 3.6 copy-start
  551.3 6.2 copy-start.2
  563.0 6.2 copy-start.1
  569.2 3.6 copy-start
  569.2 6.2 copy-start.2
  580.8 6.2 copy-start.1
  587.0 6.2 copy-start.2
  598.7 6.2 copy-start.1
  604.9 6.2 copy-start.2
  623.2 101.1 %reduce-scatter.12.cloned.1.call-start = ((), (), s32[]{:S(2)}) async-start(), calls=%async_computation.16 | async-start | bytes 4718592 | tf_op jit(solution)/shard_map/reduce_scatter | solution.py:284
  645.6 144.9 %all-reduce.13.cloned.1.call-start = ((), (), s32[]{:S(2)}) async-start(), calls=%async_computation.23 | async-start | bytes 4194304 | tf_op jit(solution)/shard_map/psum | solution.py:218
  650.6 23.9 %copy-start.29 = (f32[512,32]{0,1:T(8,128)S(1)}, f32[512,32]{0,1:T(8,128)}, u32[]{:S(2)}) copy-start(f32[512,32]{0,1:T(8,128)} %copy-done.28) | copy-start | bytes 196612
  650.7 24.0 %copy-start.33 = (f32[512,32]{0,1:T(8,128)S(1)}, f32[512,32]{0,1:T(8,128)}, u32[]{:S(2)}) copy-start(f32[512,32]{0,1:T(8,128)} %get-tuple-element.453) | copy-start | bytes 196612
  676.4 47.9 %copy-start.30 = (bf16[512,1,512]{2,0,1:T(8,128)(2,1)}, bf16[512,1,512]{2,0,1:T(8,128)(2,1)S(1)}, u32[]{:S(2)}) copy-start(bf16[512,1,512]{2,0,1:T(8,128)(2,1)S(1)} %copy.95) | copy-start | bytes 1572868
  676.7 47.6 %copy-start.31 = (bf16[512,1,512]{2,0,1:T(8,128)(2,1)}, bf16[512,1,512]{2,0,1:T(8,128)(2,1)S(1)}, u32[]{:S(2)}) copy-start(bf16[512,1,512]{2,0,1:T(8,128)(2,1)S(1)} %copy.94) | copy-start | bytes 1572868
  729.2 84.5 %reduce-scatter.16.cloned.1.call-start = ((), (), s32[]{:S(2)}) async-start(), calls=%async_computation.18 | async-start | bytes 1572864 | tf_op jit(solution)/shard_map/reduce_scatter | solution.py:317
  733.5 121.4 %reduce-scatter.20.cloned.1.call-start = ((), (), s32[]{:S(2)}) async-start(), calls=%async_computation.20 | async-start | bytes 4030464 | tf_op jit(solution)/shard_map/reduce_scatter | solution.py:323
  738.3 186.6 %reduce-scatter.18.cloned.1.call-start = ((), (), s32[]{:S(2)}) async-start(), calls=%async_computation.19 | async-start | bytes 8060928 | tf_op jit(solution)/shard_map/reduce_scatter | solution.py:320
  745.9 224.9 %reduce-scatter.14.cloned.1.call-start = ((), (), s32[]{:S(2)}) async-start(), calls=%async_computation.17 | async-start | bytes 4718592 | tf_op jit(solution)/shard_map/reduce_scatter | solution.py:314
  751.7 233.6 %reduce-scatter.22.cloned.1.call-start = ((), (), s32[]{:S(2)}) async-start(), calls=%async_computation.21 | async-start | bytes 393216
  793.7 328.7 %all-reduce.11.cloned.1.call-start = ((), (), s32[]{:S(2)}) async-start(), calls=%async_computation.22 | async-start | bytes 12255232 | tf_op jit(solution)/shard_map/psum | solution.py:331
  970.9 32.1 %copy-start.41 = (f32[2,512]{1,0:T(2,128)S(1)}, f32[2,512]{1,0:T(2,128)}, u32[]{:S(2)}) copy-start(f32[2,512]{1,0:T(2,128)} %param.33) | copy-start | bytes 12292
  970.9 32.1 %copy-start.42 = (f32[2,512]{1,0:T(2,128)S(1)}, f32[2,512]{1,0:T(2,128)}, u32[]{:S(2)}) copy-start(f32[2,512]{1,0:T(2,128)} %param.38) | copy-start | bytes 12292
  970.9 32.1 %copy-start.43 = (f32[2,512]{1,0:T(2,128)S(1)}, f32[2,512]{1,0:T(2,128)}, u32[]{:S(2)}) copy-start(f32[2,512]{1,0:T(2,128)} %param.43) | copy-start | bytes 12292
  1122.4 7.7 copy-start.11
  1122.4 7.7 copy-start.25
  1122.4 7.7 copy-start.26
  1122.4 7.7 copy-start.32
  1132.9 12.4 %copy-start.9 = (f32[1312,512]{1,0:T(8,128)S(1)}, f32[1312,512]{1,0:T(8,128)}, u32[]{:S(2)}) copy-start(f32[1312,512]{1,0:T(8,128)} %param.32) | copy-start | bytes 8060932
  1132.9 12.4 %copy-start.16 = (f32[1312,512]{1,0:T(8,128)S(1)}, f32[1312,512]{1,0:T(8,128)}, u32[]{:S(2)}) copy-start(f32[1312,512]{1,0:T(8,128)} %param.37) | copy-start | bytes 8060932
  1132.9 13.6 %copy-start.17 = (f32[1312,512]{1,0:T(8,128)S(1)}, f32[1312,512]{1,0:T(8,128)}, u32[]{:S(2)}) copy-start(f32[1312,512]{1,0:T(8,128)} %param.42) | copy-start | bytes 8060932
  1132.9 13.9 %copy-start.20 = (bf16[1312,512]{1,0:T(8,128)(2,1)S(1)}, bf16[1312,512]{1,0:T(8,128)(2,1)}, u32[]{:S(2)}) copy-start(bf16[1312,512]{1,0:T(8,128)(2,1)} %get-tuple-element.411) | copy-start | bytes 4030468
  (22 other events, 46.8 us)
Sparse Core Ops, SparseCore 0:
  10.5 47.6 all-gather.6
  64.8 47.1 all-gather.8
  114.2 45.8 all-gather.10
  162.1 20.0 all-gather.12
  184.1 39.7 all-gather.16
  293.0 39.3 all-reduce.6
  334.6 70.0 all-gather.14
  425.1 40.0 all-reduce.8
  623.3 50.0 reduce-scatter.9
  676.1 48.1 reduce-scatter.11
  729.3 61.2 all-reduce.12
  793.3 20.3 reduce-scatter.15
  816.5 38.3 reduce-scatter.19
  857.7 67.0 reduce-scatter.17
  927.5 43.3 reduce-scatter.13
  973.6 11.6 reduce-scatter.21
  987.8 134.5 all-reduce.10
where the time goes:
time: 1160 us
  waiting for transfers between devices  674 us (58%)
  matrix products  269 us (23%)
  other arithmetic  106 us (9%)
  local copies, waits for them, and re-layouts  70.3 us (6%)
  blocking collectives  21.9 us (2%)
  between operations  15.1 us (1%)
    psum x1, waiting for transfers between devices, on_device(): lax.psum(shards[0].astype(jnp.bfloat16), 'ctx').astype(jnp.float32)  119 us
    all_gather x1, waiting for transfers between devices, on_device(): lax.all_gather(wide_weight.astype(jnp.bfloat16), 'fsdp', axis=0, tiled=True)  70.1 us
    reduce_scatter x1, waiting for transfers between devices, on_device(): lax.psum_scatter(wide_grad.astype(jnp.bfloat16), 'fsdp', scatter_dimensio...  70 us
    dot_general x16, matrix products, block_scores(): jnp.einsum('qhd,khd->hqk', query_low, key_block, preferred_element_type=j...  65.1 us
    dot_general x8, matrix products, grad_step(): jnp.einsum('qhd,khd->hqk', attended_grad, value_block, preferred_element_...  47.7 us
    reduce_scatter x1, waiting for transfers between devices, on_device(): lax.psum_scatter(value_terms.reshape(group_rows, head_width).astype(jnp.b...  47.6 us
    reduce_scatter x1, waiting for transfers between devices, on_device(): lax.psum_scatter(qkv_grad.astype(jnp.bfloat16), 'fsdp', scatter_dimension...  46 us
    all_gather x1, waiting for transfers between devices, on_device(): lax.all_gather(qkv_weight.astype(jnp.bfloat16), 'fsdp', axis=0, tiled=True)  41.8 us
  transfers between devices with their start and end apart: 17, of which 15 were waited for; matrix products, arithmetic and copies ran while one was open for 19% of the time, Pallas kernels for 0%

commit v1 on v0

v1 whole, which is shorter than its diff:
```python
import functools

import jax
import jax.numpy as jnp
from jax import lax
from jax.experimental import pallas as pl
from jax.experimental.pallas import tpu as pltpu
from jax.sharding import PartitionSpec as P

D = 1024
HD = 64
FF = 2624
STEP = 10


NORM_EPS = 1e-05
ROPE_BASE = 160000.0
BETA_FIRST = 0.9
BETA_SECOND = 0.98
ADAM_EPS = 1e-06
DECAY = 0.01
RATE_ATTN = 0.5
RATE_GAIN = 0.8
MASKED = -1e30

MESH = pl.DeviceIdType.MESH
BF16 = jnp.bfloat16
F32 = jnp.float32
VMEM_BYTES = 60 * 2**20


class Sizes:
    def __init__(self, fsdp, ctx, rows, width, head_width, units):
        self.fsdp = fsdp
        self.ctx = ctx
        self.chips = ctx // 2
        self.rows = rows
        self.block = rows // 8
        self.group = rows * ctx
        self.width = width
        self.shard = width // fsdp
        self.heads = head_width // HD
        self.head_width = head_width
        self.units = units
        self.share = max(1, ctx // self.heads)
        self.chip_heads = max(1, self.heads // self.chips)
        self.chunk = self.chip_heads * 3 * HD


def remote(src, dst, send, recv, device):
    return pltpu.make_async_remote_copy(
        src_ref=src,
        dst_ref=dst,
        send_sem=send,
        recv_sem=recv,
        device_id=device,
        device_id_type=MESH,
    )


def greet(devices):
    barrier = pltpu.get_barrier_semaphore()
    for device in devices:
        pl.semaphore_signal(barrier, inc=1, device_id=device, device_id_type=MESH)
    pl.semaphore_wait(barrier, len(devices))


def vmem():
    return pl.BlockSpec(memory_space=pltpu.VMEM)


def anywhere():
    return pl.BlockSpec(memory_space=pl.ANY)


def normalize(values):
    centered = values - jnp.mean(values, axis=1, keepdims=True)
    scaling = lax.rsqrt(jnp.mean(centered * centered, axis=1, keepdims=True) + NORM_EPS)
    return (centered * scaling, scaling)


def norm_back(grad_hat, normed, scaling):
    return scaling * (
        grad_hat
        - jnp.mean(grad_hat, axis=1, keepdims=True)
        - normed * jnp.mean(grad_hat * normed, axis=1, keepdims=True)
    )


def swap_halves(values):
    lane = lax.broadcasted_iota(jnp.int32, values.shape, 1)
    return jnp.where(
        lane % HD < HD // 2, pltpu.roll(values, 2 * HD - HD // 2, 1), pltpu.roll(values, HD // 2, 1)
    )


def packed_place(local_row, device, devices, block_size):
    return (local_row // block_size * devices + device) * block_size + local_row % block_size


def sequence_ends(lengths_row, order_row):
    count_seqs = lengths_row.shape[0]
    chosen = (order_row[:, None] == jnp.arange(count_seqs, dtype=jnp.int32)[None, :]).astype(
        jnp.int32
    )
    in_order = jnp.sum(chosen * lengths_row[None, :], axis=1)
    return (in_order, jnp.cumsum(in_order))


def positions(in_order, endings, places):
    passed = (endings[None, :] <= places[:, None]).astype(jnp.int32)
    return places - jnp.sum(passed * in_order[None, :], axis=1)


def rope_tables(position):
    half_size = HD // 2
    frequency = ROPE_BASE ** (-(2.0 * jnp.arange(half_size, dtype=jnp.float32)) / (2.0 * half_size))
    angles = position.astype(jnp.float32)[:, None] * frequency[None, :]
    cosine, sines = jnp.cos(angles), jnp.sin(angles)
    return (
        jnp.concatenate([cosine] * 4, axis=1),
        jnp.concatenate([-sines, sines, -sines, sines], axis=1),
    )


def project_kernel(
    z_,
    tok_ref,
    gain_ref,
    cos_ref,
    sin_ref,
    wq_ref,
    wo_ref,
    wi_ref,
    packed_ref,
    wq_out,
    wo_out,
    wi_out,
    gain_out,
    entry_s,
    wq_s,
    send_s,
    gain_s,
    gain_send,
    gain_recv,
    wq_send,
    wq_recv,
    wq_fsend,
    wq_frecv,
    w_send,
    w_recv,
    w_fsend,
    w_frecv,
    a_send,
    a_recv,
    local_sem,
):
    f, c, t = lax.axis_index("fsdp"), lax.axis_index("ctx"), lax.axis_index("tp")
    core = lax.rem(c, 2)
    chip = c // 2
    mate = (f, c + 1 - 2 * core, t)
    others = range(1, z_.fsdp)

    def ahead(k):
        return lax.rem(f + k, z_.fsdp)

    def behind(k):
        return lax.rem(f + z_.fsdp - k, z_.fsdp)

    def chip_of(s):
        return lax.rem(chip + 1 + s, z_.chips)

    greet(
        [(ahead(k), c, t) for k in others]
        + [(f, lax.rem(c + j, z_.ctx), t) for j in range(1, z_.ctx)]
    )

    half = z_.shard // 2

    def gain_copy(k, owner):
        return remote(
            gain_ref, gain_s.at[owner], gain_send.at[k - 1], gain_recv.at[k - 1], (ahead(k), c, t)
        )

    def wq_copy(s, k, owner):
        p = chip_of(s)
        rows = pl.ds(pl.multiple_of(core * half, half), half)
        return remote(
            wq_ref.at[p, rows],
            wq_s.at[p, owner, rows],
            wq_send.at[s, k - 1],
            wq_recv.at[s, k - 1],
            (ahead(k), c, t),
        )

    def wq_pass(s, k, side):
        p = chip_of(s)
        rows = pl.ds(pl.multiple_of(side * half, half), half)
        place = wq_s.at[p, behind(k), rows]
        return remote(place, place, wq_fsend.at[s, k - 1], wq_frecv.at[s, k - 1], mate)

    attn_half = z_.head_width // 2

    def wo_copy(k, owner):
        rows = pl.ds(pl.multiple_of(core * attn_half, attn_half), attn_half)
        return remote(
            wo_ref.at[rows],
            wo_out.at[owner, rows],
            w_send.at[0, k - 1],
            w_recv.at[0, k - 1],
            (ahead(k), c, t),
        )

    def wo_pass(k, side):
        rows = pl.ds(pl.multiple_of(side * attn_half, attn_half), attn_half)
        place = wo_out.at[behind(k), rows]
        return remote(place, place, w_fsend.at[0, k - 1], w_frecv.at[0, k - 1], mate)

    def wi_copy(k, owner):
        return remote(
            wi_ref.at[core],
            wi_out.at[core, owner],
            w_send.at[1, k - 1],
            w_recv.at[1, k - 1],
            (ahead(k), c, t),
        )

    def wi_pass(k, side):
        place = wi_out.at[side, behind(k)]
        return remote(place, place, w_fsend.at[1, k - 1], w_frecv.at[1, k - 1], mate)

    def head_copy(s, side, source):
        p = chip_of(s)
        return remote(
            send_s.at[s, side % z_.chip_heads],
            packed_ref.at[:, source],
            a_send.at[s, side],
            a_recv.at[s, core],
            (f, 2 * p + side, t),
        )

    def head_arrival(s, side):
        source = 2 * lax.rem(chip + 2 * z_.chips - 1 - s, z_.chips) + side
        return remote(
            send_s.at[s, 0], packed_ref.at[:, source], a_send.at[s, 0], a_recv.at[s, side], mate
        )

    for k in others:
        gain_copy(k, f).start()
    for k in others:
        wq_copy(0, k, f).start()
    own_wq = pltpu.make_async_copy(wq_ref, wq_s.at[:, f], local_sem.at[0])
    own_wo = pltpu.make_async_copy(wo_ref, wo_out.at[f], local_sem.at[1])
    own_wi = pltpu.make_async_copy(wi_ref, wi_out.at[:, f], local_sem.at[2])
    own_wq.start()
    own_wo.start()
    own_wi.start()
    gain_s[f] = gain_ref[...]
    for k in others:
        wq_copy(1, k, f).start()
    for k in others:
        gain_copy(k, behind(k)).wait()

    gain_out[...] = gain_s[...]
    tile = min(128, z_.rows)

    def norm_tile(i, carried):
        rows = pl.ds(pl.multiple_of(i * tile, tile), tile)
        normed, nothing = normalize(tok_ref[rows, :].astype(F32))
        for g in range(z_.fsdp):
            columns = slice(g * z_.shard, (g + 1) * z_.shard)
            entry_s[g, rows, :] = (normed[:, columns] * gain_s[g, 0:1, :]).astype(BF16)
        return carried

    lax.fori_loop(0, z_.rows // tile, norm_tile, 0)
    own_wq.wait()

    def chunk_step(s, carried):
        for k in others:

            @pl.when(s + 2 < z_.chips)
            def more():
                wq_copy(s + 2, k, f).start()

            @pl.when(s + 2 == z_.chips)
            def attn_part():
                wo_copy(k, f).start()

            @pl.when(s + 1 == z_.chips)
            def wide_part():
                wi_copy(k, f).start()

            arrived = wq_copy(s, k, behind(k))
            arrived.wait_recv()
            wq_pass(s, k, core).start()
        for k in others:
            wq_pass(s, k, 1 - core).wait_recv()
        p = chip_of(s)
        total = jnp.zeros((z_.rows, z_.chunk), F32)
        for g in range(z_.fsdp):
            total = total + jnp.dot(entry_s[g], wq_s[p, g], preferred_element_type=F32)
        for i in range(z_.chip_heads):
            pair = total[:, 2 * HD * i : 2 * HD * (i + 1)]
            pair = pair * cos_ref[...] + swap_halves(pair) * sin_ref[...]
            send_s[s, i, 0:8] = pair.astype(BF16).reshape(8, z_.block, 2 * HD)
            start = z_.chip_heads * 2 * HD + HD * i
            value = total[:, start : start + HD]
            value = jnp.concatenate([value[: z_.rows // 2], value[z_.rows // 2 :]], axis=1)
            send_s[s, i, 8:12] = value.astype(BF16).reshape(4, z_.block, 2 * HD)

        @pl.when(s < z_.chips - 1)
        def away():
            for side in range(2):
                head_copy(s, side, c).start()

        return carried

    lax.fori_loop(0, z_.chips, chunk_step, 0)
    last = z_.chips - 1
    kept = pltpu.make_async_copy(
        send_s.at[last, lax.rem(core, z_.chip_heads)], packed_ref.at[:, c], local_sem.at[3]
    )
    kept.start()
    crossed = remote(
        send_s.at[last, lax.rem(1 - core, z_.chip_heads)],
        packed_ref.at[:, c],
        a_send.at[last, 0],
        a_recv.at[last, 0],
        mate,
    )
    crossed.start()
    keep_wq = pltpu.make_async_copy(wq_s, wq_out, local_sem.at[4])
    keep_wq.start()
    for k in others:
        wo_copy(k, behind(k)).wait_recv()
        wo_pass(k, core).start()
    for k in others:
        wi_copy(k, behind(k)).wait_recv()
        wi_pass(k, core).start()
    for s in range(z_.chips - 1):
        for side in range(2):
            head_arrival(s, side).wait_recv()
            head_copy(s, side, c).wait_send()
    crossed_in = remote(
        send_s.at[last, 0],
        packed_ref.at[:, c + 1 - 2 * core],
        a_send.at[last, 0],
        a_recv.at[last, 0],
        mate,
    )
    crossed_in.wait_recv()
    crossed.wait_send()
    for k in others:
        for s in range(z_.chips):
            wq_copy(s, k, f).wait_send()
            wq_pass(s, k, core).wait_send()
        wo_copy(k, f).wait_send()
        wi_copy(k, f).wait_send()
        wo_pass(k, core).wait_send()
        wi_pass(k, core).wait_send()
        wo_pass(k, 1 - core).wait_recv()
        wi_pass(k, 1 - core).wait_recv()
    kept.wait()
    keep_wq.wait()
    own_wo.wait()
    own_wi.wait()


def project(z_, tokens, gains, cosine, sines, wq, wo, wi):
    peers = max(1, z_.fsdp - 1)
    dma = pltpu.SemaphoreType.DMA
    return pl.pallas_call(
        functools.partial(project_kernel, z_),
        out_shape=(
            jax.ShapeDtypeStruct((12, z_.ctx, z_.block, 2 * HD), BF16),
            jax.ShapeDtypeStruct((z_.chips, z_.fsdp, z_.shard, z_.chunk), BF16),
            jax.ShapeDtypeStruct((z_.fsdp, z_.head_width, z_.shard), BF16),
            jax.ShapeDtypeStruct((2, z_.fsdp, z_.shard, z_.units), BF16),
            jax.ShapeDtypeStruct((z_.fsdp, 8, z_.shard), F32),
        ),
        in_specs=[vmem()] * 5 + [anywhere()] * 2,
        out_specs=(anywhere(), anywhere(), anywhere(), anywhere(), vmem()),
        scratch_shapes=[
            pltpu.VMEM((z_.fsdp, z_.rows, z_.shard), BF16),
            pltpu.VMEM((z_.chips, z_.fsdp, z_.shard, z_.chunk), BF16),
            pltpu.VMEM((z_.chips, z_.chip_heads, 12, z_.block, 2 * HD), BF16),
            pltpu.VMEM((z_.fsdp, 8, z_.shard), F32),
            dma((peers,)),
            dma((peers,)),
            dma((z_.chips, peers)),
            dma((z_.chips, peers)),
            dma((z_.chips, peers)),
            dma((z_.chips, peers)),
            dma((2, peers)),
            dma((2, peers)),
            dma((2, peers)),
            dma((2, peers)),
            dma((z_.chips, 2)),
            dma((z_.chips, 2)),
            dma((5,)),
        ],
        compiler_params=pltpu.CompilerParams(
            collective_id=0, has_side_effects=True, vmem_limit_bytes=VMEM_BYTES
        ),
        name="project",
    )(tokens, gains, cosine, sines, wq, wo, wi)


def sequence_at(ends_ref, place):
    start, end = jnp.int32(0), ends_ref[0]
    for k in range(ends_ref.shape[0] - 1):
        past = ends_ref[k] <= place
        start = jnp.where(past, ends_ref[k], start)
        end = jnp.where(past, ends_ref[k + 1], end)
    return (start, end)


def segments_of(ends_ref, places):
    segment = jnp.zeros(places.shape, jnp.int32)
    for k in range(ends_ref.shape[0]):
        segment = segment + (ends_ref[k] <= places).astype(jnp.int32)
    return segment


def attend_kernel(
    z_,
    q_tile,
    k_tile,
    ends_ref,
    packed_ref,
    out_ref,
    outt_ref,
    lse_ref,
    query_s,
    value_s,
    top_s,
    total_s,
):
    group = z_.group
    half = group // 2
    piece = min(512, half)
    scaling = HD ** (-0.5)
    sums = 16
    query_s[0:HD, :] = jnp.zeros((HD, group), BF16)
    value_s[HD : HD + sums, :] = jnp.ones((sums, group), BF16)

    def prepare(i, carried):
        rows = pl.ds(pl.multiple_of(i * piece, piece), piece)
        turned = packed_ref[rows, :].astype(F32).T
        query_s[HD : 2 * HD, rows] = (turned[0:HD] * scaling).astype(BF16)

        @pl.when(i < half // piece)
        def values():
            turned_value = (
                packed_ref[pl.ds(pl.multiple_of(group + i * piece, piece), piece), :].astype(F32).T
            ).astype(BF16)
            value_s[0:HD, rows] = turned_value[0:HD]
            value_s[0:HD, pl.ds(pl.multiple_of(half + i * piece, piece), piece)] = turned_value[
                HD : 2 * HD
            ]

        return carried

    lax.fori_loop(0, group // piece, prepare, 0)

    def one_tile(i, carried):
        first = pl.multiple_of(i * q_tile, q_tile)
        columns = pl.ds(first, q_tile)
        low, low_end = sequence_at(ends_ref, first)
        high_start, high = sequence_at(ends_ref, first + q_tile - 1)
        single = low == high_start
        top_s[...] = jnp.full(top_s.shape, MASKED, F32)
        total_s[...] = jnp.zeros(total_s.shape, F32)

        def one_step(j, masked):
            start = pl.multiple_of(j * k_tile, k_tile)
            rows = pl.ds(start, k_tile)
            scores = jnp.dot(packed_ref[rows, :], query_s[:, columns], preferred_element_type=F32)
            if masked:
                key_seg = segments_of(
                    ends_ref, start + lax.broadcasted_iota(jnp.int32, (k_tile, 1), 0)
                )
                query_seg = segments_of(
                    ends_ref, first + lax.broadcasted_iota(jnp.int32, (1, q_tile), 1)
                )
                scores = jnp.where(key_seg == query_seg, scores, MASKED)
            before = top_s[0:1, :]
            after = jnp.maximum(before, jnp.max(scores, axis=0, keepdims=True))
            weights = jnp.exp(scores - after).astype(BF16)
            top_s[0:1, :] = after
            total_s[...] = total_s[...] * jnp.exp(before - after) + jnp.dot(
                value_s[:, rows], weights, preferred_element_type=F32
            )

        def step(j, inner):
            start = j * k_tile
            whole = single & (start >= low) & (start + k_tile <= high)

            @pl.when(whole)
            def plain():
                one_step(j, False)

            @pl.when(jnp.logical_not(whole))
            def partial():
                one_step(j, True)

            return inner

        lax.fori_loop(low // k_tile, (high + k_tile - 1) // k_tile, step, 0)
        summed = total_s[HD : HD + 1, :]
        lse_ref[:, columns] = jnp.broadcast_to(top_s[0:1, :] + jnp.log(summed), (8, q_tile))
        outt_ref[:, columns] = total_s[0:HD, :] / summed
        return carried

    lax.fori_loop(0, group // q_tile, one_tile, 0)

    def finish(i, carried):
        rows = pl.ds(pl.multiple_of(i * piece, piece), piece)
        later = pl.ds(pl.multiple_of(half + i * piece, piece), piece)
        both = jnp.concatenate([outt_ref[:, rows], outt_ref[:, later]], axis=0)
        out_ref[rows, :] = both.T.astype(BF16)
        return carried

    lax.fori_loop(0, half // piece, finish, 0)


def attend(z_, ends, packed):
    q_tile, k_tile = 512, 512
    group = z_.group
    return pl.pallas_call(
        functools.partial(attend_kernel, z_, q_tile, k_tile),
        out_shape=(
            jax.ShapeDtypeStruct((group // 2, 2 * HD), BF16),
            jax.ShapeDtypeStruct((HD, group), F32),
            jax.ShapeDtypeStruct((8, group), F32),
        ),
        in_specs=[pl.BlockSpec(memory_space=pltpu.SMEM), vmem()],
        out_specs=(vmem(), vmem(), vmem()),
        scratch_shapes=[
            pltpu.VMEM((2 * HD, group), BF16),
            pltpu.VMEM((HD + 16, group), BF16),
            pltpu.VMEM((8, q_tile), F32),
            pltpu.VMEM((HD + 16, q_tile), F32),
        ],
        compiler_params=pltpu.CompilerParams(vmem_limit_bytes=VMEM_BYTES),
        name="attend",
    )(ends, packed)


def attend_back_kernel(
    z_,
    q_tile,
    k_tile,
    ends_ref,
    packed_ref,
    grad_ref,
    outt_ref,
    lse_ref,
    out_ref,
    query_s,
    key_s,
    swapped_s,
    grad_s,
    gradt_s,
    delta_s,
    query_grad_s,
    key_acc,
    value_acc,
):
    group = z_.group
    half = group // 2
    piece = min(512, half)
    scaling = HD ** (-0.5)
    query_s[0:HD, :] = jnp.zeros((HD, group), BF16)
    gradt_s[0:HD, :] = jnp.zeros((HD, group), BF16)
    gradt_s[2 * HD : 3 * HD, :] = jnp.zeros((HD, group), BF16)

    def prepare(i, carried):
        rows = pl.ds(pl.multiple_of(i * piece, piece), piece)
        pair = packed_ref[rows, :].astype(F32)
        turned = pair.T
        query_s[HD : 2 * HD, rows] = (turned[0:HD] * scaling).astype(BF16)
        key_s[:, rows] = turned[HD : 2 * HD].astype(BF16)
        swapped_s[rows, :] = pltpu.roll(pair, HD, 1).astype(BF16)
        query_grad_s[:, rows] = jnp.zeros((HD, piece), F32)

        @pl.when(i < half // piece)
        def grads():
            later = pl.ds(pl.multiple_of(half + i * piece, piece), piece)
            both = grad_ref[rows, :].astype(F32)
            turned_grad = both.T
            grad_s[rows, :] = both.astype(BF16)
            grad_s[later, :] = pltpu.roll(both, HD, 1).astype(BF16)
            for place, part in ((rows, turned_grad[0:HD]), (later, turned_grad[HD : 2 * HD])):
                gradt_s[HD : 2 * HD, place] = part.astype(BF16)
                delta = jnp.sum(part * outt_ref[:, place], axis=0, keepdims=True)
                delta_s[:, place] = jnp.broadcast_to(delta, (8, piece))

        return carried

    lax.fori_loop(0, group // piece, prepare, 0)

    def one_tile(j, carried):
        start = pl.multiple_of(j * k_tile, k_tile)
        rows = pl.ds(start, k_tile)
        upper = (start >= half).astype(jnp.int32)
        value_rows = pl.ds(pl.multiple_of(group + start - upper * half, k_tile), k_tile)
        turned_rows = pl.ds(pl.multiple_of(HD - upper * HD, HD), 2 * HD)
        low, low_end = sequence_at(ends_ref, start)
        high_start, high = sequence_at(ends_ref, start + k_tile - 1)
        single = low == high_start
        key_acc[...] = jnp.zeros(key_acc.shape, F32)
        value_acc[...] = jnp.zeros(value_acc.shape, F32)

        def one_step(i, masked):
            first = pl.multiple_of(i * q_tile, q_tile)
            columns = pl.ds(first, q_tile)
            scores = jnp.dot(packed_ref[rows, :], query_s[:, columns], preferred_element_type=F32)
            chances = jnp.exp(scores - lse_ref[0:1, columns])
            if masked:
                key_seg = segments_of(
                    ends_ref, start + lax.broadcasted_iota(jnp.int32, (k_tile, 1), 0)
                )
                query_seg = segments_of(
                    ends_ref, first + lax.broadcasted_iota(jnp.int32, (1, q_tile), 1)
                )
                chances = jnp.where(key_seg == query_seg, chances, 0.0)
            chance_grad = jnp.dot(
                packed_ref[value_rows, :],
                gradt_s[turned_rows, columns],
                preferred_element_type=F32,
            )
            score_grad = (chances * (chance_grad - delta_s[0:1, columns])).astype(BF16)
            value_acc[...] += jnp.dot(
                chances.astype(BF16), grad_s[columns, :], preferred_element_type=F32
            )
            key_acc[...] += jnp.dot(
                score_grad, swapped_s[columns, :], preferred_element_type=F32
            )
            query_grad_s[:, columns] += jnp.dot(
                key_s[:, rows], score_grad, preferred_element_type=F32
            )

        def step(i, inner):
            first = i * q_tile
            whole = single & (first >= low) & (first + q_tile <= high)

            @pl.when(whole)
            def plain():
                one_step(i, False)

            @pl.when(jnp.logical_not(whole))
            def partial():
                one_step(i, True)

            return inner

        lax.fori_loop(low // q_tile, (high + q_tile - 1) // q_tile, step, 0)
        out_ref[rows, HD : 2 * HD] = (key_acc[:, HD : 2 * HD] * scaling).astype(BF16)

        @pl.when(upper == 0)
        def lower_values():
            out_ref[pl.ds(pl.multiple_of(group + start, k_tile), k_tile), 0:HD] = value_acc[
                :, 0:HD
            ].astype(BF16)

        @pl.when(upper == 1)
        def upper_values():
            out_ref[
                pl.ds(pl.multiple_of(group + start - half, k_tile), k_tile), HD : 2 * HD
            ] = pltpu.roll(value_acc[...], HD, 1)[:, HD : 2 * HD].astype(BF16)

        return carried

    lax.fori_loop(0, group // k_tile, one_tile, 0)

    def finish(i, carried):
        rows = pl.ds(pl.multiple_of(i * piece, piece), piece)
        turned = query_grad_s[:, rows] * scaling
        out_ref[rows, 0:HD] = (
            jnp.concatenate([turned, jnp.zeros((HD, piece), F32)], axis=0).T[:, 0:HD].astype(BF16)
        )
        return carried

    lax.fori_loop(0, group // piece, finish, 0)


def attend_back(z_, ends, packed, grads, outt, lse):
    q_tile, k_tile = 512, 512
    group = z_.group
    return pl.pallas_call(
        functools.partial(attend_back_kernel, z_, q_tile, k_tile),
        out_shape=jax.ShapeDtypeStruct((group + group // 2, 2 * HD), BF16),
        in_specs=[pl.BlockSpec(memory_space=pltpu.SMEM)] + [vmem()] * 4,
        out_specs=vmem(),
        scratch_shapes=[
            pltpu.VMEM((2 * HD, group), BF16),
            pltpu.VMEM((HD, group), BF16),
            pltpu.VMEM((group, 2 * HD), BF16),
            pltpu.VMEM((group, 2 * HD), BF16),
            pltpu.VMEM((3 * HD, group), BF16),
            pltpu.VMEM((8, group), F32),
            pltpu.VMEM((HD, group), F32),
            pltpu.VMEM((k_tile, 2 * HD), F32),
            pltpu.VMEM((k_tile, 2 * HD), F32),
        ],
        compiler_params=pltpu.CompilerParams(vmem_limit_bytes=VMEM_BYTES),
        name="attend_back",
    )(ends, packed, grads, outt, lse)


def adam_step(weight, gradient, moment, squared, rate_now):
    first = BETA_FIRST * moment + (1.0 - BETA_FIRST) * gradient
    second = BETA_SECOND * squared + (1.0 - BETA_SECOND) * gradient * gradient
    corrected = first / (1.0 - BETA_FIRST**STEP)
    spread = jnp.sqrt(second / (1.0 - BETA_SECOND**STEP))
    return (weight - rate_now * (corrected / (spread + ADAM_EPS) + DECAY * weight), first, second)


def update_all(weights, gradients, moments, squares, rates):
    results = []
    for weight, gradient, moment, squared, rate_now in zip(
        weights, gradients, moments, squares, rates
    ):
        results.extend(adam_step(weight, gradient, moment, squared, rate_now))
    return results


def exact_gelu(values):
    return jax.nn.gelu(values, approximate=False)


def by_chip(z_, weight):
    rows = weight.shape[0]
    split = weight.reshape(rows, 3, z_.chips, z_.chip_heads, HD)
    pairs = split[:, 0:2].transpose(2, 0, 3, 1, 4).reshape(z_.chips, rows, -1)
    values = split[:, 2].transpose(1, 0, 2, 3).reshape(z_.chips, rows, -1)
    return jnp.concatenate([pairs, values], axis=2)


def from_chips(z_, chunked):
    rows = chunked.shape[1]
    cut = z_.chip_heads * 2 * HD
    pairs = chunked[:, :, :cut].reshape(z_.chips, rows, z_.chip_heads, 2, HD)
    pairs = pairs.transpose(1, 3, 0, 2, 4).reshape(rows, 2, z_.head_width)
    values = chunked[:, :, cut:].reshape(z_.chips, rows, z_.chip_heads, HD)
    values = values.transpose(1, 0, 2, 3).reshape(rows, 1, z_.head_width)
    return jnp.concatenate([pairs, values], axis=1)


def heads_to_tokens(z_, packed):
    parts = packed.shape[0]
    moved = lax.all_to_all(packed, "ctx", split_axis=1, concat_axis=1, tiled=True)
    moved = moved.reshape(parts, z_.heads, z_.share, z_.block, 2 * HD)
    return lax.dynamic_index_in_dim(moved, lax.axis_index("ctx") % z_.share, 2, keepdims=False)


def tokens_to_heads(z_, packed):
    return lax.all_to_all(
        jnp.repeat(packed, z_.share, axis=1), "ctx", split_axis=1, concat_axis=1, tiled=True
    )


def unpack_values(z_, packed):
    split = packed.reshape(4, z_.heads, z_.block, 2, HD)
    return split.transpose(3, 0, 2, 1, 4).reshape(z_.rows, z_.heads, HD)


def pack_values(z_, values):
    split = values.reshape(2, 4, z_.block, z_.heads, HD)
    return split.transpose(1, 3, 2, 0, 4).reshape(4, z_.heads, z_.block, 2 * HD)


def on_device(
    tokens,
    cotangent,
    lengths,
    order,
    qkv_weight,
    attn_weight,
    wide_weight,
    down_weight,
    norm_gains,
    qkv_mean,
    attn_mean,
    wide_mean,
    down_mean,
    gains_mean,
    qkv_square,
    attn_square,
    wide_square,
    down_square,
    gains_square,
):
    z_ = Sizes(
        lax.axis_size("fsdp"),
        lax.axis_size("ctx"),
        tokens.shape[0],
        tokens.shape[1],
        qkv_weight.shape[2],
        wide_weight.shape[2],
    )
    ctx_index = lax.axis_index("ctx")
    in_order, endings = sequence_ends(lengths[0], order[0])
    local_ids = jnp.arange(z_.rows, dtype=jnp.int32)
    cosine, sines = rope_tables(
        positions(in_order, endings, packed_place(local_ids, ctx_index, z_.ctx, z_.block))
    )
    gain_rows = jnp.pad(norm_gains.astype(BF16).astype(F32), ((0, 6), (0, 0)))
    packed, wq_full, wo_full, wi_full, gains_full = project(
        z_,
        tokens,
        gain_rows,
        cosine,
        sines,
        by_chip(z_, qkv_weight.astype(BF16)),
        attn_weight.astype(BF16),
        wide_weight.astype(BF16).transpose(1, 0, 2),
    )
    down_low = lax.all_gather(down_weight.astype(BF16), "fsdp", axis=1, tiled=True)
    attn_low = wo_full.transpose(1, 0, 2).reshape(z_.head_width, z_.width)
    wide_low = wi_full.reshape(2, z_.width, z_.units)
    gains = gains_full.transpose(1, 0, 2).reshape(8, z_.width)
    inputs = tokens.astype(F32)
    normed_one, scaling_one = normalize(inputs)
    entry_one = (normed_one * gains[0][None, :]).astype(BF16)
    packed = packed.reshape(12 * z_.ctx * z_.block, 2 * HD)
    attended_packed, attended_turned, lse = attend(z_, endings, packed)
    attended_low = unpack_values(
        z_, heads_to_tokens(z_, attended_packed.reshape(4, z_.ctx, z_.block, 2 * HD))
    ).reshape(z_.rows, z_.head_width)
    mixed_sum = lax.psum(
        jnp.dot(attended_low, attn_low, preferred_element_type=F32).astype(BF16), "tp"
    ).astype(F32)
    middle = inputs + mixed_sum
    normed_two, scaling_two = normalize(middle)
    entry_two = (normed_two * gains[1][None, :]).astype(BF16)
    gate_up = jnp.einsum("td,kdf->tkf", entry_two, wide_low, preferred_element_type=F32)
    activated, gelu_pull = jax.vjp(exact_gelu, gate_up[:, 0])
    hidden_low = (activated * gate_up[:, 1]).astype(BF16)
    branch = lax.psum(
        jnp.dot(hidden_low, down_low, preferred_element_type=F32).astype(BF16), "tp"
    ).astype(F32)
    output = (middle + branch).astype(BF16)
    grad_out = cotangent.astype(F32)
    down_grad = jnp.einsum("tf,td->fd", hidden_low, cotangent, preferred_element_type=F32)
    hidden_grad = jnp.einsum("td,fd->tf", cotangent, down_low, preferred_element_type=F32)
    act_grad = gelu_pull(hidden_grad * gate_up[:, 1])[0]
    gate_grad = hidden_grad * activated
    gated_grad = jnp.stack([act_grad, gate_grad], axis=1).astype(BF16)
    wide_grad = jnp.einsum("td,tkf->dkf", entry_two, gated_grad, preferred_element_type=F32)
    back_two = lax.psum(
        jnp.einsum("tkf,kdf->td", gated_grad, wide_low, preferred_element_type=F32).astype(BF16),
        "tp",
    ).astype(F32)
    gain_second = jnp.sum(back_two * normed_two, axis=0)
    middle_grad = grad_out + norm_back(back_two * gains[1][None, :], normed_two, scaling_two)
    middle_low = middle_grad.astype(BF16)
    attn_grad = jnp.einsum("tf,td->fd", attended_low, middle_low, preferred_element_type=F32)
    attended_grad = (
        jnp.einsum("td,fd->tf", middle_low, attn_low, preferred_element_type=F32)
        .astype(BF16)
        .reshape(z_.rows, z_.heads, HD)
    )
    grads_packed = tokens_to_heads(z_, pack_values(z_, attended_grad))
    head_grads = attend_back(
        z_,
        endings,
        packed,
        grads_packed.reshape(z_.group // 2, 2 * HD),
        attended_turned,
        lse,
    )
    token_grads = heads_to_tokens(z_, head_grads.reshape(12, z_.ctx, z_.block, 2 * HD))
    pair_grad = token_grads[0:8].transpose(0, 2, 1, 3).reshape(z_.rows * z_.heads, 2 * HD)
    pair_grad = pair_grad.astype(F32)
    lane = jnp.arange(2 * HD)
    swapped = jnp.where(
        lane % HD < HD // 2,
        jnp.roll(pair_grad, -(HD // 2), axis=1),
        jnp.roll(pair_grad, HD // 2, axis=1),
    )
    wide_cos = jnp.repeat(cosine, z_.heads, axis=0)
    wide_sin = jnp.repeat(sines, z_.heads, axis=0)
    pair_grad = (pair_grad * wide_cos - swapped * wide_sin).astype(BF16)
    pair_grad = pair_grad.reshape(z_.rows, z_.chips, z_.chip_heads * 2 * HD)
    value_grad = unpack_values(z_, token_grads[8:12]).reshape(
        z_.rows, z_.chips, z_.chip_heads * HD
    )
    projected_grad = jnp.concatenate([pair_grad, value_grad], axis=2)
    wq_flat = wq_full.reshape(z_.chips, z_.width, z_.chunk)
    qkv_grad = jnp.einsum("td,tpc->pdc", entry_one, projected_grad, preferred_element_type=F32)
    back_one = lax.psum(
        jnp.einsum("tpc,pdc->td", projected_grad, wq_flat, preferred_element_type=F32).astype(BF16),
        "tp",
    ).astype(F32)
    gain_first = jnp.sum(back_one * normed_one, axis=0)
    input_grad = (
        middle_grad + norm_back(back_one * gains[0][None, :], normed_one, scaling_one)
    ).astype(BF16)
    gains_grad = jnp.stack([gain_first, gain_second])
    rates = (D ** (-0.5), RATE_ATTN, D ** (-0.5), FF ** (-0.5), RATE_GAIN)
    shards = [
        lax.psum_scatter(g.astype(BF16), "fsdp", scatter_dimension=axis, tiled=True)
        for g, axis in (
            (qkv_grad, 1),
            (attn_grad, 1),
            (wide_grad, 0),
            (down_grad, 1),
            (gains_grad, 1),
        )
    ]
    shards = [lax.psum(g, "ctx").astype(F32) for g in shards]
    shards[0] = from_chips(z_, shards[0])
    final = update_all(
        (qkv_weight, attn_weight, wide_weight, down_weight, norm_gains),
        shards,
        (qkv_mean, attn_mean, wide_mean, down_mean, gains_mean),
        (qkv_square, attn_square, wide_square, down_square, gains_square),
        rates,
    )
    return (output, input_grad) + tuple(final)


def solution(mesh):
    return jax.shard_map(
        on_device,
        mesh=mesh,
        in_specs=(
            P(("fsdp", "ctx"), None),
            P(("fsdp", "ctx"), None),
            P("fsdp", None),
            P("fsdp", None),
            P("fsdp", None, "tp"),
            P("tp", "fsdp"),
            P("fsdp", None, "tp"),
            P("tp", "fsdp"),
            P(None, "fsdp"),
            P("fsdp", None, "tp"),
            P("tp", "fsdp"),
            P("fsdp", None, "tp"),
            P("tp", "fsdp"),
            P(None, "fsdp"),
            P("fsdp", None, "tp"),
            P("tp", "fsdp"),
            P("fsdp", None, "tp"),
            P("tp", "fsdp"),
            P(None, "fsdp"),
        ),
        out_specs=(
            P(("fsdp", "ctx"), None),
            P(("fsdp", "ctx"), None),
            P("fsdp", None, "tp"),
            P("fsdp", None, "tp"),
            P("fsdp", None, "tp"),
            P("tp", "fsdp"),
            P("tp", "fsdp"),
            P("tp", "fsdp"),
            P("fsdp", None, "tp"),
            P("fsdp", None, "tp"),
            P("fsdp", None, "tp"),
            P("tp", "fsdp"),
            P("tp", "fsdp"),
            P("tp", "fsdp"),
            P(None, "fsdp"),
            P(None, "fsdp"),
            P(None, "fsdp"),
        ),
        check_vma=False,
    )
```

time: 1160 us -> 839 us (0.72)
  waiting for transfers between devices: 674 us -> 382 us
  matrix products: 269 us -> 48.2 us
  Pallas kernels: 0 us -> 161 us
  local copies, waits for them, and re-layouts: 70.3 us -> 98.1 us
  other arithmetic: 106 us -> 79.1 us
  blocking collectives: 21.9 us -> 37.4 us
    dot_general x67 -> x10, matrix products: 266 us -> 45.5 us  [the longest x1 9.47 us: on_device(): jnp.einsum('td,kdf->tkf', entry_two, wide_low, preferred_element_type=F32)]
    all_gather x6 -> x1, waiting for transfers between devices: 190 us -> 0.01 us  [on_device(): lax.all_gather(down_weight.astype(BF16), 'fsdp', axis=1, tiled=True)]
    pallas_call x0 -> x3, Pallas kernels: none -> 161 us  [the longest x1 112 us: project(): pl.pallas_call(functools.partial(project_kernel, z_), out_shape=(jax.Shap...]
    reduce_scatter x6 -> x4, waiting for transfers between devices: 246 us -> 114 us  [on_device(): lax.psum_scatter(g.astype(BF16), 'fsdp', scatter_dimension=axis, tiled=True)]
    reduce_sum x11 -> x2, other arithmetic: 36.1 us -> 0.27 us  [the longest x1 0.18 us: sequence_ends(): in_order = jnp.sum(chosen * lengths_row[None, :], axis=1)]
    all_to_all x0 -> x2, waiting for transfers between devices: none -> 34.8 us  [heads_to_tokens(): lax.all_to_all(packed, 'ctx', split_axis=1, concat_axis=1, tiled=True)]
    convert_element_type x3 -> x2, local copies, waits for them, and re-layouts: 27 us -> 5.86 us  [the longest x1 3.15 us: on_device(): pair_grad = pair_grad.astype(F32)]
    reshape x1 -> x10, local copies, waits for them, and re-layouts: 0.01 us -> 20.6 us  [the longest x3 6.46 us: unpack_values(): split = packed.reshape(4, z_.heads, z_.block, 2, HD)]
  transfers between devices with their start and end apart: 17 -> 12, of which waited for: 15 -> 9; matrix products, arithmetic and copies ran while one was open for 19% -> 8% of each run, Pallas kernels for 0% -> 0%
where the time goes in v1:
time: 839 us; the launch traced here: 830 us
  waiting for transfers between devices  382 us (46%)
  Pallas kernels  161 us (19%)
  local copies, waits for them, and re-layouts  98.1 us (12%)
  other arithmetic  79.1 us (9%)
  matrix products  48.2 us (6%)
  blocking collectives  37.4 us (4%)
  between operations  16.2 us (2%)
  starting transfers between devices  8.44 us (1%)
    reduce_scatter x4, waiting for transfers between devices, on_device(): lax.psum_scatter(g.astype(BF16), 'fsdp', scatter_dimension=axis, tiled=True)  114 us
    pallas_call x1, Pallas kernels, project(): pl.pallas_call(functools.partial(project_kernel, z_), out_shape=(jax.Shap...  112 us
    psum x1, waiting for transfers between devices, on_device(): shards = [lax.psum(g, 'ctx').astype(F32) for g in shards]  101 us
    psum x1, waiting for transfers between devices, on_device(): lax.psum(jnp.dot(hidden_low, down_low, preferred_element_type=F32).astype...  47.7 us
    psum x1, waiting for transfers between devices, on_device(): lax.psum(jnp.dot(attended_low, attn_low, preferred_element_type=F32).asty...  40.3 us
    psum x1, waiting for transfers between devices, on_device(): lax.psum(jnp.einsum('tkf,kdf->td', gated_grad, wide_low, preferred_elemen...  40.2 us
    all_to_all x2, waiting for transfers between devices, heads_to_tokens(): lax.all_to_all(packed, 'ctx', split_axis=1, concat_axis=1, tiled=True)  34.8 us
    pallas_call x1, Pallas kernels, attend_back(): pl.pallas_call(functools.partial(attend_back_kernel, z_, q_tile, k_tile),...  27.6 us
  transfers between devices with their start and end apart: 12, of which 9 were waited for; matrix products, arithmetic and copies ran while one was open for 8% of the time, Pallas kernels for 0%

profile of v1, /device:TPU:0, one launch (start us, length us, event | category | flops | bytes accessed | tf_op | source)
XLA Modules:
  0.0 830.2 jit_solution(3597129886478872148)
XLA Ops:
  8.0 2.4 copy.169
  14.4 2.0 copy.172
  20.0 2.9 convert_element_type.135
  22.8 2.7 copy.173
  26.5 2.7 pad_maximum_fusion.6.wq_ref
  30.5 112.4 %project.1 = (bf16[12,8,64,128]{3,2,1,0:T(8,128)(2,1)}, bf16[4,2,512,384]{3,2,1,0:T(8,128)(2,1)}, bf16[2,512,512]{2,1,0:T(8,128)(2,1)}, bf16[2,2,512,1312]{3,2,1,0:T(8,128)(2,1)}, f32[2,8,512]{2,1,0:T(8,128)}) custom-call(bf16[512,1024]{1,0:T(8,128)(2,1)} %tok_ref.1, f32[8,512]{1,0:T(8,128)} %pad_convert_fusion.gain_ref, ...), custom_call_target="tpu_custom_call" | custom-call | tf_op jit(solution)/shard_map/project/pallas_call | solution.py:372
  142.9 20.6 %attend.1 = (bf16[2048,128]{1,0:T(8,128)(2,1)}, f32[64,4096]{1,0:T(8,128)}, f32[8,4096]{1,0:T(8,128)}) custom-call(s32[4]{0:T(128)} %bitcast.213, bf16[6144,128]{1,0:T(8,128)(2,1)} %bitcast.187), custom_call_target="tpu_custom_call" | custom-call | tf_op jit(solution)/shard_map/attend/pallas_call | solution.py:530
  165.4 3.5 all-to-all-start
  169.6 14.7 %all-to-all-done = bf16[4,8,64,128]{3,2,0,1:T(8,128)(2,1)S(1)} async-done(((bf16[4,8,64,128]{3,2,0,1:T(8,128)(2,1)}), bf16[4,8,64,128]{3,2,0,1:T(8,128)(2,1)S(1)}, u32[]{:S(2)}, u32[]{:S(2)}) %all-to-all-start) | async-done | bytes 524320 | tf_op jit(solution)/shard_map/all_to_all | solution.py:753
  187.8 3.1 convert_element_type.140
  191.8 40.3 %all-reduce.8.cloned.1.call-done = bf16[512,1024]{1,0:T(8,128)(2,1)} async-done(((bf16[512,1024]{1,0:T(8,128)(2,1)}), bf16[512,1024]{1,0:T(8,128)(2,1)}) %all-reduce.8.cloned.1.call-update) | async-done | bytes 1048592 | tf_op jit(solution)/shard_map/psum | solution.py:832
  234.3 9.5 %fusion.67 = f32[512,2,1312]{0,2,1:T(8,128)} fusion(bf16[2,1024,1312]{2,1,0:T(8,128)(2,1)} %bitcast.217, f32[1024]{0:T(1024)S(1)} %bitcast.208, bf16[512,1024]{1,0:T(8,128)(2,1)S(1)} %copy-done.3, bf16[512,1024]{1,0:T(8,128)(2,1)S(1)} %copy-done, f32[512]{0:T(512)S(1)} %add_rsqrt_fusion.1, f32[512]{0:T(512)S(1)} %broadcast_multiply_fusion.5), kind=kOutput, calls=%fused_computation.124 | convolution fusion | flops 2755133440 | bytes 12853248 | tf_op jit(solution)/shard_map/td,kdf->tkf/dot_general | solution.py:838
  243.8 3.5 fusion.101
  247.3 6.4 fusion.54
  253.8 2.7 fusion.53
  257.6 4.2 bitcast_convert_fusion.1
  261.8 40.2 %all-reduce.10.cloned.1.call-done = bf16[512,1024]{1,0:T(8,128)(2,1)} async-done(((bf16[512,1024]{1,0:T(8,128)(2,1)}), bf16[512,1024]{1,0:T(8,128)(2,1)}) %all-reduce.10.cloned.1.call-update) | async-done | bytes 1048592 | tf_op jit(solution)/shard_map/psum | solution.py:852
  302.0 2.7 fusion.45
  304.7 3.1 fusion.40
  309.3 2.4 reshape_reshape.10
  311.7 3.3 copy.180
  314.9 3.1 reshape_broadcast_in_dim_reshape.3
  318.0 20.0 %all_to_all.15 = bf16[4,8,64,128]{3,2,0,1:T(8,128)(2,1)S(1)} all-to-all(bf16[4,8,64,128]{3,2,0,1:T(8,128)(2,1)} %reshape_broadcast_in_dim_reshape.3), channel_id=1, replica_groups=mesh['fsdp'=2,'ctx'=8,'tp'=2] {'ctx'}, dimensions={1} | all-to-all | bytes 1048576 | tf_op jit(solution)/shard_map/all_to_all | solution.py:759
  338.8 27.6 %attend_back.1 = bf16[6144,128]{1,0:T(8,128)(2,1)} custom-call(s32[4]{0:T(128)} %bitcast.214, bf16[6144,128]{1,0:T(8,128)(2,1)} %bitcast.188, bf16[2048,128]{1,0:T(8,128)(2,1)} %bitcast.199, f32[64,4096]{1,0:T(8,128)} %get-tuple-element.30.outt_ref, f32[8,4096]{1,0:T(8,128)} %get-tuple-element.31.lse_ref), custom_call_target="tpu_custom_call" | custom-call | tf_op jit(solution)/shard_map/attend_back/pallas_call | solution.py:691
  366.4 2.8 copy.182
  369.2 4.3 all-to-all-start.2
  376.2 2.5 broadcast_in_dim.16
  378.7 3.0 copy.190
  383.3 2.9 copy.186
  386.2 4.9 convolution_convert_fusion.2
  391.2 20.2 %all-to-all-done.2 = bf16[12,8,64,128]{3,2,0,1:T(8,128)(2,1)} async-done(((bf16[12,8,64,128]{3,2,0,1:T(8,128)(2,1)}), bf16[12,8,64,128]{3,2,0,1:T(8,128)(2,1)}, u32[]{:S(2)}, u32[]{:S(2)}) %all-to-all-start.2) | async-done | bytes 1572896 | tf_op jit(solution)/shard_map/all_to_all | solution.py:753
  414.7 2.7 fusion.98
  417.3 2.7 fusion.99
  421.8 3.2 reshape.234
  425.0 2.9 copy.223
  427.9 2.6 reshape_reshape.11
  432.4 4.2 pad_maximum_fusion.3
  436.5 3.2 concatenate.33
  439.7 4.2 pad_maximum_fusion.2
  443.8 3.2 concatenate.31
  447.0 3.2 reshape.240
  450.1 5.3 fusion.50
  456.4 2.8 bitcast_convert_fusion
  459.5 2.7 convolution_convert_fusion.3
  462.3 4.7 convolution_convert_fusion.1
  467.1 7.6 convolution_convert_fusion
  474.8 5.0 convert_bitcast_fusion
  479.9 47.7 %all-reduce.14.cloned.1.call-done = (bf16[512,1024]{1,0:T(8,128)(2,1)}, bf16[512,1024]{1,0:T(8,128)(2,1)}) async-done(((bf16[512,1024]{1,0:T(8,128)(2,1)}, bf16[512,1024]{1,0:T(8,128)(2,1)}), (bf16[512,1024]{1,0:T(8,128)(2,1)}, bf16[512,1024]{1,0:T(8,128)(2,1)})) %all-reduce.14.cloned.1.call-update) | async-done | bytes 2097168 | tf_op jit(solution)/shard_map/psum | solution.py:841
  527.6 2.2 fusion.47
  530.9 68.1 %reduce-scatter.12.cloned.1.call-done = bf16[512,2,1312]{0,2,1:T(8,128)(2,1)} async-done(((bf16[1024,2,1312]{0,2,1:T(8,128)(2,1)}), bf16[512,2,1312]{0,2,1:T(8,128)(2,1)}) %reduce-scatter.12.cloned.1.call-update) | async-done | bytes 2686992 | tf_op jit(solution)/shard_map/reduce_scatter | solution.py:904
  599.0 46.1 %reduce-scatter.8.cloned.1.call-done = bf16[4,512,384]{1,2,0:T(8,128)(2,1)} async-done(((bf16[4,1024,384]{1,2,0:T(8,128)(2,1)}), bf16[4,512,384]{1,2,0:T(8,128)(2,1)}) %reduce-scatter.8.cloned.1.call-update) | async-done | bytes 1572880 | tf_op jit(solution)/shard_map/reduce_scatter | solution.py:904
  645.2 3.5 copy.193
  648.7 3.5 copy.196
  652.3 4.2 fusion.38
  656.5 3.1 reduce-scatter.16.cloned.1.call-done
  660.6 17.5 %psum.71 = bf16[2,512]{1,0:T(2,128)(2,1)S(1)} all-reduce(bf16[2,512]{1,0:T(2,128)(2,1)S(1)} %copy.206), channel_id=1, replica_groups=mesh['fsdp'=2,'ctx'=8,'tp'=2] {'ctx'}, use_global_device_ids=true, to_apply=%region_26.27 | all-reduce | flops 1024 | bytes 4096 | tf_op jit(solution)/shard_map/psum | solution.py:913
  678.7 101.4 %all-reduce.12.cloned.1.call-done = (bf16[4,512,384]{1,2,0:T(8,128)(2,1)}, bf16[512,512]{1,0:T(8,128)(2,1)}, bf16[512,2,1312]{0,2,1:T(8,128)(2,1)}, bf16[1312,512]{1,0:T(8,128)(2,1)}) async-done(((bf16[4,512,384]{1,2,0:T(8,128)(2,1)}, bf16[512,512]{1,0:T(8,128)(2,1)}, bf16[512,2,1312]{0,2,1:T(8,128)(2,1)}, bf16[1312,512]{1,0:T(8,128)(2,1)}), (bf16[4,512,384]{1,2,0:T(8,128)(2,1)}, ...) | async-done | bytes 6127632 | tf_op jit(solution)/shard_map/psum | solution.py:913
  785.2 4.8 multiply_subtract_fusion.1
  790.0 3.5 copy.199
  793.5 3.7 copy.200
  797.2 2.4 copy.201
  799.6 4.4 multiply_subtract_fusion.3
  804.0 12.4 %multiply_subtract_fusion = (f32[512,2,1312]{0,2,1:T(8,128)}, f32[512,2,1312]{0,2,1:T(8,128)}, f32[512,2,1312]{0,2,1:T(8,128)}) fusion(f32[512,2,1312]{0,2,1:T(8,128)} %param.25, bf16[512,2,1312]{0,2,1:T(8,128)(2,1)S(1)} %copy-done.13, f32[512,2,1312]{0,2,1:T(8,128)} %param.30, f32[512,2,1312]{0,2,1:T(8,128)} %param.35), kind=kLoop, calls=%fused_computation.4 | loop fusion | flops 21495808 | bytes 34930688 | tf_op jit(solution)/shard_map/sub | solution.py:717
  817.9 4.7 multiply_subtract_fusion.2
  (148 shorter events, 44.3 us)
Async XLA Ops:
  10.4 1.8 copy-start.1
  10.6 2.7 copy-start.26
  10.7 3.3 copy-start.31
  10.7 3.3 copy-start.32
  13.3 5.8 copy-start.12
  14.3 5.6 copy-start.27
  142.9 26.0 %copy-start.23 = (bf16[2,512,512]{2,1,0:T(8,128)(2,1)S(1)}, bf16[2,512,512]{2,1,0:T(8,128)(2,1)}, u32[]{:S(2)}) copy-start(bf16[2,512,512]{2,1,0:T(8,128)(2,1)} %get-tuple-element.27) | copy-start | bytes 3145732
  165.4 18.8 %all-to-all-start = ((bf16[4,8,64,128]{3,2,0,1:T(8,128)(2,1)}), bf16[4,8,64,128]{3,2,0,1:T(8,128)(2,1)S(1)}, u32[]{:S(2)}, u32[]{:S(2)}) async-start(bf16[4,8,64,128]{3,2,0,1:T(8,128)(2,1)} %copy.174), calls=%async_computation | async-start | bytes 1048576 | tf_op jit(solution)/shard_map/all_to_all | solution.py:753
  168.9 63.2 %all-reduce.8.cloned.1.call-start = ((), (), s32[]{:S(2)}) async-start(), calls=%async_computation.8 | async-start | bytes 2097152 | tf_op jit(solution)/shard_map/psum | solution.py:832
  169.5 16.5 %copy-start.9 = (bf16[512,2,512]{0,2,1:T(8,128)(2,1)}, bf16[512,2,512]{0,2,1:T(8,128)(2,1)S(1)}, u32[]{:S(2)}) copy-start(bf16[512,2,512]{0,2,1:T(8,128)(2,1)S(1)} %copy.177) | copy-start | bytes 3145732
  186.0 4.9 copy-start.17
  187.7 44.4 %copy-start = (bf16[512,1024]{1,0:T(8,128)(2,1)S(1)}, bf16[512,1024]{1,0:T(8,128)(2,1)}, u32[]{:S(2)}) copy-start(bf16[512,1024]{1,0:T(8,128)(2,1)} %tok_ref.1) | copy-start | bytes 3145732
  187.7 56.1 %all-gather.2.cloned.1.call-start = ((), (), s32[]{:S(2)}) async-start(), calls=%async_computation.9 | async-start | bytes 4030464 | tf_op jit(solution)/shard_map/all_gather | solution.py:820
  190.9 111.1 %all-reduce.10.cloned.1.call-start = ((), (), s32[]{:S(2)}) async-start(), calls=%async_computation.10 | async-start | bytes 2097152 | tf_op jit(solution)/shard_map/psum | solution.py:852
  232.1 1.7 copy-start.3
  234.3 9.5 %copy-start.24 = (bf16[512,1024]{1,0:T(8,128)(2,1)S(1)}, bf16[512,1024]{1,0:T(8,128)(2,1)}, u32[]{:S(2)}) copy-start(bf16[512,1024]{1,0:T(8,128)(2,1)} %param.20) | copy-start | bytes 3145732
  243.8 3.5 copy-start.4
  247.3 10.2 %slice-start = ((s8[5767168]{0:T(1024)(128)(4,1)}), s8[4194304]{0:T(1024)(128)(4,1)S(1)}, s32[]{:S(2)}) async-start(s8[5767168]{0:T(1024)(128)(4,1)} %bitcast.218), calls=%async_computation.18 | async-start | bytes 8388608
  253.8 2.7 copy-start.19
  253.8 3.8 slice-start.1
  256.5 1.1 copy-start.20
  302.0 2.7 copy-start.11
  304.7 3.1 copy-start.10
  366.4 8.9 %copy-start.16 = (f32[512,128]{1,0:T(8,128)S(1)}, f32[512,128]{1,0:T(8,128)}, u32[]{:S(2)}) copy-start(f32[512,128]{1,0:T(8,128)} %get-tuple-element.165.cos_ref) | copy-start | bytes 786436
  369.2 42.1 %all-to-all-start.2 = ((bf16[12,8,64,128]{3,2,0,1:T(8,128)(2,1)}), bf16[12,8,64,128]{3,2,0,1:T(8,128)(2,1)}, u32[]{:S(2)}, u32[]{:S(2)}) async-start(bf16[12,8,64,128]{3,2,0,1:T(8,128)(2,1)} %copy.182), calls=%async_computation.2 | async-start | bytes 3145728 | tf_op jit(solution)/shard_map/all_to_all | solution.py:753
  373.5 154.1 %all-reduce.14.cloned.1.call-start = ((), (), s32[]{:S(2)}) async-start(), calls=%async_computation.17 | async-start | bytes 4194304 | tf_op jit(solution)/shard_map/psum | solution.py:841
  378.7 3.0 copy-start.22
  450.1 6.3 copy-start.25
  450.1 6.3 copy-start.30
  455.4 1.0 copy-start.21
  459.2 71.6 %reduce-scatter.10.cloned.1.call-start = ((), (), s32[]{:S(2)}) async-start(), calls=%async_computation.12 | async-start | bytes 1572864 | tf_op jit(solution)/shard_map/reduce_scatter | solution.py:904
  462.2 68.6 %reduce-scatter.14.cloned.1.call-start = ((), (), s32[]{:S(2)}) async-start(), calls=%async_computation.14 | async-start | bytes 4030464 | tf_op jit(solution)/shard_map/reduce_scatter | solution.py:904
  467.0 132.0 %reduce-scatter.12.cloned.1.call-start = ((), (), s32[]{:S(2)}) async-start(), calls=%async_computation.13 | async-start | bytes 8060928 | tf_op jit(solution)/shard_map/reduce_scatter | solution.py:904
  474.7 170.4 %reduce-scatter.8.cloned.1.call-start = ((), (), s32[]{:S(2)}) async-start(), calls=%async_computation.11 | async-start | bytes 4718592 | tf_op jit(solution)/shard_map/reduce_scatter | solution.py:904
  479.8 179.8 %reduce-scatter.16.cloned.1.call-start = ((), (), s32[]{:S(2)}) async-start(), calls=%async_computation.15 | async-start | bytes 393216
  530.8 249.3 %all-reduce.12.cloned.1.call-start = ((), (), s32[]{:S(2)}) async-start(), calls=%async_computation.16 | async-start | bytes 12255232 | tf_op jit(solution)/shard_map/psum | solution.py:913
  652.3 25.8 %copy-start.28 = (f32[2,512]{1,0:T(2,128)S(1)}, f32[2,512]{1,0:T(2,128)}, u32[]{:S(2)}) copy-start(f32[2,512]{1,0:T(2,128)} %param.32) | copy-start | bytes 12292
  652.3 25.8 %copy-start.29 = (f32[2,512]{1,0:T(2,128)S(1)}, f32[2,512]{1,0:T(2,128)}, u32[]{:S(2)}) copy-start(f32[2,512]{1,0:T(2,128)} %param.37) | copy-start | bytes 12292
  780.1 3.3 copy-start.6
  781.4 2.4 copy-start.5
  783.1 2.1 copy-start.2
  793.5 3.7 copy-start.7
  799.6 4.4 copy-start.13
  804.0 12.4 %copy-start.8 = (f32[1312,512]{1,0:T(8,128)S(1)}, f32[1312,512]{1,0:T(8,128)}, u32[]{:S(2)}) copy-start(f32[1312,512]{1,0:T(8,128)} %param.26) | copy-start | bytes 8060932
  804.0 12.4 %copy-start.14 = (f32[1312,512]{1,0:T(8,128)S(1)}, f32[1312,512]{1,0:T(8,128)}, u32[]{:S(2)}) copy-start(f32[1312,512]{1,0:T(8,128)} %param.31) | copy-start | bytes 8060932
  804.0 13.6 %copy-start.15 = (f32[1312,512]{1,0:T(8,128)S(1)}, f32[1312,512]{1,0:T(8,128)}, u32[]{:S(2)}) copy-start(f32[1312,512]{1,0:T(8,128)} %param.36) | copy-start | bytes 8060932
  804.0 13.9 %copy-start.18 = (bf16[1312,512]{1,0:T(8,128)(2,1)S(1)}, bf16[1312,512]{1,0:T(8,128)(2,1)}, u32[]{:S(2)}) copy-start(bf16[1312,512]{1,0:T(8,128)(2,1)} %get-tuple-element.128) | copy-start | bytes 4030468
Sparse Core Ops, SparseCore 0:
  187.9 44.2 all-reduce.7
  261.9 40.0 all-reduce.9
  459.3 68.2 all-reduce.13
  645.3 134.7 all-reduce.11
Sparse Core Ops, SparseCore 1:
  191.0 43.8 all-gather.1
  462.6 25.3 reduce-scatter.9
  490.7 38.2 reduce-scatter.13
  532.0 67.0 reduce-scatter.11
  601.8 43.2 reduce-scatter.7
  648.0 11.6 reduce-scatter.15

commit v2 on v1

--- a/solution.py
+++ b/solution.py
@@ -441,6 +441,8 @@
     piece = min(512, half)
     scaling = HD ** (-0.5)
     sums = 16
+    packed_ref = packed_ref.reshape(group + half, 2 * HD)
+    out_ref = out_ref.reshape(half, 2 * HD)
     query_s[0:HD, :] = jnp.zeros((HD, group), BF16)
     value_s[HD : HD + sums, :] = jnp.ones((sums, group), BF16)
 
@@ -530,7 +532,7 @@
     return pl.pallas_call(
         functools.partial(attend_kernel, z_, q_tile, k_tile),
         out_shape=(
-            jax.ShapeDtypeStruct((group // 2, 2 * HD), BF16),
+            jax.ShapeDtypeStruct((4, z_.ctx, z_.block, 2 * HD), BF16),
             jax.ShapeDtypeStruct((HD, group), F32),
             jax.ShapeDtypeStruct((8, group), F32),
         ),
@@ -571,6 +573,9 @@
     half = group // 2
     piece = min(512, half)
     scaling = HD ** (-0.5)
+    packed_ref = packed_ref.reshape(group + half, 2 * HD)
+    grad_ref = grad_ref.reshape(half, 2 * HD)
+    out_ref = out_ref.reshape(group + half, 2 * HD)
     query_s[0:HD, :] = jnp.zeros((HD, group), BF16)
     gradt_s[0:HD, :] = jnp.zeros((HD, group), BF16)
     gradt_s[2 * HD : 3 * HD, :] = jnp.zeros((HD, group), BF16)
@@ -690,7 +695,7 @@
     group = z_.group
     return pl.pallas_call(
         functools.partial(attend_back_kernel, z_, q_tile, k_tile),
-        out_shape=jax.ShapeDtypeStruct((group + group // 2, 2 * HD), BF16),
+        out_shape=jax.ShapeDtypeStruct((12, z_.ctx, z_.block, 2 * HD), BF16),
         in_specs=[pl.BlockSpec(memory_space=pltpu.SMEM)] + [vmem()] * 4,
         out_specs=vmem(),
         scratch_shapes=[
@@ -707,6 +712,553 @@
         compiler_params=pltpu.CompilerParams(vmem_limit_bytes=VMEM_BYTES),
         name="attend_back",
     )(ends, packed, grads, outt, lse)
+
+
+def cuts_of(rows, count):
+    unit = rows // 16
+    marks = [16 * (unit * i // count) for i in range(count + 1)]
+    return [(a, b - a) for a, b in zip(marks, marks[1:]) if b > a]
+
+
+def over_rows(start, rows, step, body):
+    whole = rows // step
+
+    def turn(i, carried):
+        body(pl.multiple_of(start + i * step, 16), step)
+        return carried
+
+    if whole > 1:
+        lax.fori_loop(0, whole, turn, 0)
+    elif whole == 1:
+        body(start, step)
+    if rows % step:
+        body(start + whole * step, rows % step)
+
+
+class Item:
+    def __init__(self, number, rows, columns, cuts):
+        self.number = number
+        self.rows = rows
+        self.columns = columns
+        self.cuts = cuts_of(rows, cuts)
+
+
+class Reducer:
+    def __init__(self, z_, items, refs, sems):
+        self.z_ = z_
+        self.items = items
+        self.refs = refs
+        self.sems = sems
+        f, c, t = lax.axis_index("fsdp"), lax.axis_index("ctx"), lax.axis_index("tp")
+        self.f, self.c, self.t = f, c, t
+        self.core = lax.rem(c, 2)
+        self.chip = c // 2
+        self.mate = (f, c + 1 - 2 * self.core, t)
+        middle = z_.chips // 2
+        low = self.chip < middle
+        self.is_mid = (self.chip == middle - 1) | (self.chip == middle)
+        self.has_outer = (self.chip > 0) & (self.chip < z_.chips - 1)
+        towards = jnp.where(low, 2, -2)
+        self.inner = (f, c + towards, t)
+        self.outer = (f, c - towards, t)
+        self.numbers = {}
+        for item in items:
+            for cut in range(len(item.cuts)):
+                self.numbers[(item.number, cut)] = len(self.numbers)
+
+    def ahead(self, k):
+        return lax.rem(self.f + k, self.z_.fsdp)
+
+    def behind(self, k):
+        return lax.rem(self.f + self.z_.fsdp - k, self.z_.fsdp)
+
+
+    def core_copy(self, item):
+        source, own, mate_in = self.refs[item.number][:3]
+        n = item.number
+        return remote(
+            source.at[:, 1 - self.core],
+            mate_in,
+            self.sems["core_send"].at[n],
+            self.sems["core_recv"].at[n],
+            self.mate,
+        )
+
+    def own_copy(self, item):
+        source, own = self.refs[item.number][:2]
+        return pltpu.make_async_copy(
+            source.at[:, self.core], own, self.sems["own"].at[item.number]
+        )
+
+    def core_sum(self, item):
+        own, mate_in = self.refs[item.number][1:3]
+        self.core_copy(item).wait_recv()
+        for g in range(self.z_.fsdp):
+
+            def add(first, rows, g=g):
+                place = pl.ds(first, rows)
+                own[g, place, :] = (
+                    own[g, place, :].astype(F32) + mate_in[g, place, :].astype(F32)
+                ).astype(BF16)
+
+            over_rows(0, item.rows, 128, add)
+
+
+    def peer_copy(self, item, k, owner):
+        own, peer_in = self.refs[item.number][1], self.refs[item.number][3]
+        return remote(
+            own.at[owner],
+            peer_in.at[k - 1],
+            self.sems["peer_send"].at[item.number, k - 1],
+            self.sems["peer_recv"].at[item.number, k - 1],
+            (self.ahead(k), self.c, self.t),
+        )
+
+    def peer_start(self, item):
+        for k in range(1, self.z_.fsdp):
+            self.peer_copy(item, k, self.ahead(k)).start()
+
+    def peer_sum(self, item):
+        own, peer_in = self.refs[item.number][1], self.refs[item.number][3]
+        for k in range(1, self.z_.fsdp):
+            self.peer_copy(item, k, self.ahead(k)).wait_recv()
+
+        def add(first, rows):
+            place = pl.ds(first, rows)
+            total = own[self.f, place, :].astype(F32)
+            for k in range(1, self.z_.fsdp):
+                total = total + peer_in[k - 1, place, :].astype(F32)
+            own[self.f, place, :] = total.astype(BF16)
+
+        over_rows(0, item.rows, 128, add)
+
+
+    def in_copy(self, item, cut, middle):
+        own, peer_in, outer_in, inner_in = self.refs[item.number][1:2] + self.refs[item.number][3:6]
+        rows = pl.ds(*item.cuts[cut])
+        n = self.numbers[(item.number, cut)]
+        if middle:
+            target, name = inner_in, "inner_recv"
+        else:
+            target, name = outer_in, "outer_recv"
+        return remote(
+            own.at[self.f, rows],
+            target.at[rows],
+            self.sems["in_send"].at[n],
+            self.sems[name].at[n],
+            self.inner,
+        )
+
+    def out_copy(self, item, cut):
+        inner_in = self.refs[item.number][5]
+        rows = pl.ds(*item.cuts[cut])
+        n = self.numbers[(item.number, cut)]
+        return remote(
+            inner_in.at[rows],
+            inner_in.at[rows],
+            self.sems["out_send"].at[n],
+            self.sems["inner_recv"].at[n],
+            self.outer,
+        )
+
+    def done_copy(self, item, cut):
+        inner_in, out = self.refs[item.number][5:7]
+        rows = pl.ds(*item.cuts[cut])
+        n = self.numbers[(item.number, cut)]
+        return remote(
+            inner_in.at[rows],
+            out.at[self.core, rows],
+            self.sems["done_send"].at[n],
+            self.sems["done_recv"].at[n],
+            self.mate,
+        )
+
+    def keep_copy(self, item, cut):
+        inner_in, out = self.refs[item.number][5:7]
+        rows = pl.ds(*item.cuts[cut])
+        n = self.numbers[(item.number, cut)]
+        return pltpu.make_async_copy(
+            inner_in.at[rows], out.at[self.core, rows], self.sems["keep"].at[n]
+        )
+
+    def outermost_start(self, item):
+        @pl.when(jnp.logical_not(self.has_outer))
+        def first():
+            for cut in range(len(item.cuts)):
+                self.inward_start(item, cut)
+
+    def inward_start(self, item, cut):
+        @pl.when(self.is_mid)
+        def cross():
+            self.in_copy(item, cut, True).start()
+
+        @pl.when(jnp.logical_not(self.is_mid))
+        def along():
+            self.in_copy(item, cut, False).start()
+
+    def inward(self, item, cut):
+        own, outer_in = self.refs[item.number][1], self.refs[item.number][4]
+        first, rows = item.cuts[cut]
+
+        @pl.when(self.has_outer)
+        def passed():
+            self.in_copy(item, cut, False).wait_recv()
+
+            def add(start, count):
+                place = pl.ds(start, count)
+                own[self.f, place, :] = (
+                    own[self.f, place, :].astype(F32) + outer_in[place, :].astype(F32)
+                ).astype(BF16)
+
+            over_rows(first, rows, 128, add)
+            self.inward_start(item, cut)
+
+    def outward(self, item, cut):
+        own, inner_in = self.refs[item.number][1], self.refs[item.number][5]
+        first, rows = item.cuts[cut]
+        self.out_copy(item, cut).wait_recv()
+
+        @pl.when(self.is_mid)
+        def total():
+            def add(start, count):
+                place = pl.ds(start, count)
+                inner_in[place, :] = (
+                    own[self.f, place, :].astype(F32) + inner_in[place, :].astype(F32)
+                ).astype(BF16)
+
+            over_rows(first, rows, 128, add)
+
+        @pl.when(self.has_outer)
+        def onward():
+            self.out_copy(item, cut).start()
+
+        self.done_copy(item, cut).start()
+        self.keep_copy(item, cut).start()
+
+    def line(self, parts):
+        for i, (item, cut) in enumerate(parts):
+            self.inward(item, cut)
+            if i:
+                self.outward(*parts[i - 1])
+        self.outward(*parts[-1])
+
+    def settle(self):
+        for item in self.items:
+            self.core_copy(item).wait_send()
+            for k in range(1, self.z_.fsdp):
+                self.peer_copy(item, k, self.ahead(k)).wait_send()
+            for cut in range(len(item.cuts)):
+                self.in_copy(item, cut, False).wait_send()
+
+                @pl.when(self.has_outer)
+                def outwards(item=item, cut=cut):
+                    self.out_copy(item, cut).wait_send()
+
+                self.done_copy(item, cut).wait()
+                self.keep_copy(item, cut).wait()
+
+
+def reduce_kernel(
+    z_,
+    items,
+    tok_ref,
+    gain_ref,
+    cos_ref,
+    sin_ref,
+    branch_ref,
+    middle_ref,
+    mgrad_ref,
+    gain2_ref,
+    heads_ref,
+    wq_ref,
+    g_down,
+    g_wide,
+    g_attn,
+    out_ref,
+    igrad_ref,
+    o_down,
+    o_wide,
+    o_attn,
+    o_qkv,
+    o_gain,
+    *scratch,
+):
+    down, wide, attn, qkv, gain = items
+    scratch = list(scratch)
+
+    def take(count):
+        taken = scratch[:count]
+        del scratch[:count]
+        return taken
+
+    heads_s, wq_s, entry_s, grads_s, branch_s, back_s, back_in = take(7)
+    g_qkv, g_gain, gain_acc = take(3)
+    groups = [take(5) for item in items]
+    (a_send, a_recv, y_send, y_recv, local_sem) = take(5)
+    names = (
+        "core_send",
+        "core_recv",
+        "own",
+        "peer_send",
+        "peer_recv",
+        "in_send",
+        "outer_recv",
+        "inner_recv",
+        "out_send",
+        "done_send",
+        "done_recv",
+        "keep",
+    )
+    sems = dict(zip(names, take(len(names))))
+    sources = (g_down, g_wide, g_attn, g_qkv, g_gain)
+    outs = (o_down, o_wide, o_attn, o_qkv, o_gain)
+    refs = [
+        (source, *group, out) for source, group, out in zip(sources, groups, outs)
+    ]
+    red = Reducer(z_, items, refs, sems)
+    f, c, t = red.f, red.c, red.t
+    other = (f, c, 1 - t)
+    count = z_.ctx // z_.share
+
+    def to_token(j):
+        return lax.rem(c + z_.share * j, z_.ctx)
+
+    def from_head(j):
+        return lax.rem(c + z_.ctx - z_.share * j, z_.ctx)
+
+    def heads_copy(j):
+        return remote(
+            heads_ref.at[:, to_token(j)],
+            heads_s.at[c // z_.share],
+            a_send.at[j],
+            a_recv.at[j],
+            (f, to_token(j), t),
+        )
+
+    def branch_copy():
+        return remote(branch_ref, branch_s, y_send.at[0], y_recv.at[0], other)
+
+    def back_copy():
+        return remote(back_s, back_in, y_send.at[1], y_recv.at[1], other)
+
+    greet(
+        [(red.ahead(k), c, t) for k in range(1, z_.fsdp)]
+        + [(f, lax.rem(c + j, z_.ctx), t) for j in range(1, z_.ctx)]
+        + [other]
+    )
+    for j in range(1, count):
+        heads_copy(j).start()
+    branch_copy().start()
+    own_heads = pltpu.make_async_copy(heads_ref.at[:, c], heads_s.at[c // z_.share], local_sem.at[0])
+    own_heads.start()
+    for item in (down, wide, attn):
+        red.core_copy(item).start()
+        red.own_copy(item).start()
+    load_wq = pltpu.make_async_copy(wq_ref, wq_s, local_sem.at[1])
+    load_wq.start()
+
+    for item in (down, wide, attn):
+        red.own_copy(item).wait()
+        red.core_sum(item)
+        red.peer_start(item)
+
+    tile = min(128, z_.rows)
+
+    def entry_tile(i, carried):
+        rows = pl.ds(pl.multiple_of(i * tile, tile), tile)
+        normed, nothing = normalize(tok_ref[rows, :].astype(F32))
+        for g in range(z_.fsdp):
+            columns = slice(g * z_.shard, (g + 1) * z_.shard)
+            entry_s[g, :, rows] = (normed[:, columns] * gain_ref[g, 0:1, :]).T.astype(BF16)
+        return carried
+
+    lax.fori_loop(0, z_.rows // tile, entry_tile, 0)
+
+    red.peer_sum(down)
+    red.outermost_start(down)
+
+    branch_copy().wait_recv()
+
+    def output_tile(i, carried):
+        rows = pl.ds(pl.multiple_of(i * tile, tile), tile)
+        branch = branch_ref[rows, :].astype(F32) + branch_s[rows, :].astype(F32)
+        out_ref[rows, :] = (middle_ref[rows, :] + branch).astype(BF16)
+        return carried
+
+    lax.fori_loop(0, z_.rows // tile, output_tile, 0)
+
+    own_heads.wait()
+    for j in range(1, count):
+        remote(
+            heads_ref.at[:, c],
+            heads_s.at[from_head(j) // z_.share],
+            a_send.at[j],
+            a_recv.at[j],
+            red.mate,
+        ).wait_recv()
+    load_wq.wait()
+
+    def chunk_grads(p, carried):
+        for i in range(z_.chip_heads):
+            h = p * z_.chip_heads + i
+            pair = heads_s[h, 0:8].reshape(z_.rows, 2 * HD).astype(F32)
+            pair = pair * cos_ref[...] - swap_halves(pair) * sin_ref[...]
+            grads_s[p, :, 2 * HD * i : 2 * HD * (i + 1)] = pair.astype(BF16)
+            value = heads_s[h, 8:12].reshape(z_.rows // 2, 2 * HD).astype(F32)
+            start = z_.chip_heads * 2 * HD + HD * i
+            grads_s[p, 0 : z_.rows // 2, start : start + HD] = value[:, 0:HD].astype(BF16)
+            grads_s[p, z_.rows // 2 :, start : start + HD] = value[:, HD : 2 * HD].astype(BF16)
+        return carried
+
+    lax.fori_loop(0, z_.chips, chunk_grads, 0)
+
+    for g in range(z_.fsdp):
+        columns = slice(g * z_.shard, (g + 1) * z_.shard)
+
+        def back_tile(i, carried):
+            rows = pl.ds(pl.multiple_of(i * tile, tile), tile)
+            total = jnp.zeros((tile, z_.shard), F32)
+            for p in range(z_.chips):
+                total = total + lax.dot_general(
+                    grads_s[p, rows, :],
+                    wq_s[p, g],
+                    (((1,), (1,)), ((), ())),
+                    preferred_element_type=F32,
+                )
+            back_s[rows, columns] = total.astype(BF16)
+            return carried
+
+        lax.fori_loop(0, z_.rows // tile, back_tile, 0)
+    back_copy().start()
+
+    half = z_.shard // 2
+
+    def qkv_tile(p, carried):
+        for g in range(z_.fsdp):
+            for side in range(2):
+                grad = jnp.dot(
+                    entry_s[g, side * half : (side + 1) * half, :],
+                    grads_s[p],
+                    preferred_element_type=F32,
+                )
+                rows = pl.ds(pl.multiple_of(p * half, half), half)
+                g_qkv[g, side, rows, :] = grad.astype(BF16)
+        return carried
+
+    lax.fori_loop(0, z_.chips, qkv_tile, 0)
+    red.core_copy(qkv).start()
+    red.own_copy(qkv).start()
+    red.peer_sum(wide)
+    red.outermost_start(wide)
+    red.own_copy(qkv).wait()
+    red.core_sum(qkv)
+    red.peer_start(qkv)
+    red.peer_sum(attn)
+    red.outermost_start(attn)
+
+    parts = [(item, cut) for item in (down, wide, attn) for cut in range(len(item.cuts))]
+    early = len(parts) - 2
+    red.line(parts[:early])
+
+    back_copy().wait_recv()
+    gain_acc[...] = jnp.zeros(gain_acc.shape, F32)
+
+    def input_tile(i, carried):
+        rows = pl.ds(pl.multiple_of(i * tile, tile), tile)
+        normed, scaling = normalize(tok_ref[rows, :].astype(F32))
+        back = back_s[rows, :].astype(F32) + back_in[rows, :].astype(F32)
+        gain_acc[0:1, :] += jnp.sum(back * normed, axis=0, keepdims=True)
+        gains = jnp.concatenate([gain_ref[g, 0:1, :] for g in range(z_.fsdp)], axis=1)
+        igrad_ref[rows, :] = (
+            mgrad_ref[rows, :] + norm_back(back * gains, normed, scaling)
+        ).astype(BF16)
+        return carried
+
+    lax.fori_loop(0, z_.rows // tile, input_tile, 0)
+    top = lax.broadcasted_iota(jnp.int32, (16, z_.shard), 0) == 0
+    for g in range(z_.fsdp):
+        columns = slice(g * z_.shard, (g + 1) * z_.shard)
+        for side, row in ((0, gain_acc[0:1, columns]), (1, gain2_ref[0:1, columns])):
+            g_gain[g, side] = jnp.where(top, row, 0.0).astype(BF16)
+    red.core_copy(gain).start()
+    red.own_copy(gain).start()
+    red.peer_sum(qkv)
+    red.outermost_start(qkv)
+    red.own_copy(gain).wait()
+    red.core_sum(gain)
+    red.peer_start(gain)
+    rest = parts[early:] + [(qkv, cut) for cut in range(len(qkv.cuts))]
+    red.line(rest[:2])
+    red.peer_sum(gain)
+    red.outermost_start(gain)
+    red.line(rest[2:] + [(gain, 0)])
+
+    own_sends = [heads_copy(j) for j in range(1, count)] + [branch_copy(), back_copy()]
+    for copy in own_sends:
+        copy.wait_send()
+    red.settle()
+
+
+def reduce_all(
+    z_, tokens, gains, cosine, sines, branch, middle, middle_grad, gain2, heads, wq, g_down, g_wide, g_attn
+):
+    items = (
+        Item(0, z_.units // 2, z_.shard, 2),
+        Item(1, z_.shard, z_.units, 4),
+        Item(2, z_.head_width // 2, z_.shard, 1),
+        Item(3, z_.chips * (z_.shard // 2), z_.chunk, 4),
+        Item(4, 16, z_.shard, 1),
+    )
+    dma = pltpu.SemaphoreType.DMA
+    peers = max(1, z_.fsdp - 1)
+    pieces = sum(len(item.cuts) for item in items)
+    groups = []
+    for item in items:
+        groups += [
+            pltpu.VMEM((z_.fsdp, item.rows, item.columns), BF16),
+            pltpu.VMEM((z_.fsdp, item.rows, item.columns), BF16),
+            pltpu.VMEM((peers, item.rows, item.columns), BF16),
+            pltpu.VMEM((item.rows, item.columns), BF16),
+            pltpu.VMEM((item.rows, item.columns), BF16),
+        ]
+    count = z_.ctx // z_.share
+    number = len(items)
+    return pl.pallas_call(
+        functools.partial(reduce_kernel, z_, items),
+        out_shape=(
+            jax.ShapeDtypeStruct((z_.rows, z_.width), BF16),
+            jax.ShapeDtypeStruct((z_.rows, z_.width), BF16),
+        )
+        + tuple(jax.ShapeDtypeStruct((2, item.rows, item.columns), BF16) for item in items),
+        in_specs=[vmem()] * 8 + [anywhere()] * 5,
+        out_specs=tuple([vmem()] * 2 + [anywhere()] * 5),
+        scratch_shapes=[
+            pltpu.VMEM((z_.heads, 12, z_.block, 2 * HD), BF16),
+            pltpu.VMEM((z_.chips, z_.fsdp, z_.shard, z_.chunk), BF16),
+            pltpu.VMEM((z_.fsdp, z_.shard, z_.rows), BF16),
+            pltpu.VMEM((z_.chips, z_.rows, z_.chunk), BF16),
+            pltpu.VMEM((z_.rows, z_.width), BF16),
+            pltpu.VMEM((z_.rows, z_.width), BF16),
+            pltpu.VMEM((z_.rows, z_.width), BF16),
+            pltpu.VMEM((z_.fsdp, 2, items[3].rows, items[3].columns), BF16),
+            pltpu.VMEM((z_.fsdp, 2, 16, z_.shard), BF16),
+            pltpu.VMEM((8, z_.width), F32),
+        ]
+        + groups
+        + [dma((count,)), dma((count,)), dma((2,)), dma((2,)), dma((2,))]
+        + [
+            dma((number,)),
+            dma((number,)),
+            dma((number,)),
+            dma((number, peers)),
+            dma((number, peers)),
+        ]
+        + [dma((pieces,))] * 7,
+        compiler_params=pltpu.CompilerParams(
+            collective_id=1, has_side_effects=True, vmem_limit_bytes=VMEM_BYTES
+        ),
+        name="reduce",
+    )(tokens, gains, cosine, sines, branch, middle, middle_grad, gain2, heads, wq, g_down, g_wide, g_attn)
 
 
 def adam_step(weight, gradient, moment, squared, rate_now):
@@ -822,12 +1374,9 @@
     wide_low = wi_full.reshape(2, z_.width, z_.units)
     gains = gains_full.transpose(1, 0, 2).reshape(8, z_.width)
     inputs = tokens.astype(F32)
-    normed_one, scaling_one = normalize(inputs)
-    entry_one = (normed_one * gains[0][None, :]).astype(BF16)
-    packed = packed.reshape(12 * z_.ctx * z_.block, 2 * HD)
     attended_packed, attended_turned, lse = attend(z_, endings, packed)
     attended_low = unpack_values(
-        z_, heads_to_tokens(z_, attended_packed.reshape(4, z_.ctx, z_.block, 2 * HD))
+        z_, heads_to_tokens(z_, attended_packed)
     ).reshape(z_.rows, z_.head_width)
     mixed_sum = lax.psum(
         jnp.dot(attended_low, attn_low, preferred_element_type=F32).astype(BF16), "tp"
@@ -838,17 +1387,13 @@
     gate_up = jnp.einsum("td,kdf->tkf", entry_two, wide_low, preferred_element_type=F32)
     activated, gelu_pull = jax.vjp(exact_gelu, gate_up[:, 0])
     hidden_low = (activated * gate_up[:, 1]).astype(BF16)
-    branch = lax.psum(
-        jnp.dot(hidden_low, down_low, preferred_element_type=F32).astype(BF16), "tp"
-    ).astype(F32)
-    output = (middle + branch).astype(BF16)
     grad_out = cotangent.astype(F32)
     down_grad = jnp.einsum("tf,td->fd", hidden_low, cotangent, preferred_element_type=F32)
     hidden_grad = jnp.einsum("td,fd->tf", cotangent, down_low, preferred_element_type=F32)
     act_grad = gelu_pull(hidden_grad * gate_up[:, 1])[0]
     gate_grad = hidden_grad * activated
     gated_grad = jnp.stack([act_grad, gate_grad], axis=1).astype(BF16)
-    wide_grad = jnp.einsum("td,tkf->dkf", entry_two, gated_grad, preferred_element_type=F32)
+    wide_grad = jnp.einsum("td,tkf->kdf", entry_two, gated_grad, preferred_element_type=F32)
     back_two = lax.psum(
         jnp.einsum("tkf,kdf->td", gated_grad, wide_low, preferred_element_type=F32).astype(BF16),
         "tp",
@@ -867,51 +1412,41 @@
         z_,
         endings,
         packed,
-        grads_packed.reshape(z_.group // 2, 2 * HD),
+        grads_packed,
         attended_turned,
         lse,
     )
-    token_grads = heads_to_tokens(z_, head_grads.reshape(12, z_.ctx, z_.block, 2 * HD))
-    pair_grad = token_grads[0:8].transpose(0, 2, 1, 3).reshape(z_.rows * z_.heads, 2 * HD)
-    pair_grad = pair_grad.astype(F32)
-    lane = jnp.arange(2 * HD)
-    swapped = jnp.where(
-        lane % HD < HD // 2,
-        jnp.roll(pair_grad, -(HD // 2), axis=1),
-        jnp.roll(pair_grad, HD // 2, axis=1),
-    )
-    wide_cos = jnp.repeat(cosine, z_.heads, axis=0)
-    wide_sin = jnp.repeat(sines, z_.heads, axis=0)
-    pair_grad = (pair_grad * wide_cos - swapped * wide_sin).astype(BF16)
-    pair_grad = pair_grad.reshape(z_.rows, z_.chips, z_.chip_heads * 2 * HD)
-    value_grad = unpack_values(z_, token_grads[8:12]).reshape(
-        z_.rows, z_.chips, z_.chip_heads * HD
-    )
-    projected_grad = jnp.concatenate([pair_grad, value_grad], axis=2)
-    wq_flat = wq_full.reshape(z_.chips, z_.width, z_.chunk)
-    qkv_grad = jnp.einsum("td,tpc->pdc", entry_one, projected_grad, preferred_element_type=F32)
-    back_one = lax.psum(
-        jnp.einsum("tpc,pdc->td", projected_grad, wq_flat, preferred_element_type=F32).astype(BF16),
-        "tp",
-    ).astype(F32)
-    gain_first = jnp.sum(back_one * normed_one, axis=0)
-    input_grad = (
-        middle_grad + norm_back(back_one * gains[0][None, :], normed_one, scaling_one)
-    ).astype(BF16)
-    gains_grad = jnp.stack([gain_first, gain_second])
+    branch_low = jnp.dot(hidden_low, down_low, preferred_element_type=F32).astype(BF16)
+    by_half = (z_.fsdp, 2)
+    output, input_grad, down_sum, wide_sum, attn_sum, qkv_sum, gain_sum = reduce_all(
+        z_,
+        tokens,
+        gains_full,
+        cosine,
+        sines,
+        branch_low,
+        middle,
+        middle_grad,
+        jnp.broadcast_to(gain_second[None, :], (8, z_.width)),
+        head_grads,
+        wq_full,
+        down_grad.astype(BF16)
+        .reshape(2, z_.units // 2, z_.fsdp, z_.shard)
+        .transpose(2, 0, 1, 3),
+        wide_grad.astype(BF16).reshape(2, z_.fsdp, z_.shard, z_.units).transpose(1, 0, 2, 3),
+        attn_grad.astype(BF16)
+        .reshape(2, z_.head_width // 2, z_.fsdp, z_.shard)
+        .transpose(2, 0, 1, 3),
+    )
+    qkv_sum = qkv_sum.reshape(2, z_.chips, z_.shard // 2, z_.chunk).transpose(1, 0, 2, 3)
+    shards = (
+        from_chips(z_, qkv_sum.reshape(z_.chips, z_.shard, z_.chunk)).astype(F32),
+        attn_sum.reshape(z_.head_width, z_.shard).astype(F32),
+        wide_sum.transpose(1, 0, 2).astype(F32),
+        down_sum.reshape(z_.units, z_.shard).astype(F32),
+        gain_sum[:, 0, :].astype(F32),
+    )
     rates = (D ** (-0.5), RATE_ATTN, D ** (-0.5), FF ** (-0.5), RATE_GAIN)
-    shards = [
-        lax.psum_scatter(g.astype(BF16), "fsdp", scatter_dimension=axis, tiled=True)
-        for g, axis in (
-            (qkv_grad, 1),
-            (attn_grad, 1),
-            (wide_grad, 0),
-            (down_grad, 1),
-            (gains_grad, 1),
-        )
-    ]
-    shards = [lax.psum(g, "ctx").astype(F32) for g in shards]
-    shards[0] = from_chips(z_, shards[0])
     final = update_all(
         (qkv_weight, attn_weight, wide_weight, down_weight, norm_gains),
         shards,

time: 839 us -> 644 us (0.77)
  waiting for transfers between devices: 382 us -> 62.8 us
  Pallas kernels: 161 us -> 320 us
  blocking collectives: 37.4 us -> 0 us
  local copies, waits for them, and re-layouts: 98.1 us -> 133 us
  other arithmetic: 79.1 us -> 60.1 us
  matrix products: 48.2 us -> 35.7 us
    pallas_call x0 -> x1, Pallas kernels: none -> 159 us  [reduce_all(): pl.pallas_call(functools.partial(reduce_kernel, z_, items), out_shape=(ja...]
    psum x2 -> x0, waiting for transfers between devices: 149 us -> none  [the longest x1 101 us: on_device(): shards = [lax.psum(g, 'ctx').astype(F32) for g in shards]]
    reduce_scatter x4 -> x0, waiting for transfers between devices: 114 us -> none  [on_device(): lax.psum_scatter(g.astype(BF16), 'fsdp', scatter_dimension=axis, tiled=True)]
    psum x1, waiting for transfers between devices: 40.2 us -> 7.64 us  [on_device(): lax.psum(jnp.einsum('tkf,kdf->td', gated_grad, wide_low, preferred_elemen...]
    unnamed x78 -> x86, local copies, waits for them, and re-layouts: 27.1 us -> 59.3 us
    reshape x5 -> x7, local copies, waits for them, and re-layouts: 10.8 us -> 42.9 us  [the longest x2 28 us: on_device(): wide_grad.astype(BF16).reshape(2, z_.fsdp, z_.shard, z_.units)]
    all_to_all x2 -> x1, waiting for transfers between devices: 34.8 us -> 14.7 us  [heads_to_tokens(): lax.all_to_all(packed, 'ctx', split_axis=1, concat_axis=1, tiled=True)]
    all_to_all x1 -> x0, blocking collectives: 20 us -> none  [tokens_to_heads(): lax.all_to_all(jnp.repeat(packed, z_.share, axis=1), 'ctx', split_axis=1,...]
  transfers between devices with their start and end apart: 12 -> 5, of which waited for: 9 -> 3; matrix products, arithmetic and copies ran while one was open for 8% -> 15% of each run, Pallas kernels for 0% -> 0%
where the time goes in v2:
time: 644 us; the launch traced here: 636 us
  Pallas kernels  320 us (50%)
  local copies, waits for them, and re-layouts  133 us (21%)
  waiting for transfers between devices  62.8 us (10%)
  other arithmetic  60.1 us (9%)
  matrix products  35.7 us (6%)
  between operations  16.4 us (3%)
  starting transfers between devices  8.49 us (1%)
    pallas_call x1, Pallas kernels, reduce_all(): pl.pallas_call(functools.partial(reduce_kernel, z_, items), out_shape=(ja...  159 us
    pallas_call x1, Pallas kernels, project(): pl.pallas_call(functools.partial(project_kernel, z_), out_shape=(jax.Shap...  112 us
    unnamed x86, local copies, waits for them, and re-layouts  59.3 us
    psum x1, waiting for transfers between devices, on_device(): lax.psum(jnp.dot(attended_low, attn_low, preferred_element_type=F32).asty...  40.5 us
    sub x5, other arithmetic, adam_step(): weight - rate_now * (corrected / (spread + ADAM_EPS) + DECAY * weight)  30.6 us
    reshape x2, local copies, waits for them, and re-layouts, on_device(): wide_grad.astype(BF16).reshape(2, z_.fsdp, z_.shard, z_.units)  28 us
    pallas_call x1, Pallas kernels, attend_back(): pl.pallas_call(functools.partial(attend_back_kernel, z_, q_tile, k_tile),...  27.6 us
    pallas_call x1, Pallas kernels, attend(): pl.pallas_call(functools.partial(attend_kernel, z_, q_tile, k_tile), out_...  20.6 us
  transfers between devices with their start and end apart: 5, of which 3 were waited for; matrix products, arithmetic and copies ran while one was open for 15% of the time, Pallas kernels for 0%

profile of v2, /device:TPU:0, one launch (start us, length us, event | category | flops | bytes accessed | tf_op | source)
XLA Modules:
  0.0 635.9 jit_solution(3124033582978349762)
XLA Ops:
  8.0 2.4 copy.147
  10.7 1.3 slice_bitcast_fusion.1
  13.8 1.3 copy.148
  15.1 1.3 copy.149
  16.7 2.9 convert_element_type.104
  19.6 2.7 copy.151
  22.3 2.2 convert_element_type.103.wo_ref
  25.1 1.0 fusion.42
  26.1 1.3 pad_maximum_fusion.3.wq_ref
  27.4 1.3 pad_maximum_fusion.7
  28.7 112.4 %project.1 = (bf16[12,8,64,128]{3,2,1,0:T(8,128)(2,1)}, bf16[4,2,512,384]{3,2,1,0:T(8,128)(2,1)}, bf16[2,512,512]{2,1,0:T(8,128)(2,1)}, bf16[2,2,512,1312]{3,2,1,0:T(8,128)(2,1)}, f32[2,8,512]{2,1,0:T(8,128)}) custom-call(bf16[512,1024]{1,0:T(8,128)(2,1)} %tok_ref.3, f32[8,512]{1,0:T(8,128)} %pad_convert_fusion.gain_ref, ...), custom_call_target="tpu_custom_call" | custom-call | tf_op jit(solution)/shard_map/project/pallas_call | solution.py:372
  141.1 20.6 %attend.1 = (bf16[4,8,64,128]{3,2,1,0:T(8,128)(2,1)}, f32[64,4096]{1,0:T(8,128)}, f32[8,4096]{1,0:T(8,128)}) custom-call(s32[4]{0:T(128)} %bitcast.215, bf16[12,8,64,128]{3,2,1,0:T(8,128)(2,1)} %get-tuple-element.33.packed_ref), custom_call_target="tpu_custom_call" | custom-call | tf_op jit(solution)/shard_map/attend/pallas_call | solution.py:532
  161.7 1.9 copy.152
  163.6 3.5 all-to-all-start
  167.7 14.7 %all-to-all-done = bf16[4,8,64,128]{3,2,0,1:T(8,128)(2,1)S(1)} async-done(((bf16[4,8,64,128]{3,2,0,1:T(8,128)(2,1)}), bf16[4,8,64,128]{3,2,0,1:T(8,128)(2,1)S(1)}, u32[]{:S(2)}, u32[]{:S(2)}) %all-to-all-start) | async-done | bytes 524320 | tf_op jit(solution)/shard_map/all_to_all | solution.py:1305
  184.1 1.7 convolution_convert_fusion.3
  185.9 3.1 convert_element_type.110
  189.8 40.5 %all-reduce.4.cloned.1.call-done = bf16[512,1024]{1,0:T(8,128)(2,1)} async-done(((bf16[512,1024]{1,0:T(8,128)(2,1)}), bf16[512,1024]{1,0:T(8,128)(2,1)}) %all-reduce.4.cloned.1.call-update) | async-done | bytes 1048592 | tf_op jit(solution)/shard_map/psum | solution.py:1381
  230.3 1.7 fusion.61
  232.5 9.6 %fusion.59 = f32[512,2,1312]{0,2,1:T(8,128)} fusion(bf16[2,1024,1312]{2,1,0:T(8,128)(2,1)} %bitcast.218, f32[1024]{0:T(1024)S(1)} %bitcast.210, f32[512]{0:T(512)S(1)} %add_rsqrt_fusion, f32[512]{0:T(512)S(1)} %broadcast_multiply_fusion.2, bf16[512,1024]{1,0:T(8,128)(2,1)S(1)} %copy-done.5, bf16[512,1024]{1,0:T(8,128)(2,1)S(1)} %copy-done), kind=kOutput, calls=%fused_computation.126 | convolution fusion | flops 2755133440 | bytes 12853248 | tf_op jit(solution)/shard_map/td,kdf->tkf/dot_general | solution.py:1387
  242.1 3.5 fusion.73
  245.7 6.4 %fusion.36 = (bf16[512,1,1312]{0,2,1:T(8,128)(2,1)S(1)}, f32[512,1312]{0,1:T(8,128)S(1)}) fusion(f32[512,1312]{0,1:T(8,128)S(1)} %fusion.73, f32[512,2,1312]{0,2,1:T(8,128)S(1)} %copy-done.4), kind=kLoop, calls=%fused_computation.77 | loop fusion | flops 49037312 | bytes 12091392 | tf_op jit(solution)/shard_map/stack | solution.py:1395
  252.1 2.5 fusion.35
  254.7 1.1 copy-done.18
  255.7 4.2 bitcast_convert_fusion
  259.9 6.1 copy.173
  266.1 6.1 copy.170
  272.2 6.1 copy.171
  278.3 3.5 copy.162
  281.9 3.7 copy.167
  285.6 7.0 %convert_bitcast_fusion = bf16[2,1024,1312]{1,2,0:T(8,128)(2,1)} fusion(bf16[512,1,1312]{0,2,1:T(8,128)(2,1)} %copy-done.18, bf16[512,1,1312]{0,2,1:T(8,128)(2,1)S(1)} %get-tuple-element.150, f32[1024]{0:T(1024)S(1)} %bitcast.211, f32[512]{0:T(512)S(1)} %add_rsqrt_fusion, f32[512]{0:T(512)S(1)} %broadcast_multiply_fusion.2, ...), kind=kOutput, calls=%fused_computation.5 | convolution fusion | flops 2759163904 | bytes 10166272 | tf_op jit(solution)/shard_map/td,tkf->kdf/dot_general | solution.py:1396
  292.5 7.6 %all-reduce.6.cloned.1.call-done = bf16[512,1024]{1,0:T(8,128)(2,1)} async-done(((bf16[512,1024]{1,0:T(8,128)(2,1)}), bf16[512,1024]{1,0:T(8,128)(2,1)}) %all-reduce.6.cloned.1.call-update) | async-done | bytes 1048592 | tf_op jit(solution)/shard_map/psum | solution.py:1397
  300.2 2.5 fusion.33
  302.7 2.2 fusion.31
  304.9 1.5 convolution_convert_fusion.4
  306.4 1.6 reshape_reshape.7
  308.0 2.1 copy.157
  310.1 3.1 reshape_broadcast_in_dim_reshape.3
  313.1 4.9 all-to-all-start.1
  318.0 4.7 convolution_convert_fusion
  322.7 13.0 %reshape.191 = bf16[2,2,512,1312]{2,1,3,0:T(2,128)(2,1)} reshape(bf16[2,1024,1312]{1,2,0:T(8,128)(2,1)} %convert_bitcast_fusion) | data formatting | bytes 10747904 | tf_op jit(solution)/shard_map/reshape | solution.py:1436
  335.7 15.0 %copy.160 = bf16[2,2,512,1312]{3,2,0,1:T(8,128)(2,1)} copy(bf16[2,2,512,1312]{2,1,3,0:T(2,128)(2,1)} %reshape.191) | data formatting | bytes 10747904 | tf_op jit(solution)/shard_map/reshape | solution.py:1436
  350.8 7.3 %reshape.190 = bf16[2,656,2,512]{3,2,1,0:T(2,128)(2,1)} reshape(bf16[1312,1024]{1,0:T(8,128)(2,1)} %convolution_convert_fusion) | data formatting | bytes 5373952 | tf_op jit(solution)/shard_map/reshape | solution.py:1434
  358.1 3.9 copy.190
  361.9 2.8 convolution_convert_fusion.1.branch_ref
  366.3 1.1 copy.191
  367.4 1.9 copy.158.grad_ref
  369.3 27.6 %attend_back.1.heads_ref = bf16[12,8,64,128]{3,2,1,0:T(8,128)(2,1)} custom-call(s32[4]{0:T(128)} %bitcast.216, bf16[12,8,64,128]{3,2,1,0:T(8,128)(2,1)} %get-tuple-element.33.packed_ref, bf16[4,8,64,128]{3,2,1,0:T(8,128)(2,1)} %copy.158.grad_ref, f32[64,4096]{1,0:T(8,128)} %get-tuple-element.37.outt_ref, f32[8,4096]{1,0:T(8,128)} %get-tuple-element.38.lse_ref), custom_call_target="tpu_custom_call" | custom-call | tf_op jit(solution)/shard_map/attend_back/pallas_call | solution.py:696
  397.6 159.0 %reduce.1 = (bf16[512,1024]{1,0:T(8,128)(2,1)}, bf16[512,1024]{1,0:T(8,128)(2,1)}, bf16[2,656,512]{2,1,0:T(8,128)(2,1)}, bf16[2,512,1312]{2,1,0:T(8,128)(2,1)}, ...) custom-call(bf16[512,1024]{1,0:T(8,128)(2,1)} %tok_ref.3, ...), custom_call_target="tpu_custom_call" | custom-call | tf_op jit(solution)/shard_map/reduce/pallas_call | solution.py:1226
  556.5 1.7 copy.163
  558.3 1.0 slice.40
  560.2 12.1 %multiply_subtract_fusion = (f32[512,2,1312]{2,0,1:T(8,128)}, f32[512,2,1312]{2,0,1:T(8,128)}, f32[512,2,1312]{2,0,1:T(8,128)}) fusion(f32[512,2,1312]{2,0,1:T(8,128)} %copy.173, bf16[2,512,1312]{2,1,0:T(8,128)(2,1)S(1)} %copy-done.13, f32[512,2,1312]{2,0,1:T(8,128)} %copy.170, f32[512,2,1312]{2,0,1:T(8,128)} %copy.171), kind=kLoop, calls=%fused_computation.4 | loop fusion | flops 21495808 | bytes 34930688 | tf_op jit(solution)/shard_map/sub | solution.py:1269
  572.3 6.0 copy.177
  578.4 6.0 copy.178
  584.4 6.0 copy.179
  590.5 2.4 copy.164
  592.9 2.3 copy.165
  595.2 2.0 copy.166
  597.2 7.0 %multiply_subtract_fusion.1 = (f32[512,3,512]{0,2,1:T(8,128)}, f32[512,3,512]{0,2,1:T(8,128)}, f32[512,3,512]{0,2,1:T(8,128)}) fusion(f32[512,3,512]{0,2,1:T(8,128)S(1)} %copy-done.3, bf16[512,1,512]{0,2,1:T(8,128)(2,1)} %bitcast.205, bf16[512,2,512]{0,2,1:T(8,128)(2,1)} %bitcast.200, f32[512,3,512]{0,2,1:T(8,128)} %copy.162, f32[512,3,512]{0,2,1:T(8,128)} %copy.167), kind=kLoop, calls=%fused_computation.15 | loop fusion | flops 13369344 | bytes 20447232 | tf_op jit(solution)/shard_map/sub | solution.py:1269
  604.2 3.5 copy.174
  607.8 3.7 copy.175
  611.5 2.4 copy.176
  614.6 8.6 %multiply_subtract_fusion.2 = (f32[1312,512]{1,0:T(8,128)}, f32[1312,512]{1,0:T(8,128)}, f32[1312,512]{1,0:T(8,128)}) fusion(f32[1312,512]{1,0:T(8,128)} %param.26, bf16[2,656,512]{2,1,0:T(8,128)(2,1)} %get-tuple-element.45, f32[1312,512]{1,0:T(8,128)} %param.31, f32[1312,512]{1,0:T(8,128)} %param.36), kind=kLoop, calls=%fused_computation.35 | loop fusion | flops 10747904 | bytes 17465344 | tf_op jit(solution)/shard_map/sub | solution.py:1269
  623.2 2.3 multiply_subtract_fusion.3
  (109 shorter events, 13.0 us)
Async XLA Ops:
  10.4 2.0 copy-start.2
  10.6 2.6 copy-start.32
  10.7 2.6 copy-start.33
  13.3 3.1 copy-start.16
  13.7 5.9 copy-start.28
  19.6 4.9 copy-start.27
  22.3 3.8 copy-start.11
  141.1 26.0 %copy-start.23 = (bf16[2,512,512]{2,1,0:T(8,128)(2,1)S(1)}, bf16[2,512,512]{2,1,0:T(8,128)(2,1)}, u32[]{:S(2)}) copy-start(bf16[2,512,512]{2,1,0:T(8,128)(2,1)} %get-tuple-element.35) | copy-start | bytes 3145732
  163.6 18.8 %all-to-all-start = ((bf16[4,8,64,128]{3,2,0,1:T(8,128)(2,1)}), bf16[4,8,64,128]{3,2,0,1:T(8,128)(2,1)S(1)}, u32[]{:S(2)}, u32[]{:S(2)}) async-start(bf16[4,8,64,128]{3,2,0,1:T(8,128)(2,1)} %copy.152), calls=%async_computation | async-start | bytes 1048576 | tf_op jit(solution)/shard_map/all_to_all | solution.py:1305
  167.1 63.2 %all-reduce.4.cloned.1.call-start = ((), (), s32[]{:S(2)}) async-start(), calls=%async_computation.2 | async-start | bytes 2097152 | tf_op jit(solution)/shard_map/psum | solution.py:1381
  167.7 18.1 %copy-start.9 = (bf16[512,2,512]{0,2,1:T(8,128)(2,1)}, bf16[512,2,512]{0,2,1:T(8,128)(2,1)S(1)}, u32[]{:S(2)}) copy-start(bf16[512,2,512]{0,2,1:T(8,128)(2,1)S(1)} %copy.154) | copy-start | bytes 3145732
  184.1 4.9 copy-start.14
  185.8 44.5 %copy-start = (bf16[512,1024]{1,0:T(8,128)(2,1)S(1)}, bf16[512,1024]{1,0:T(8,128)(2,1)}, u32[]{:S(2)}) copy-start(bf16[512,1024]{1,0:T(8,128)(2,1)} %tok_ref.3) | copy-start | bytes 3145732
  185.8 56.3 %all-gather.2.cloned.1.call-start = ((), (), s32[]{:S(2)}) async-start(), calls=%async_computation.3 | async-start | bytes 4030464 | tf_op jit(solution)/shard_map/all_gather | solution.py:1372
  189.0 111.2 %all-reduce.6.cloned.1.call-start = ((), (), s32[]{:S(2)}) async-start(), calls=%async_computation.4 | async-start | bytes 2097152 | tf_op jit(solution)/shard_map/psum | solution.py:1397
  230.3 1.7 copy-start.5
  232.5 9.7 %copy-start.19 = (bf16[512,1024]{1,0:T(8,128)(2,1)S(1)}, bf16[512,1024]{1,0:T(8,128)(2,1)}, u32[]{:S(2)}) copy-start(bf16[512,1024]{1,0:T(8,128)(2,1)} %param.20) | copy-start | bytes 3145732
  242.1 3.5 copy-start.4
  245.6 10.1 %slice-start = ((s8[5767168]{0:T(1024)(128)(4,1)}), s8[4194304]{0:T(1024)(128)(4,1)S(1)}, s32[]{:S(2)}) async-start(s8[5767168]{0:T(1024)(128)(4,1)} %bitcast.219), calls=%async_computation.5 | async-start | bytes 8388608
  252.1 3.6 slice-start.1
  254.7 1.1 copy-start.18
  300.2 2.5 copy-start.6
  300.2 2.5 copy-start.8
  300.2 2.5 copy-start.20
  302.7 2.2 copy-start.10
  304.8 59.9 %copy-start.1 = (f32[512,1024]{1,0:T(8,128)}, f32[512,1024]{1,0:T(8,128)S(1)}, u32[]{:S(2)}) copy-start(f32[512,1024]{1,0:T(8,128)S(1)} %get-tuple-element.154.mgrad_ref) | copy-start | bytes 6291460
  313.1 54.3 %all-to-all-start.1 = ((bf16[4,8,64,128]{3,2,0,1:T(8,128)(2,1)}), bf16[4,8,64,128]{3,2,0,1:T(8,128)(2,1)}, u32[]{:S(2)}, u32[]{:S(2)}) async-start(bf16[4,8,64,128]{3,2,0,1:T(8,128)(2,1)} %reshape_broadcast_in_dim_reshape.3), calls=%async_computation.1 | async-start | bytes 1048576 | tf_op jit(solution)/shard_map/all_to_all | solution.py:1311
  358.1 3.9 copy-start.17
  358.1 3.9 copy-start.31
  361.9 2.8 copy-start.15
  556.5 3.7 copy-start.13
  590.5 6.8 %copy-start.3 = (f32[512,3,512]{0,2,1:T(8,128)S(1)}, f32[512,3,512]{0,2,1:T(8,128)}, u32[]{:S(2)}) copy-start(f32[512,3,512]{0,2,1:T(8,128)} %copy-done.2) | copy-start | bytes 9437188
  607.8 3.7 copy-start.7
  614.5 8.6 %copy-start.12 = (f32[512,512]{1,0:T(8,128)S(1)}, f32[512,512]{1,0:T(8,128)}, u32[]{:S(2)}) copy-start(f32[512,512]{1,0:T(8,128)} %param.24) | copy-start | bytes 3145732
  614.5 8.6 %copy-start.24 = (f32[512,512]{1,0:T(8,128)S(1)}, f32[512,512]{1,0:T(8,128)}, u32[]{:S(2)}) copy-start(f32[512,512]{1,0:T(8,128)} %param.29) | copy-start | bytes 3145732
  614.5 8.6 %copy-start.25 = (f32[512,512]{1,0:T(8,128)S(1)}, f32[512,512]{1,0:T(8,128)}, u32[]{:S(2)}) copy-start(f32[512,512]{1,0:T(8,128)} %param.34) | copy-start | bytes 3145732
  614.5 8.6 %copy-start.26 = (bf16[2,256,512]{2,1,0:T(8,128)(2,1)S(1)}, bf16[2,256,512]{2,1,0:T(8,128)(2,1)}, u32[]{:S(2)}) copy-start(bf16[2,256,512]{2,1,0:T(8,128)(2,1)} %get-tuple-element.43) | copy-start | bytes 1572868
  623.2 2.3 copy-start.29
  623.2 2.3 copy-start.30
  623.2 2.9 copy-start.22
  625.5 1.6 copy-start.21
Sparse Core Ops, SparseCore 0:
  185.9 44.2 all-reduce.3
  260.1 40.0 all-reduce.5
Sparse Core Ops, SparseCore 1:
  189.1 43.8 all-gather.1

commit v3 on v2

--- a/solution.py
+++ b/solution.py
@@ -714,6 +714,442 @@
     )(ends, packed, grads, outt, lse)
 
 
+def middle_kernel(
+    z_,
+    tok_ref,
+    cot_ref,
+    gain_ref,
+    heads_ref,
+    wo_ref,
+    wi_ref,
+    wm_ref,
+    branch_ref,
+    middle_ref,
+    mgrad_ref,
+    gain2_ref,
+    grads_ref,
+    g_down,
+    g_wide,
+    g_attn,
+    heads_s,
+    wo_s,
+    wi_s,
+    wm_s,
+    mixed_s,
+    mixed_t,
+    sum_s,
+    sum_in,
+    back_s,
+    back_in,
+    entry_s,
+    entry_t,
+    normed_s,
+    scale_s,
+    gate_s,
+    hgrad_s,
+    hidden_s,
+    hidden_t,
+    gated_s,
+    mgrad_s,
+    dsend_s,
+    down_s,
+    wide_s,
+    attn_s,
+    a_send,
+    a_recv,
+    d_send,
+    d_recv,
+    y_send,
+    y_recv,
+    w_send,
+    w_recv,
+    f_send,
+    f_recv,
+    local_sem,
+):
+    f, c, t = lax.axis_index("fsdp"), lax.axis_index("ctx"), lax.axis_index("tp")
+    core = lax.rem(c, 2)
+    mate = (f, c + 1 - 2 * core, t)
+    other = (f, c, 1 - t)
+    count = z_.ctx // z_.share
+    others = range(1, z_.fsdp)
+    half = z_.rows // 2
+
+    def ahead(k):
+        return lax.rem(f + k, z_.fsdp)
+
+    def behind(k):
+        return lax.rem(f + z_.fsdp - k, z_.fsdp)
+
+    def to_token(j):
+        return lax.rem(c + z_.share * j, z_.ctx)
+
+    def from_head(j):
+        return lax.rem(c + z_.ctx - z_.share * j, z_.ctx)
+
+    def heads_copy(j):
+        return remote(
+            heads_ref.at[:, to_token(j)],
+            heads_s.at[c // z_.share],
+            a_send.at[j],
+            a_recv.at[j],
+            (f, to_token(j), t),
+        )
+
+    def heads_arrival(j):
+        return remote(
+            heads_ref.at[:, c],
+            heads_s.at[from_head(j) // z_.share],
+            a_send.at[j],
+            a_recv.at[j],
+            mate,
+        )
+
+    def grads_copy(j):
+        rank = lax.rem(c + j, z_.ctx)
+        return remote(
+            dsend_s.at[rank // z_.share],
+            grads_ref.at[:, c],
+            d_send.at[j],
+            d_recv.at[j],
+            (f, rank, t),
+        )
+
+    def grads_arrival(j):
+        source = lax.rem(c + z_.ctx - j, z_.ctx)
+        return remote(
+            dsend_s.at[0], grads_ref.at[:, source], d_send.at[j], d_recv.at[j], mate
+        )
+
+    units_half = z_.units // 2
+
+    def down_copy(k):
+        rows = pl.ds(pl.multiple_of(core * units_half, 16), units_half)
+        return remote(
+            wm_ref.at[rows],
+            wm_s.at[f, rows],
+            w_send.at[k - 1],
+            w_recv.at[k - 1],
+            (ahead(k), c, t),
+        )
+
+    def down_pass(k, side):
+        rows = pl.ds(pl.multiple_of(side * units_half, 16), units_half)
+        place = wm_s.at[behind(k), rows]
+        return remote(place, place, f_send.at[k - 1], f_recv.at[k - 1], mate)
+
+    def sum_copy(r):
+        rows = pl.ds(r * half, half)
+        return remote(sum_s.at[rows], sum_in.at[rows], y_send.at[r], y_recv.at[r], other)
+
+    def back_copy(r):
+        rows = pl.ds(r * half, half)
+        return remote(
+            back_s.at[rows], back_in.at[rows], y_send.at[2 + r], y_recv.at[2 + r], other
+        )
+
+    greet(
+        [(ahead(k), c, t) for k in others]
+        + [(f, lax.rem(c + j, z_.ctx), t) for j in range(1, z_.ctx)]
+        + [other]
+    )
+    for j in range(1, count):
+        heads_copy(j).start()
+    for k in others:
+        down_copy(k).start()
+    own_heads = pltpu.make_async_copy(
+        heads_ref.at[:, c], heads_s.at[c // z_.share], local_sem.at[0]
+    )
+    load_wo = pltpu.make_async_copy(wo_ref, wo_s, local_sem.at[1])
+    load_wi = pltpu.make_async_copy(wi_ref, wi_s, local_sem.at[2])
+    own_wm = pltpu.make_async_copy(wm_ref, wm_s.at[f], local_sem.at[3])
+    for copy in (own_heads, load_wo, own_wm, load_wi):
+        copy.start()
+    load_wo.wait()
+    own_heads.wait()
+    for j in range(1, count):
+        heads_arrival(j).wait_recv()
+
+    low_lane = lax.broadcasted_iota(jnp.int32, (half, 2 * HD), 1) < HD
+    for h in range(0, z_.heads, 2):
+        columns = slice(h * HD, (h + 2) * HD)
+        one = heads_s[h].reshape(half, 2 * HD).astype(F32)
+        two = heads_s[h + 1].reshape(half, 2 * HD).astype(F32)
+        early = jnp.where(low_lane, one, pltpu.roll(two, HD, 1))
+        late = jnp.where(low_lane, pltpu.roll(one, HD, 1), two)
+        mixed_s[0:half, columns] = early.astype(BF16)
+        mixed_s[half:, columns] = late.astype(BF16)
+        mixed_t[columns, 0:half] = early.T.astype(BF16)
+        mixed_t[columns, half:] = late.T.astype(BF16)
+
+    for r in range(2):
+        rows = slice(r * half, (r + 1) * half)
+        for g in range(z_.fsdp):
+            sum_s[rows, g * z_.shard : (g + 1) * z_.shard] = jnp.dot(
+                mixed_s[rows, :], wo_s[g], preferred_element_type=F32
+            ).astype(BF16)
+        sum_copy(r).start()
+
+    for k in others:
+        down_copy(k).wait_recv()
+        down_pass(k, core).start()
+    own_wm.wait()
+    for k in others:
+        down_pass(k, 1 - core).wait_recv()
+
+    tile = min(128, half)
+
+    def hidden_grad(i, carried):
+        rows = pl.ds(pl.multiple_of(i * tile, tile), tile)
+        total = jnp.zeros((tile, z_.units), F32)
+        for g in range(z_.fsdp):
+            total = total + lax.dot_general(
+                cot_ref[rows, g * z_.shard : (g + 1) * z_.shard],
+                wm_s[g],
+                (((1,), (1,)), ((), ())),
+                preferred_element_type=F32,
+            )
+        hgrad_s[rows, :] = total
+        return carried
+
+    lax.fori_loop(0, z_.rows // tile, hidden_grad, 0)
+    load_wi.wait()
+    full = z_.units // 128 * 128
+
+    for r in range(2):
+        sum_copy(r).wait_recv()
+
+        def middle_tile(i, carried):
+            rows = pl.ds(pl.multiple_of(r * half + i * tile, tile), tile)
+            middle = tok_ref[rows, :].astype(F32) + (
+                sum_s[rows, :].astype(F32) + sum_in[rows, :].astype(F32)
+            )
+            middle_ref[rows, :] = middle
+            normed, scaling = normalize(middle)
+            normed_s[rows, :] = normed
+            scale_s[rows, :] = jnp.broadcast_to(scaling, (tile, 128))
+            gains = jnp.concatenate([gain_ref[g, 1:2, :] for g in range(z_.fsdp)], axis=1)
+            entry = normed * gains
+            entry_s[rows, :] = entry.astype(BF16)
+            entry_t[:, rows] = entry.T.astype(BF16)
+            return carried
+
+        lax.fori_loop(0, half // tile, middle_tile, 0)
+        rows = pl.ds(r * half, half)
+
+        def gate(k, carried):
+            gate_s[k] = jnp.dot(entry_s[rows, :], wi_s[k], preferred_element_type=F32)
+            return carried
+
+        lax.fori_loop(0, 2, gate, 0)
+
+        def activate(i, carried):
+            inner = pl.ds(pl.multiple_of(i * 16, 16), 16)
+            outer = pl.ds(pl.multiple_of(r * half + i * 16, 16), 16)
+            up, side = gate_s[0, inner, :], gate_s[1, inner, :]
+            grad = hgrad_s[outer, :]
+            chance = 0.5 + 0.5 * lax.erf(up * (0.5**0.5))
+            slope = chance + up * (jnp.exp(-0.5 * up * up) * 0.3989422804014327)
+            active = up * chance
+            hidden_s[outer, :] = (active * side).astype(BF16)
+            gated_s[0, outer, :] = (grad * side * slope).astype(BF16)
+            gated_s[1, outer, :] = (grad * active).astype(BF16)
+            return carried
+
+        lax.fori_loop(0, half // 16, activate, 0)
+
+        for g in range(z_.fsdp):
+            place = slice(g * z_.shard, (g + 1) * z_.shard)
+            total = jnp.zeros((half, z_.shard), F32)
+            for k in range(2):
+                total = total + lax.dot_general(
+                    gated_s[k, rows, :],
+                    wi_s[k, place, :],
+                    (((1,), (1,)), ((), ())),
+                    preferred_element_type=F32,
+                )
+            back_s[rows, place] = total.astype(BF16)
+        back_copy(r).start()
+
+    def turn(i, carried):
+        rows = pl.ds(pl.multiple_of(i * tile, tile), tile)
+        for first in range(0, full, 128):
+            block = hidden_s[rows, first : first + 128].astype(F32)
+            hidden_t[first : first + 128, rows] = block.T.astype(BF16)
+        if full < z_.units:
+            rest = z_.units - full
+            block = hidden_s[rows, full : z_.units].astype(F32)
+            block = jnp.concatenate([block, jnp.zeros((tile, 128 - rest), F32)], axis=1)
+            hidden_t[full : z_.units, rows] = block.T[0:rest].astype(BF16)
+        return carried
+
+    lax.fori_loop(0, z_.rows // tile, turn, 0)
+    for g in range(z_.fsdp):
+        place = slice(g * z_.shard, (g + 1) * z_.shard)
+        for side in range(2):
+            rows = slice(side * units_half, (side + 1) * units_half)
+            down_s[g, side] = jnp.dot(
+                hidden_t[rows, :], cot_ref[:, place], preferred_element_type=F32
+            ).astype(BF16)
+    keep_down = pltpu.make_async_copy(down_s, g_down, local_sem.at[4])
+    keep_down.start()
+
+    def wide_grad(k, carried):
+        for g in range(z_.fsdp):
+            wide_s[g, k] = jnp.dot(
+                entry_t[g * z_.shard : (g + 1) * z_.shard, :],
+                gated_s[k],
+                preferred_element_type=F32,
+            ).astype(BF16)
+        return carried
+
+    lax.fori_loop(0, 2, wide_grad, 0)
+    keep_wide = pltpu.make_async_copy(wide_s, g_wide, local_sem.at[5])
+    keep_wide.start()
+    for g in range(z_.fsdp):
+        place = slice(g * z_.shard, (g + 1) * z_.shard)
+        branch_ref[:, place] = jnp.dot(
+            hidden_s[...], wm_s[g], preferred_element_type=F32
+        ).astype(BF16)
+
+    gain2_ref[...] = jnp.zeros(gain2_ref.shape, F32)
+    for r in range(2):
+        back_copy(r).wait_recv()
+
+        def back_tile(i, carried):
+            rows = pl.ds(pl.multiple_of(r * half + i * tile, tile), tile)
+            back = back_s[rows, :].astype(F32) + back_in[rows, :].astype(F32)
+            normed = normed_s[rows, :]
+            gain2_ref[0:1, :] += jnp.sum(back * normed, axis=0, keepdims=True)
+            gains = jnp.concatenate([gain_ref[g, 1:2, :] for g in range(z_.fsdp)], axis=1)
+            grad = cot_ref[rows, :].astype(F32) + norm_back(
+                back * gains, normed, scale_s[rows, 0:1]
+            )
+            mgrad_ref[rows, :] = grad
+            mgrad_s[rows, :] = grad.astype(BF16)
+            return carried
+
+        lax.fori_loop(0, half // tile, back_tile, 0)
+
+    def heads_grad(rows):
+        total = jnp.zeros((half, z_.head_width), F32)
+        for g in range(z_.fsdp):
+            total = total + lax.dot_general(
+                mgrad_s[rows, g * z_.shard : (g + 1) * z_.shard],
+                wo_s[g],
+                (((1,), (1,)), ((), ())),
+                preferred_element_type=F32,
+            )
+        return total
+
+    early = heads_grad(slice(0, half))
+    late = heads_grad(slice(half, z_.rows))
+    for h in range(0, z_.heads, 2):
+        columns = slice(h * HD, (h + 2) * HD)
+        one = jnp.where(low_lane, early[:, columns], pltpu.roll(late[:, columns], HD, 1))
+        two = jnp.where(low_lane, pltpu.roll(early[:, columns], HD, 1), late[:, columns])
+        dsend_s[h] = one.astype(BF16).reshape(4, z_.block, 2 * HD)
+        dsend_s[h + 1] = two.astype(BF16).reshape(4, z_.block, 2 * HD)
+    for j in range(1, z_.ctx):
+        grads_copy(j).start()
+    own_grads = pltpu.make_async_copy(
+        dsend_s.at[c // z_.share], grads_ref.at[:, c], local_sem.at[6]
+    )
+    own_grads.start()
+    attn_half = z_.head_width // 2
+    for g in range(z_.fsdp):
+        for side in range(2):
+            attn_s[g, side] = jnp.dot(
+                mixed_t[side * attn_half : (side + 1) * attn_half, :],
+                mgrad_s[:, g * z_.shard : (g + 1) * z_.shard],
+                preferred_element_type=F32,
+            ).astype(BF16)
+    keep_attn = pltpu.make_async_copy(attn_s, g_attn, local_sem.at[7])
+    keep_attn.start()
+
+    own_grads.wait()
+    for j in range(1, z_.ctx):
+        grads_arrival(j).wait_recv()
+        grads_copy(j).wait_send()
+    for j in range(1, count):
+        heads_copy(j).wait_send()
+    for k in others:
+        down_copy(k).wait_send()
+        down_pass(k, core).wait_send()
+    for r in range(2):
+        sum_copy(r).wait_send()
+        back_copy(r).wait_send()
+    keep_down.wait()
+    keep_wide.wait()
+    keep_attn.wait()
+
+
+def middle_part(z_, tokens, cotangent, gains, heads, wo, wi, wm):
+    dma = pltpu.SemaphoreType.DMA
+    peers = max(1, z_.fsdp - 1)
+    count = z_.ctx // z_.share
+    rows, width, units = z_.rows, z_.width, z_.units
+    down = (z_.fsdp, 2, units // 2, z_.shard)
+    wide = (z_.fsdp, 2, z_.shard, units)
+    attn = (z_.fsdp, 2, z_.head_width // 2, z_.shard)
+    return pl.pallas_call(
+        functools.partial(middle_kernel, z_),
+        out_shape=(
+            jax.ShapeDtypeStruct((rows, width), BF16),
+            jax.ShapeDtypeStruct((rows, width), F32),
+            jax.ShapeDtypeStruct((rows, width), F32),
+            jax.ShapeDtypeStruct((8, width), F32),
+            jax.ShapeDtypeStruct((4, z_.ctx, z_.block, 2 * HD), BF16),
+            jax.ShapeDtypeStruct(down, BF16),
+            jax.ShapeDtypeStruct(wide, BF16),
+            jax.ShapeDtypeStruct(attn, BF16),
+        ),
+        in_specs=[vmem()] * 3 + [anywhere()] * 4,
+        out_specs=tuple([vmem()] * 4 + [anywhere()] * 4),
+        scratch_shapes=[
+            pltpu.VMEM((z_.heads, 4, z_.block, 2 * HD), BF16),
+            pltpu.VMEM((z_.fsdp, z_.head_width, z_.shard), BF16),
+            pltpu.VMEM((2, width, units), BF16),
+            pltpu.VMEM((z_.fsdp, units, z_.shard), BF16),
+            pltpu.VMEM((rows, z_.head_width), BF16),
+            pltpu.VMEM((z_.head_width, rows), BF16),
+            pltpu.VMEM((rows, width), BF16),
+            pltpu.VMEM((rows, width), BF16),
+            pltpu.VMEM((rows, width), BF16),
+            pltpu.VMEM((rows, width), BF16),
+            pltpu.VMEM((rows, width), BF16),
+            pltpu.VMEM((width, rows), BF16),
+            pltpu.VMEM((rows, width), F32),
+            pltpu.VMEM((rows, 128), F32),
+            pltpu.VMEM((2, rows // 2, units), F32),
+            pltpu.VMEM((rows, units), F32),
+            pltpu.VMEM((rows, units), BF16),
+            pltpu.VMEM((units, rows), BF16),
+            pltpu.VMEM((2, rows, units), BF16),
+            pltpu.VMEM((rows, width), BF16),
+            pltpu.VMEM((z_.heads, 4, z_.block, 2 * HD), BF16),
+            pltpu.VMEM(down, BF16),
+            pltpu.VMEM(wide, BF16),
+            pltpu.VMEM(attn, BF16),
+            dma((count,)),
+            dma((count,)),
+            dma((z_.ctx,)),
+            dma((z_.ctx,)),
+            dma((4,)),
+            dma((4,)),
+            dma((peers,)),
+            dma((peers,)),
+            dma((peers,)),
+            dma((peers,)),
+            dma((8,)),
+        ],
+        compiler_params=pltpu.CompilerParams(
+            collective_id=2, has_side_effects=True, vmem_limit_bytes=VMEM_BYTES
+        ),
+        name="middle",
+    )(tokens, cotangent, gains, heads, wo, wi, wm)
+
+
 def cuts_of(rows, count):
     unit = rows // 16
     marks = [16 * (unit * i // count) for i in range(count + 1)]
@@ -1278,10 +1714,6 @@
     return results
 
 
-def exact_gelu(values):
-    return jax.nn.gelu(values, approximate=False)
-
-
 def by_chip(z_, weight):
     rows = weight.shape[0]
     split = weight.reshape(rows, 3, z_.chips, z_.chip_heads, HD)
@@ -1298,29 +1730,6 @@
     values = chunked[:, :, cut:].reshape(z_.chips, rows, z_.chip_heads, HD)
     values = values.transpose(1, 0, 2, 3).reshape(rows, 1, z_.head_width)
     return jnp.concatenate([pairs, values], axis=1)
-
-
-def heads_to_tokens(z_, packed):
-    parts = packed.shape[0]
-    moved = lax.all_to_all(packed, "ctx", split_axis=1, concat_axis=1, tiled=True)
-    moved = moved.reshape(parts, z_.heads, z_.share, z_.block, 2 * HD)
-    return lax.dynamic_index_in_dim(moved, lax.axis_index("ctx") % z_.share, 2, keepdims=False)
-
-
-def tokens_to_heads(z_, packed):
-    return lax.all_to_all(
-        jnp.repeat(packed, z_.share, axis=1), "ctx", split_axis=1, concat_axis=1, tiled=True
-    )
-
-
-def unpack_values(z_, packed):
-    split = packed.reshape(4, z_.heads, z_.block, 2, HD)
-    return split.transpose(3, 0, 2, 1, 4).reshape(z_.rows, z_.heads, HD)
-
-
-def pack_values(z_, values):
-    split = values.reshape(2, 4, z_.block, z_.heads, HD)
-    return split.transpose(1, 3, 2, 0, 4).reshape(4, z_.heads, z_.block, 2 * HD)
 
 
 def on_device(
@@ -1369,45 +1778,19 @@
         attn_weight.astype(BF16),
         wide_weight.astype(BF16).transpose(1, 0, 2),
     )
-    down_low = lax.all_gather(down_weight.astype(BF16), "fsdp", axis=1, tiled=True)
-    attn_low = wo_full.transpose(1, 0, 2).reshape(z_.head_width, z_.width)
-    wide_low = wi_full.reshape(2, z_.width, z_.units)
-    gains = gains_full.transpose(1, 0, 2).reshape(8, z_.width)
-    inputs = tokens.astype(F32)
     attended_packed, attended_turned, lse = attend(z_, endings, packed)
-    attended_low = unpack_values(
-        z_, heads_to_tokens(z_, attended_packed)
-    ).reshape(z_.rows, z_.head_width)
-    mixed_sum = lax.psum(
-        jnp.dot(attended_low, attn_low, preferred_element_type=F32).astype(BF16), "tp"
-    ).astype(F32)
-    middle = inputs + mixed_sum
-    normed_two, scaling_two = normalize(middle)
-    entry_two = (normed_two * gains[1][None, :]).astype(BF16)
-    gate_up = jnp.einsum("td,kdf->tkf", entry_two, wide_low, preferred_element_type=F32)
-    activated, gelu_pull = jax.vjp(exact_gelu, gate_up[:, 0])
-    hidden_low = (activated * gate_up[:, 1]).astype(BF16)
-    grad_out = cotangent.astype(F32)
-    down_grad = jnp.einsum("tf,td->fd", hidden_low, cotangent, preferred_element_type=F32)
-    hidden_grad = jnp.einsum("td,fd->tf", cotangent, down_low, preferred_element_type=F32)
-    act_grad = gelu_pull(hidden_grad * gate_up[:, 1])[0]
-    gate_grad = hidden_grad * activated
-    gated_grad = jnp.stack([act_grad, gate_grad], axis=1).astype(BF16)
-    wide_grad = jnp.einsum("td,tkf->kdf", entry_two, gated_grad, preferred_element_type=F32)
-    back_two = lax.psum(
-        jnp.einsum("tkf,kdf->td", gated_grad, wide_low, preferred_element_type=F32).astype(BF16),
-        "tp",
-    ).astype(F32)
-    gain_second = jnp.sum(back_two * normed_two, axis=0)
-    middle_grad = grad_out + norm_back(back_two * gains[1][None, :], normed_two, scaling_two)
-    middle_low = middle_grad.astype(BF16)
-    attn_grad = jnp.einsum("tf,td->fd", attended_low, middle_low, preferred_element_type=F32)
-    attended_grad = (
-        jnp.einsum("td,fd->tf", middle_low, attn_low, preferred_element_type=F32)
-        .astype(BF16)
-        .reshape(z_.rows, z_.heads, HD)
-    )
-    grads_packed = tokens_to_heads(z_, pack_values(z_, attended_grad))
+    branch_low, middle, middle_grad, gain_second, grads_packed, down_grad, wide_grad, attn_grad = (
+        middle_part(
+            z_,
+            tokens,
+            cotangent,
+            gains_full,
+            attended_packed,
+            wo_full,
+            wi_full.reshape(2, z_.width, z_.units),
+            down_weight.astype(BF16),
+        )
+    )
     head_grads = attend_back(
         z_,
         endings,
@@ -1416,8 +1799,6 @@
         attended_turned,
         lse,
     )
-    branch_low = jnp.dot(hidden_low, down_low, preferred_element_type=F32).astype(BF16)
-    by_half = (z_.fsdp, 2)
     output, input_grad, down_sum, wide_sum, attn_sum, qkv_sum, gain_sum = reduce_all(
         z_,
         tokens,
@@ -1427,16 +1808,12 @@
         branch_low,
         middle,
         middle_grad,
-        jnp.broadcast_to(gain_second[None, :], (8, z_.width)),
+        gain_second,
         head_grads,
         wq_full,
-        down_grad.astype(BF16)
-        .reshape(2, z_.units // 2, z_.fsdp, z_.shard)
-        .transpose(2, 0, 1, 3),
-        wide_grad.astype(BF16).reshape(2, z_.fsdp, z_.shard, z_.units).transpose(1, 0, 2, 3),
-        attn_grad.astype(BF16)
-        .reshape(2, z_.head_width // 2, z_.fsdp, z_.shard)
-        .transpose(2, 0, 1, 3),
+        down_grad,
+        wide_grad,
+        attn_grad,
     )
     qkv_sum = qkv_sum.reshape(2, z_.chips, z_.shard // 2, z_.chunk).transpose(1, 0, 2, 3)
     shards = (

time: 644 us -> 549 us (0.85)
  Pallas kernels: 320 us -> 405 us
  waiting for transfers between devices: 62.8 us -> 0 us
  local copies, waits for them, and re-layouts: 133 us -> 83.1 us
  matrix products: 35.7 us -> 0 us
  between operations: 16.4 us -> 1.29 us
  other arithmetic: 60.1 us -> 49.7 us
  starting transfers between devices: 8.49 us -> 0 us
    pallas_call x0 -> x1, Pallas kernels: none -> 78.6 us  [middle_part(): pl.pallas_call(functools.partial(middle_kernel, z_), out_shape=(jax.Shape...]
    psum x2 -> x0, waiting for transfers between devices: 48.1 us -> none  [the longest x1 40.5 us: on_device(): lax.psum(jnp.dot(attended_low, attn_low, preferred_element_type=F32).asty...]
    reshape x8 -> x0, local copies, waits for them, and re-layouts: 42.2 us -> none  [the longest x2 28 us: on_device(): wide_grad.astype(BF16).reshape(2, z_.fsdp, z_.shard, z_.units)]
    dot_general x9 -> x0, matrix products: 35.7 us -> none  [the longest x1 9.64 us: on_device(): jnp.einsum('td,kdf->tkf', entry_two, wide_low, preferred_element_type=F32)]
    all_to_all x2 -> x0, waiting for transfers between devices: 14.7 us -> none  [the longest x1 14.7 us: heads_to_tokens(): lax.all_to_all(packed, 'ctx', split_axis=1, concat_axis=1, tiled=True)]
    another operation x3 -> x1, other arithmetic: 9.17 us -> 0.18 us  [the longest x2 8.99 us: on_device(): gated_grad = jnp.stack([act_grad, gate_grad], axis=1).astype(BF16)]
    all_to_all x2 -> x0, starting transfers between devices: 8.37 us -> none  [the longest x1 4.87 us: tokens_to_heads(): lax.all_to_all(jnp.repeat(packed, z_.share, axis=1), 'ctx', split_axis=1,...]
    unnamed x86 -> x40, local copies, waits for them, and re-layouts: 59.3 us -> 60.2 us
  transfers between devices with their start and end apart: 5 -> 0, of which waited for: 3 -> 0; matrix products, arithmetic and copies ran while one was open for 15% -> 0% of each run, Pallas kernels for 0% -> 0%
where the time goes in v3:
time: 549 us; the launch traced here: 539 us
  Pallas kernels  405 us (74%)
  local copies, waits for them, and re-layouts  83.1 us (15%)
  other arithmetic  49.7 us (9%)
    pallas_call x1, Pallas kernels, reduce_all(): pl.pallas_call(functools.partial(reduce_kernel, z_, items), out_shape=(ja...  165 us
    pallas_call x1, Pallas kernels, project(): pl.pallas_call(functools.partial(project_kernel, z_), out_shape=(jax.Shap...  112 us
    pallas_call x1, Pallas kernels, middle_part(): pl.pallas_call(functools.partial(middle_kernel, z_), out_shape=(jax.Shape...  78.6 us
    unnamed x40, local copies, waits for them, and re-layouts  60.2 us
    sub x5, other arithmetic, adam_step(): weight - rate_now * (corrected / (spread + ADAM_EPS) + DECAY * weight)  32.6 us
    pallas_call x1, Pallas kernels, attend_back(): pl.pallas_call(functools.partial(attend_back_kernel, z_, q_tile, k_tile),...  27.6 us
    pallas_call x1, Pallas kernels, attend(): pl.pallas_call(functools.partial(attend_kernel, z_, q_tile, k_tile), out_...  20.5 us

profile of v3, /device:TPU:0, one launch (start us, length us, event | category | flops | bytes accessed | tf_op | source)
XLA Modules:
  0.0 538.6 jit_solution(536730469194723180)
XLA Ops:
  0.7 0.9 select_reduce_fusion.1
  1.5 0.2 reduce-window.8
  1.7 0.1 select_reduce_fusion
  1.8 1.0 fusion.8
  2.8 1.3 pad_maximum_fusion.2
  4.1 2.4 copy.93
  6.5 0.0 copy-done.10
  6.5 0.2 convert_element_type.56
  6.7 0.0 copy-start.2
  6.7 1.1 copy-done.2
  7.8 0.1 slice_bitcast_fusion
  7.9 1.1 copy.94
  9.0 2.3 copy.95
  11.3 1.9 slice.21
  13.1 2.0 copy.96
  15.2 2.7 pad_maximum_fusion.wq_ref
  17.9 4.4 convert_element_type.58
  22.2 4.5 copy.97
  26.7 2.1 convert_element_type.57.wo_ref
  28.8 0.0 copy-done.9
  28.8 0.6 pad_convert_fusion.gain_ref
  29.4 112.4 %project.1 = (bf16[12,8,64,128]{3,2,1,0:T(8,128)(2,1)}, bf16[4,2,512,384]{3,2,1,0:T(8,128)(2,1)}, bf16[2,512,512]{2,1,0:T(8,128)(2,1)}, bf16[2,2,512,1312]{3,2,1,0:T(8,128)(2,1)}, f32[2,8,512]{2,1,0:T(8,128)}) custom-call(bf16[512,1024]{1,0:T(8,128)(2,1)} %tok_ref.5, f32[8,512]{1,0:T(8,128)} %pad_convert_fusion.gain_ref, ...), custom_call_target="tpu_custom_call" | custom-call | tf_op jit(solution)/shard_map/project/pallas_call | solution.py:372
  141.9 20.5 %attend.1 = (bf16[4,8,64,128]{3,2,1,0:T(8,128)(2,1)}, f32[64,4096]{1,0:T(8,128)}, f32[8,4096]{1,0:T(8,128)}) custom-call(s32[4]{0:T(128)} %bitcast.67, bf16[12,8,64,128]{3,2,1,0:T(8,128)(2,1)} %get-tuple-element.41.packed_ref), custom_call_target="tpu_custom_call" | custom-call | tf_op jit(solution)/shard_map/attend/pallas_call | solution.py:532
  162.4 3.0 convert_element_type.59.wm_ref
  165.4 78.6 %middle.1 = (bf16[512,1024]{1,0:T(8,128)(2,1)}, f32[512,1024]{1,0:T(8,128)}, f32[512,1024]{1,0:T(8,128)}, f32[8,1024]{1,0:T(8,128)}, bf16[4,8,64,128]{3,2,1,0:T(...) custom-call(bf16[512,1024]{1,0:T(8,128)(2,1)} %tok_ref.5, ...), custom_call_target="tpu_custom_call" | custom-call | tf_op jit(solution)/shard_map/middle/pallas_call | solution.py:1095
  244.0 27.6 %attend_back.1.heads_ref = bf16[12,8,64,128]{3,2,1,0:T(8,128)(2,1)} custom-call(s32[4]{0:T(128)} %bitcast.68, bf16[12,8,64,128]{3,2,1,0:T(8,128)(2,1)} %get-tuple-element.41.packed_ref, bf16[4,8,64,128]{3,2,1,0:T(8,128)(2,1)} %get-tuple-element.49.grad_ref, f32[64,4096]{1,0:T(8,128)} %get-tuple-element.50.outt_ref, f32[8,4096]{1,0:T(8,128)} %get-tuple-element.51.lse_ref), custom_call_target="tpu_custom_call" | custom-call | tf_op jit(solution)/shard_map/attend_back/pallas_call | solution.py:696
  271.6 165.4 %reduce.1 = (bf16[512,1024]{1,0:T(8,128)(2,1)}, bf16[512,1024]{1,0:T(8,128)(2,1)}, bf16[2,656,512]{2,1,0:T(8,128)(2,1)}, bf16[2,512,1312]{2,1,0:T(8,128)(2,1)}, ...) custom-call(bf16[512,1024]{1,0:T(8,128)(2,1)} %tok_ref.5, ...), custom_call_target="tpu_custom_call" | custom-call | tf_op jit(solution)/shard_map/reduce/pallas_call | solution.py:1662
  437.0 6.2 %copy.106 = f32[512,2,1312]{2,0,1:T(8,128)} copy(f32[512,2,1312]{0,2,1:T(8,128)} %param.30) | data formatting | bytes 10747904 | tf_op args[11]
  443.2 6.1 %copy.107 = f32[512,2,1312]{2,0,1:T(8,128)} copy(f32[512,2,1312]{0,2,1:T(8,128)} %param.35) | data formatting | bytes 10747904 | tf_op args[16]
  449.3 6.2 %copy.109 = f32[512,2,1312]{2,0,1:T(8,128)} copy(f32[512,2,1312]{0,2,1:T(8,128)} %param.25) | data formatting | bytes 10747904 | tf_op args[6]
  455.5 14.1 %multiply_subtract_fusion = (f32[512,2,1312]{2,0,1:T(8,128)}, f32[512,2,1312]{2,0,1:T(8,128)}, f32[512,2,1312]{2,0,1:T(8,128)}) fusion(f32[512,2,1312]{2,0,1:T(8,128)} %copy.109, bf16[2,512,1312]{2,1,0:T(8,128)(2,1)} %get-tuple-element.60, f32[512,2,1312]{2,0,1:T(8,128)} %copy.106, f32[512,2,1312]{2,0,1:T(8,128)} %copy.107), kind=kLoop, calls=%fused_computation.4 | loop fusion | flops 21495808 | bytes 34930688 | tf_op jit(solution)/shard_map/sub | solution.py:1705
  469.6 6.0 %copy.113 = f32[512,2,1312]{0,2,1:T(8,128)} copy(f32[512,2,1312]{2,0,1:T(8,128)} %get-tuple-element.137) | data formatting | bytes 10747904
  475.6 6.0 %copy.114 = f32[512,2,1312]{0,2,1:T(8,128)} copy(f32[512,2,1312]{2,0,1:T(8,128)} %get-tuple-element.138) | data formatting | bytes 10747904
  481.7 6.0 %copy.115 = f32[512,2,1312]{0,2,1:T(8,128)} copy(f32[512,2,1312]{2,0,1:T(8,128)} %get-tuple-element.139) | data formatting | bytes 10747904
  487.7 1.6 copy.99
  489.3 0.0 copy-start.1
  489.3 1.1 copy-done.1
  490.4 1.0 slice.22
  491.5 2.3 copy.100
  493.8 2.3 copy.101
  496.0 1.9 slice.23
  497.9 2.0 copy.102
  499.9 3.5 copy.103
  503.5 3.5 copy.98
  507.0 7.0 %multiply_subtract_fusion.1 = (f32[512,3,512]{0,2,1:T(8,128)}, f32[512,3,512]{0,2,1:T(8,128)}, f32[512,3,512]{0,2,1:T(8,128)}) fusion(f32[512,3,512]{0,2,1:T(8,128)S(1)} %copy.93, bf16[512,1,512]{0,2,1:T(8,128)(2,1)} %bitcast.63, bf16[512,2,512]{0,2,1:T(8,128)(2,1)} %bitcast.60, f32[512,3,512]{0,2,1:T(8,128)} %copy.98, f32[512,3,512]{0,2,1:T(8,128)} %copy.103), kind=kLoop, calls=%fused_computation.12 | loop fusion | flops 13369344 | bytes 20447232 | tf_op jit(solution)/shard_map/sub | solution.py:1705
  514.0 3.5 copy.110
  517.6 3.7 copy.111
  521.3 0.0 copy-done
  521.3 2.6 copy.112
  523.9 0.0 copy-start.3
  523.9 0.0 copy-start.6
  523.9 0.0 copy-start.7
  523.9 0.0 copy-start.8
  523.9 8.6 %multiply_subtract_fusion.2 = (f32[1312,512]{1,0:T(8,128)}, f32[1312,512]{1,0:T(8,128)}, f32[1312,512]{1,0:T(8,128)}) fusion(f32[1312,512]{1,0:T(8,128)} %param.26, bf16[2,656,512]{2,1,0:T(8,128)(2,1)} %get-tuple-element.61, f32[1312,512]{1,0:T(8,128)} %param.31, f32[1312,512]{1,0:T(8,128)} %param.36), kind=kLoop, calls=%fused_computation.15 | loop fusion | flops 10747904 | bytes 17465344 | tf_op jit(solution)/shard_map/sub | solution.py:1705
  532.5 0.0 copy-done.8
  532.6 0.0 copy-start.11
  532.6 0.0 copy-start.12
  532.6 2.3 multiply_subtract_fusion.3
  534.9 0.7 slice_convert_fusion
  535.6 0.6 multiply_subtract_fusion.4
  536.2 0.0 copy-done.5
  536.2 1.0 copy.123
  537.2 0.0 copy-done.4
  537.2 1.0 copy.124
  (14 shorter events, 0.1 us)
Async XLA Ops:
  1.7 4.8 copy-start.10
  6.7 1.1 copy-start.2
  22.2 6.6 %copy-start.9 = (f32[2,512]{1,0:T(2,128)S(1)}, f32[2,512]{1,0:T(2,128)}, u32[]{:S(2)}) copy-start(f32[2,512]{1,0:T(2,128)} %param.27) | copy-start | bytes 12292
  489.3 1.1 copy-start.1
  517.6 3.7 copy-start
  523.9 8.7 %copy-start.3 = (f32[512,512]{1,0:T(8,128)S(1)}, f32[512,512]{1,0:T(8,128)}, u32[]{:S(2)}) copy-start(f32[512,512]{1,0:T(8,128)} %param.24) | copy-start | bytes 3145732
  523.9 8.7 %copy-start.6 = (f32[512,512]{1,0:T(8,128)S(1)}, f32[512,512]{1,0:T(8,128)}, u32[]{:S(2)}) copy-start(f32[512,512]{1,0:T(8,128)} %param.29) | copy-start | bytes 3145732
  523.9 8.7 %copy-start.7 = (f32[512,512]{1,0:T(8,128)S(1)}, f32[512,512]{1,0:T(8,128)}, u32[]{:S(2)}) copy-start(f32[512,512]{1,0:T(8,128)} %param.34) | copy-start | bytes 3145732
  523.9 8.6 %copy-start.8 = (bf16[2,256,512]{2,1,0:T(8,128)(2,1)S(1)}, bf16[2,256,512]{2,1,0:T(8,128)(2,1)}, u32[]{:S(2)}) copy-start(bf16[2,256,512]{2,1,0:T(8,128)(2,1)} %get-tuple-element.59) | copy-start | bytes 1572868
  532.6 3.0 copy-start.11
  532.6 3.0 copy-start.12
  532.6 3.6 copy-start.5
  532.6 4.6 copy-start.4

commit v4 on v3

--- a/solution.py
+++ b/solution.py
@@ -43,8 +43,8 @@
         self.head_width = head_width
         self.units = units
         self.share = max(1, ctx // self.heads)
-        self.chip_heads = max(1, self.heads // self.chips)
-        self.chunk = self.chip_heads * 3 * HD
+        self.pairs = self.heads // 2
+        self.ranks = ctx // self.pairs
 
 
 def remote(src, dst, send, recv, device):
@@ -121,6 +121,27 @@
         jnp.concatenate([cosine] * 4, axis=1),
         jnp.concatenate([-sines, sines, -sines, sines], axis=1),
     )
+
+
+def cuts_of(rows, count):
+    unit = rows // 16
+    marks = [16 * (unit * i // count) for i in range(count + 1)]
+    return [(a, b - a) for a, b in zip(marks, marks[1:]) if b > a]
+
+
+def over_rows(start, rows, step, body):
+    whole = rows // step
+
+    def turn(i, carried):
+        body(pl.multiple_of(start + i * step, 16), step)
+        return carried
+
+    if whole > 1:
+        lax.fori_loop(0, whole, turn, 0)
+    elif whole == 1:
+        body(start, step)
+    if rows % step:
+        body(start + whole * step, rows % step)
 
 
 def project_kernel(
@@ -138,7 +159,12 @@
     wi_out,
     gain_out,
     entry_s,
+    wq_f,
+    wo_f,
+    wi_f,
     wq_s,
+    wo_s,
+    wi_s,
     send_s,
     gain_s,
     gain_send,
@@ -157,9 +183,12 @@
 ):
     f, c, t = lax.axis_index("fsdp"), lax.axis_index("ctx"), lax.axis_index("tp")
     core = lax.rem(c, 2)
-    chip = c // 2
     mate = (f, c + 1 - 2 * core, t)
     others = range(1, z_.fsdp)
+    mine = c // z_.ranks
+    place_in = lax.rem(c, z_.ranks)
+    last = z_.pairs - 1
+    unit_half = z_.units // 2
 
     def ahead(k):
         return lax.rem(f + k, z_.fsdp)
@@ -167,15 +196,23 @@
     def behind(k):
         return lax.rem(f + z_.fsdp - k, z_.fsdp)
 
-    def chip_of(s):
-        return lax.rem(chip + 1 + s, z_.chips)
-
+    def pair_of(s):
+        return lax.rem(mine + 1 + s, z_.pairs)
+
+    load_wq = pltpu.make_async_copy(wq_ref, wq_f, local_sem.at[0])
+    load_wo = pltpu.make_async_copy(wo_ref, wo_f, local_sem.at[1])
+    load_wi = pltpu.make_async_copy(wi_ref.at[:, 0:unit_half], wi_f, local_sem.at[2])
+    load_wq.start()
+    load_wo.start()
+    load_wi.start()
     greet(
         [(ahead(k), c, t) for k in others]
         + [(f, lax.rem(c + j, z_.ctx), t) for j in range(1, z_.ctx)]
     )
 
     half = z_.shard // 2
+    own_half = pl.ds(pl.multiple_of(core * half, half), half)
+    mate_half = pl.ds(pl.multiple_of((1 - core) * half, half), half)
 
     def gain_copy(k, owner):
         return remote(
@@ -183,81 +220,80 @@
         )
 
     def wq_copy(s, k, owner):
-        p = chip_of(s)
-        rows = pl.ds(pl.multiple_of(core * half, half), half)
+        place = wq_s.at[pair_of(s), owner, own_half]
         return remote(
-            wq_ref.at[p, rows],
-            wq_s.at[p, owner, rows],
-            wq_send.at[s, k - 1],
-            wq_recv.at[s, k - 1],
-            (ahead(k), c, t),
+            place, place, wq_send.at[s, k - 1], wq_recv.at[s, k - 1], (ahead(k), c, t)
         )
 
-    def wq_pass(s, k, side):
-        p = chip_of(s)
-        rows = pl.ds(pl.multiple_of(side * half, half), half)
-        place = wq_s.at[p, behind(k), rows]
+    def wq_pass(s, k, rows):
+        place = wq_s.at[pair_of(s), behind(k), rows]
         return remote(place, place, wq_fsend.at[s, k - 1], wq_frecv.at[s, k - 1], mate)
 
     attn_half = z_.head_width // 2
 
-    def wo_copy(k, owner):
-        rows = pl.ds(pl.multiple_of(core * attn_half, attn_half), attn_half)
+    def weight_places(side, owner):
+        rows = pl.ds(pl.multiple_of(side * attn_half, attn_half), attn_half)
+        return (
+            (wo_s.at[rows], wo_out.at[owner, rows]),
+            (wi_s.at[side], wi_out.at[side, owner]),
+        )
+
+    pieces = 2
+
+    def w_copy(n, k, owner):
+        source, place = weight_places(core, owner)[n]
+        return remote(source, place, w_send.at[n, k - 1], w_recv.at[n, k - 1], (ahead(k), c, t))
+
+    def w_pass(n, k, side):
+        place = weight_places(side, behind(k))[n][1]
+        return remote(place, place, w_fsend.at[n, k - 1], w_frecv.at[n, k - 1], mate)
+
+    def head_copy(s, i):
         return remote(
-            wo_ref.at[rows],
-            wo_out.at[owner, rows],
-            w_send.at[0, k - 1],
-            w_recv.at[0, k - 1],
-            (ahead(k), c, t),
+            send_s.at[s, i // z_.share],
+            packed_ref.at[:, c],
+            a_send.at[s, i],
+            a_recv.at[s, place_in],
+            (f, pair_of(s) * z_.ranks + i, t),
         )
 
-    def wo_pass(k, side):
-        rows = pl.ds(pl.multiple_of(side * attn_half, attn_half), attn_half)
-        place = wo_out.at[behind(k), rows]
-        return remote(place, place, w_fsend.at[0, k - 1], w_frecv.at[0, k - 1], mate)
-
-    def wi_copy(k, owner):
+    def head_arrival(s, i):
+        source = lax.rem(mine + 2 * z_.pairs - 1 - s, z_.pairs) * z_.ranks + i
         return remote(
-            wi_ref.at[core],
-            wi_out.at[core, owner],
-            w_send.at[1, k - 1],
-            w_recv.at[1, k - 1],
-            (ahead(k), c, t),
+            send_s.at[s, 0], packed_ref.at[:, source], a_send.at[s, 0], a_recv.at[s, i], mate
         )
 
-    def wi_pass(k, side):
-        place = wi_out.at[side, behind(k)]
-        return remote(place, place, w_fsend.at[1, k - 1], w_frecv.at[1, k - 1], mate)
-
-    def head_copy(s, side, source):
-        p = chip_of(s)
+    def near_copy(j):
+        i = lax.rem(place_in + j, z_.ranks)
         return remote(
-            send_s.at[s, side % z_.chip_heads],
-            packed_ref.at[:, source],
-            a_send.at[s, side],
-            a_recv.at[s, core],
-            (f, 2 * p + side, t),
+            send_s.at[last, i // z_.share],
+            packed_ref.at[:, c],
+            a_send.at[last, j],
+            a_recv.at[last, j],
+            (f, mine * z_.ranks + i, t),
         )
 
-    def head_arrival(s, side):
-        source = 2 * lax.rem(chip + 2 * z_.chips - 1 - s, z_.chips) + side
+    def near_arrival(j):
+        source = mine * z_.ranks + lax.rem(place_in + z_.ranks - j, z_.ranks)
         return remote(
-            send_s.at[s, 0], packed_ref.at[:, source], a_send.at[s, 0], a_recv.at[s, side], mate
+            send_s.at[last, 0], packed_ref.at[:, source], a_send.at[last, j], a_recv.at[last, j], mate
         )
 
     for k in others:
         gain_copy(k, f).start()
-    for k in others:
-        wq_copy(0, k, f).start()
-    own_wq = pltpu.make_async_copy(wq_ref, wq_s.at[:, f], local_sem.at[0])
-    own_wo = pltpu.make_async_copy(wo_ref, wo_out.at[f], local_sem.at[1])
-    own_wi = pltpu.make_async_copy(wi_ref, wi_out.at[:, f], local_sem.at[2])
-    own_wq.start()
-    own_wo.start()
-    own_wi.start()
+    load_wq.wait()
+
+    def round_pair(s):
+        p = pair_of(s)
+        columns = pl.ds(pl.multiple_of(p * 2 * HD, 2 * HD), 2 * HD)
+        for kind in range(3):
+            wq_s[p, f, :, kind * 2 * HD : (kind + 1) * 2 * HD] = wq_f[kind, :, columns].astype(BF16)
+
+    for s in range(2):
+        round_pair(s)
+        for k in others:
+            wq_copy(s, k, f).start()
     gain_s[f] = gain_ref[...]
-    for k in others:
-        wq_copy(1, k, f).start()
     for k in others:
         gain_copy(k, behind(k)).wait()
 
@@ -273,93 +309,108 @@
         return carried
 
     lax.fori_loop(0, z_.rows // tile, norm_tile, 0)
-    own_wq.wait()
+    load_wo.wait()
+    wo_s[...] = wo_f[...].astype(BF16)
+    own_wo = pltpu.make_async_copy(wo_s, wo_out.at[f], local_sem.at[1])
+    own_wo.start()
+    load_wi.wait()
+    own_wi = pltpu.make_async_copy(wi_s, wi_out.at[:, f], local_sem.at[2])
+
+    def round_wide(side):
+        def turn(first, rows):
+            place = pl.ds(first, rows)
+            wi_s[side, place, :] = wi_f[side, place, :].astype(BF16)
+
+        over_rows(0, unit_half, 128, turn)
+
+    lane = lax.broadcasted_iota(jnp.int32, (z_.rows, 2 * HD), 1) < HD
+    lane_half = lax.broadcasted_iota(jnp.int32, (z_.rows // 2, 2 * HD), 1) < HD
 
     def chunk_step(s, carried):
+        @pl.when(s + 2 < z_.pairs)
+        def more():
+            round_pair(s + 2)
+            for k in others:
+                wq_copy(s + 2, k, f).start()
+
+        @pl.when(s + 2 == z_.pairs)
+        def attn_part():
+            for k in others:
+                w_copy(0, k, f).start()
+            round_wide(core)
+
+        @pl.when(s + 1 == z_.pairs)
+        def wide_part():
+            for k in others:
+                w_copy(1, k, f).start()
+
         for k in others:
-
-            @pl.when(s + 2 < z_.chips)
-            def more():
-                wq_copy(s + 2, k, f).start()
-
-            @pl.when(s + 2 == z_.chips)
-            def attn_part():
-                wo_copy(k, f).start()
-
-            @pl.when(s + 1 == z_.chips)
-            def wide_part():
-                wi_copy(k, f).start()
-
-            arrived = wq_copy(s, k, behind(k))
-            arrived.wait_recv()
-            wq_pass(s, k, core).start()
+            wq_copy(s, k, behind(k)).wait_recv()
+            wq_pass(s, k, own_half).start()
         for k in others:
-            wq_pass(s, k, 1 - core).wait_recv()
-        p = chip_of(s)
-        total = jnp.zeros((z_.rows, z_.chunk), F32)
+            wq_pass(s, k, mate_half).wait_recv()
+        p = pair_of(s)
+        total = jnp.zeros((z_.rows, 6 * HD), F32)
         for g in range(z_.fsdp):
             total = total + jnp.dot(entry_s[g], wq_s[p, g], preferred_element_type=F32)
-        for i in range(z_.chip_heads):
-            pair = total[:, 2 * HD * i : 2 * HD * (i + 1)]
-            pair = pair * cos_ref[...] + swap_halves(pair) * sin_ref[...]
-            send_s[s, i, 0:8] = pair.astype(BF16).reshape(8, z_.block, 2 * HD)
-            start = z_.chip_heads * 2 * HD + HD * i
-            value = total[:, start : start + HD]
-            value = jnp.concatenate([value[: z_.rows // 2], value[z_.rows // 2 :]], axis=1)
-            send_s[s, i, 8:12] = value.astype(BF16).reshape(4, z_.block, 2 * HD)
-
-        @pl.when(s < z_.chips - 1)
+        turned = []
+        for kind in range(2):
+            part = total[:, kind * 2 * HD : (kind + 1) * 2 * HD]
+            turned.append(part * cos_ref[...] + swap_halves(part) * sin_ref[...])
+        query, key = turned
+        value = total[:, 4 * HD : 6 * HD]
+        early, late = value[: z_.rows // 2], value[z_.rows // 2 :]
+        both = (
+            (
+                jnp.where(lane, query, pltpu.roll(key, HD, 1)),
+                jnp.where(lane_half, early, pltpu.roll(late, HD, 1)),
+            ),
+            (
+                jnp.where(lane, pltpu.roll(query, HD, 1), key),
+                jnp.where(lane_half, pltpu.roll(early, HD, 1), late),
+            ),
+        )
+        for i in range(2):
+            send_s[s, i, 0:8] = both[i][0].astype(BF16).reshape(8, z_.block, 2 * HD)
+            send_s[s, i, 8:12] = both[i][1].astype(BF16).reshape(4, z_.block, 2 * HD)
+
+        @pl.when(s < last)
         def away():
-            for side in range(2):
-                head_copy(s, side, c).start()
+            for i in range(z_.ranks):
+                head_copy(s, i).start()
 
         return carried
 
-    lax.fori_loop(0, z_.chips, chunk_step, 0)
-    last = z_.chips - 1
+    lax.fori_loop(0, z_.pairs, chunk_step, 0)
     kept = pltpu.make_async_copy(
-        send_s.at[last, lax.rem(core, z_.chip_heads)], packed_ref.at[:, c], local_sem.at[3]
+        send_s.at[last, place_in // z_.share], packed_ref.at[:, c], local_sem.at[3]
     )
     kept.start()
-    crossed = remote(
-        send_s.at[last, lax.rem(1 - core, z_.chip_heads)],
-        packed_ref.at[:, c],
-        a_send.at[last, 0],
-        a_recv.at[last, 0],
-        mate,
-    )
-    crossed.start()
+    for j in range(1, z_.ranks):
+        near_copy(j).start()
     keep_wq = pltpu.make_async_copy(wq_s, wq_out, local_sem.at[4])
     keep_wq.start()
+    round_wide(1 - core)
+    own_wi.start()
+    for n in range(pieces):
+        for k in others:
+            w_copy(n, k, behind(k)).wait_recv()
+            w_pass(n, k, core).start()
+    for s in range(last):
+        for i in range(z_.ranks):
+            head_arrival(s, i).wait_recv()
+            head_copy(s, i).wait_send()
+    for j in range(1, z_.ranks):
+        near_arrival(j).wait_recv()
+        near_copy(j).wait_send()
     for k in others:
-        wo_copy(k, behind(k)).wait_recv()
-        wo_pass(k, core).start()
-    for k in others:
-        wi_copy(k, behind(k)).wait_recv()
-        wi_pass(k, core).start()
-    for s in range(z_.chips - 1):
-        for side in range(2):
-            head_arrival(s, side).wait_recv()
-            head_copy(s, side, c).wait_send()
-    crossed_in = remote(
-        send_s.at[last, 0],
-        packed_ref.at[:, c + 1 - 2 * core],
-        a_send.at[last, 0],
-        a_recv.at[last, 0],
-        mate,
-    )
-    crossed_in.wait_recv()
-    crossed.wait_send()
-    for k in others:
-        for s in range(z_.chips):
+        for s in range(z_.pairs):
             wq_copy(s, k, f).wait_send()
-            wq_pass(s, k, core).wait_send()
-        wo_copy(k, f).wait_send()
-        wi_copy(k, f).wait_send()
-        wo_pass(k, core).wait_send()
-        wi_pass(k, core).wait_send()
-        wo_pass(k, 1 - core).wait_recv()
-        wi_pass(k, 1 - core).wait_recv()
+            wq_pass(s, k, own_half).wait_send()
+        for n in range(pieces):
+            w_copy(n, k, f).wait_send()
+            w_pass(n, k, core).wait_send()
+            w_pass(n, k, 1 - core).wait_recv()
     kept.wait()
     keep_wq.wait()
     own_wo.wait()
@@ -373,30 +424,35 @@
         functools.partial(project_kernel, z_),
         out_shape=(
             jax.ShapeDtypeStruct((12, z_.ctx, z_.block, 2 * HD), BF16),
-            jax.ShapeDtypeStruct((z_.chips, z_.fsdp, z_.shard, z_.chunk), BF16),
+            jax.ShapeDtypeStruct((z_.pairs, z_.fsdp, z_.shard, 6 * HD), BF16),
             jax.ShapeDtypeStruct((z_.fsdp, z_.head_width, z_.shard), BF16),
-            jax.ShapeDtypeStruct((2, z_.fsdp, z_.shard, z_.units), BF16),
+            jax.ShapeDtypeStruct((2, z_.fsdp, z_.units // 2, z_.shard), BF16),
             jax.ShapeDtypeStruct((z_.fsdp, 8, z_.shard), F32),
         ),
-        in_specs=[vmem()] * 5 + [anywhere()] * 2,
+        in_specs=[vmem()] * 4 + [anywhere()] * 3,
         out_specs=(anywhere(), anywhere(), anywhere(), anywhere(), vmem()),
         scratch_shapes=[
             pltpu.VMEM((z_.fsdp, z_.rows, z_.shard), BF16),
-            pltpu.VMEM((z_.chips, z_.fsdp, z_.shard, z_.chunk), BF16),
-            pltpu.VMEM((z_.chips, z_.chip_heads, 12, z_.block, 2 * HD), BF16),
+            pltpu.VMEM((3, z_.shard, z_.head_width), F32),
+            pltpu.VMEM((z_.head_width, z_.shard), F32),
+            pltpu.VMEM((2, z_.units // 2, z_.shard), F32),
+            pltpu.VMEM((z_.pairs, z_.fsdp, z_.shard, 6 * HD), BF16),
+            pltpu.VMEM((z_.head_width, z_.shard), BF16),
+            pltpu.VMEM((2, z_.units // 2, z_.shard), BF16),
+            pltpu.VMEM((z_.pairs, 2, 12, z_.block, 2 * HD), BF16),
             pltpu.VMEM((z_.fsdp, 8, z_.shard), F32),
             dma((peers,)),
             dma((peers,)),
-            dma((z_.chips, peers)),
-            dma((z_.chips, peers)),
-            dma((z_.chips, peers)),
-            dma((z_.chips, peers)),
+            dma((z_.pairs, peers)),
+            dma((z_.pairs, peers)),
+            dma((z_.pairs, peers)),
+            dma((z_.pairs, peers)),
             dma((2, peers)),
             dma((2, peers)),
             dma((2, peers)),
             dma((2, peers)),
-            dma((z_.chips, 2)),
-            dma((z_.chips, 2)),
+            dma((z_.pairs, z_.ranks)),
+            dma((z_.pairs, z_.ranks)),
             dma((5,)),
         ],
         compiler_params=pltpu.CompilerParams(
@@ -722,7 +778,8 @@
     heads_ref,
     wo_ref,
     wi_ref,
-    wm_ref,
+    wide_ref,
+    down_ref,
     branch_ref,
     middle_ref,
     mgrad_ref,
@@ -734,6 +791,8 @@
     heads_s,
     wo_s,
     wi_s,
+    wide_f,
+    down_f,
     wm_s,
     mixed_s,
     mixed_t,
@@ -742,7 +801,9 @@
     back_s,
     back_in,
     entry_s,
-    entry_t,
+    branch_s,
+    middle_s,
+    grad_f,
     normed_s,
     scale_s,
     gate_s,
@@ -750,6 +811,7 @@
     hidden_s,
     hidden_t,
     gated_s,
+    gated_t,
     mgrad_s,
     dsend_s,
     down_s,
@@ -823,20 +885,19 @@
 
     units_half = z_.units // 2
 
-    def down_copy(k):
-        rows = pl.ds(pl.multiple_of(core * units_half, 16), units_half)
-        return remote(
-            wm_ref.at[rows],
-            wm_s.at[f, rows],
-            w_send.at[k - 1],
-            w_recv.at[k - 1],
-            (ahead(k), c, t),
-        )
-
-    def down_pass(k, side):
-        rows = pl.ds(pl.multiple_of(side * units_half, 16), units_half)
-        place = wm_s.at[behind(k), rows]
-        return remote(place, place, f_send.at[k - 1], f_recv.at[k - 1], mate)
+    def weight_place(n, side, owner):
+        if n == 0:
+            rows = pl.ds(pl.multiple_of(side * units_half, 16), units_half)
+            return wm_s.at[owner, rows]
+        return wi_s.at[side, owner, units_half : z_.units]
+
+    def w_copy(n, k, owner):
+        place = weight_place(n, core, owner)
+        return remote(place, place, w_send.at[n, k - 1], w_recv.at[n, k - 1], (ahead(k), c, t))
+
+    def w_pass(n, k, side):
+        place = weight_place(n, side, behind(k))
+        return remote(place, place, f_send.at[n, k - 1], f_recv.at[n, k - 1], mate)
 
     def sum_copy(r):
         rows = pl.ds(r * half, half)
@@ -848,6 +909,18 @@
             back_s.at[rows], back_in.at[rows], y_send.at[2 + r], y_recv.at[2 + r], other
         )
 
+    load_down = pltpu.make_async_copy(down_ref, down_f, local_sem.at[3])
+    load_down.start()
+    load_wide = pltpu.make_async_copy(
+        wide_ref.at[:, units_half : z_.units], wide_f, local_sem.at[8]
+    )
+    load_wide.start()
+    load_wo = pltpu.make_async_copy(wo_ref, wo_s, local_sem.at[1])
+    load_wi = pltpu.make_async_copy(
+        wi_ref, wi_s.at[:, :, 0:units_half], local_sem.at[2]
+    )
+    load_wo.start()
+    load_wi.start()
     greet(
         [(ahead(k), c, t) for k in others]
         + [(f, lax.rem(c + j, z_.ctx), t) for j in range(1, z_.ctx)]
@@ -855,16 +928,30 @@
     )
     for j in range(1, count):
         heads_copy(j).start()
-    for k in others:
-        down_copy(k).start()
     own_heads = pltpu.make_async_copy(
         heads_ref.at[:, c], heads_s.at[c // z_.share], local_sem.at[0]
     )
-    load_wo = pltpu.make_async_copy(wo_ref, wo_s, local_sem.at[1])
-    load_wi = pltpu.make_async_copy(wi_ref, wi_s, local_sem.at[2])
-    own_wm = pltpu.make_async_copy(wm_ref, wm_s.at[f], local_sem.at[3])
-    for copy in (own_heads, load_wo, own_wm, load_wi):
-        copy.start()
+    own_heads.start()
+    load_down.wait()
+
+    def round_down(first, rows):
+        place = pl.ds(first, rows)
+        wm_s[f, place, :] = down_f[place, :].astype(BF16)
+
+    over_rows(0, z_.units, 128, round_down)
+    for k in others:
+        w_copy(0, k, f).start()
+    load_wide.wait()
+    for side in range(2):
+
+        def round_wide(first, rows, side=side):
+            wi_s[side, f, pl.ds(units_half + first, rows), :] = wide_f[
+                side, pl.ds(first, rows), :
+            ].astype(BF16)
+
+        over_rows(0, units_half, 128, round_wide)
+    for k in others:
+        w_copy(1, k, f).start()
     load_wo.wait()
     own_heads.wait()
     for j in range(1, count):
@@ -891,11 +978,10 @@
         sum_copy(r).start()
 
     for k in others:
-        down_copy(k).wait_recv()
-        down_pass(k, core).start()
-    own_wm.wait()
+        w_copy(0, k, behind(k)).wait_recv()
+        w_pass(0, k, core).start()
     for k in others:
-        down_pass(k, 1 - core).wait_recv()
+        w_pass(0, k, 1 - core).wait_recv()
 
     tile = min(128, half)
 
@@ -914,6 +1000,11 @@
 
     lax.fori_loop(0, z_.rows // tile, hidden_grad, 0)
     load_wi.wait()
+    for k in others:
+        w_copy(1, k, behind(k)).wait_recv()
+        w_pass(1, k, core).start()
+    for k in others:
+        w_pass(1, k, 1 - core).wait_recv()
     full = z_.units // 128 * 128
 
     for r in range(2):
@@ -924,21 +1015,27 @@
             middle = tok_ref[rows, :].astype(F32) + (
                 sum_s[rows, :].astype(F32) + sum_in[rows, :].astype(F32)
             )
-            middle_ref[rows, :] = middle
+            middle_s[rows, :] = middle
             normed, scaling = normalize(middle)
             normed_s[rows, :] = normed
             scale_s[rows, :] = jnp.broadcast_to(scaling, (tile, 128))
             gains = jnp.concatenate([gain_ref[g, 1:2, :] for g in range(z_.fsdp)], axis=1)
-            entry = normed * gains
-            entry_s[rows, :] = entry.astype(BF16)
-            entry_t[:, rows] = entry.T.astype(BF16)
+            entry_s[rows, :] = (normed * gains).astype(BF16)
             return carried
 
         lax.fori_loop(0, half // tile, middle_tile, 0)
         rows = pl.ds(r * half, half)
 
         def gate(k, carried):
-            gate_s[k] = jnp.dot(entry_s[rows, :], wi_s[k], preferred_element_type=F32)
+            total = jnp.zeros((half, z_.units), F32)
+            for g in range(z_.fsdp):
+                total = total + lax.dot_general(
+                    entry_s[rows, g * z_.shard : (g + 1) * z_.shard],
+                    wi_s[k, g],
+                    (((1,), (1,)), ((), ())),
+                    preferred_element_type=F32,
+                )
+            gate_s[k] = total
             return carried
 
         lax.fori_loop(0, 2, gate, 0)
@@ -962,28 +1059,31 @@
             place = slice(g * z_.shard, (g + 1) * z_.shard)
             total = jnp.zeros((half, z_.shard), F32)
             for k in range(2):
-                total = total + lax.dot_general(
-                    gated_s[k, rows, :],
-                    wi_s[k, place, :],
-                    (((1,), (1,)), ((), ())),
-                    preferred_element_type=F32,
+                total = total + jnp.dot(
+                    gated_s[k, rows, :], wi_s[k, g], preferred_element_type=F32
                 )
             back_s[rows, place] = total.astype(BF16)
         back_copy(r).start()
 
-    def turn(i, carried):
-        rows = pl.ds(pl.multiple_of(i * tile, tile), tile)
-        for first in range(0, full, 128):
-            block = hidden_s[rows, first : first + 128].astype(F32)
-            hidden_t[first : first + 128, rows] = block.T.astype(BF16)
-        if full < z_.units:
-            rest = z_.units - full
-            block = hidden_s[rows, full : z_.units].astype(F32)
-            block = jnp.concatenate([block, jnp.zeros((tile, 128 - rest), F32)], axis=1)
-            hidden_t[full : z_.units, rows] = block.T[0:rest].astype(BF16)
-        return carried
-
-    lax.fori_loop(0, z_.rows // tile, turn, 0)
+    keep_middle = pltpu.make_async_copy(middle_s, middle_ref, local_sem.at[9])
+    keep_middle.start()
+
+    def turn(source, target):
+        def turn_tile(i, carried):
+            rows = pl.ds(pl.multiple_of(i * tile, tile), tile)
+            for first in range(0, full, 128):
+                block = source[rows, first : first + 128].astype(F32)
+                target[first : first + 128, rows] = block.T.astype(BF16)
+            if full < z_.units:
+                rest = z_.units - full
+                block = source[rows, full : z_.units].astype(F32)
+                block = jnp.concatenate([block, jnp.zeros((tile, 128 - rest), F32)], axis=1)
+                target[full : z_.units, rows] = block.T[0:rest].astype(BF16)
+            return carried
+
+        lax.fori_loop(0, z_.rows // tile, turn_tile, 0)
+
+    turn(hidden_s, hidden_t)
     for g in range(z_.fsdp):
         place = slice(g * z_.shard, (g + 1) * z_.shard)
         for side in range(2):
@@ -994,23 +1094,23 @@
     keep_down = pltpu.make_async_copy(down_s, g_down, local_sem.at[4])
     keep_down.start()
 
-    def wide_grad(k, carried):
+    for k in range(2):
+        turn(gated_s.at[k], gated_t.at[k])
         for g in range(z_.fsdp):
             wide_s[g, k] = jnp.dot(
-                entry_t[g * z_.shard : (g + 1) * z_.shard, :],
-                gated_s[k],
+                gated_t[k],
+                entry_s[:, g * z_.shard : (g + 1) * z_.shard],
                 preferred_element_type=F32,
             ).astype(BF16)
-        return carried
-
-    lax.fori_loop(0, 2, wide_grad, 0)
     keep_wide = pltpu.make_async_copy(wide_s, g_wide, local_sem.at[5])
     keep_wide.start()
     for g in range(z_.fsdp):
         place = slice(g * z_.shard, (g + 1) * z_.shard)
-        branch_ref[:, place] = jnp.dot(
+        branch_s[:, place] = jnp.dot(
             hidden_s[...], wm_s[g], preferred_element_type=F32
         ).astype(BF16)
+    keep_branch = pltpu.make_async_copy(branch_s, branch_ref, local_sem.at[10])
+    keep_branch.start()
 
     gain2_ref[...] = jnp.zeros(gain2_ref.shape, F32)
     for r in range(2):
@@ -1025,11 +1125,14 @@
             grad = cot_ref[rows, :].astype(F32) + norm_back(
                 back * gains, normed, scale_s[rows, 0:1]
             )
-            mgrad_ref[rows, :] = grad
+            grad_f[rows, :] = grad
             mgrad_s[rows, :] = grad.astype(BF16)
             return carried
 
         lax.fori_loop(0, half // tile, back_tile, 0)
+
+    keep_grad = pltpu.make_async_copy(grad_f, mgrad_ref, local_sem.at[11])
+    keep_grad.start()
 
     def heads_grad(rows):
         total = jnp.zeros((half, z_.head_width), F32)
@@ -1074,23 +1177,27 @@
     for j in range(1, count):
         heads_copy(j).wait_send()
     for k in others:
-        down_copy(k).wait_send()
-        down_pass(k, core).wait_send()
+        for n in range(2):
+            w_copy(n, k, f).wait_send()
+            w_pass(n, k, core).wait_send()
     for r in range(2):
         sum_copy(r).wait_send()
         back_copy(r).wait_send()
     keep_down.wait()
     keep_wide.wait()
     keep_attn.wait()
-
-
-def middle_part(z_, tokens, cotangent, gains, heads, wo, wi, wm):
+    keep_middle.wait()
+    keep_branch.wait()
+    keep_grad.wait()
+
+
+def middle_part(z_, tokens, cotangent, gains, heads, wo, wi, wide_weight, down_weight):
     dma = pltpu.SemaphoreType.DMA
     peers = max(1, z_.fsdp - 1)
     count = z_.ctx // z_.share
     rows, width, units = z_.rows, z_.width, z_.units
     down = (z_.fsdp, 2, units // 2, z_.shard)
-    wide = (z_.fsdp, 2, z_.shard, units)
+    wide = (z_.fsdp, 2, units, z_.shard)
     attn = (z_.fsdp, 2, z_.head_width // 2, z_.shard)
     return pl.pallas_call(
         functools.partial(middle_kernel, z_),
@@ -1104,12 +1211,14 @@
             jax.ShapeDtypeStruct(wide, BF16),
             jax.ShapeDtypeStruct(attn, BF16),
         ),
-        in_specs=[vmem()] * 3 + [anywhere()] * 4,
-        out_specs=tuple([vmem()] * 4 + [anywhere()] * 4),
+        in_specs=[vmem()] * 3 + [anywhere()] * 5,
+        out_specs=tuple([anywhere()] * 3 + [vmem()] + [anywhere()] * 4),
         scratch_shapes=[
             pltpu.VMEM((z_.heads, 4, z_.block, 2 * HD), BF16),
             pltpu.VMEM((z_.fsdp, z_.head_width, z_.shard), BF16),
-            pltpu.VMEM((2, width, units), BF16),
+            pltpu.VMEM((2, z_.fsdp, units, z_.shard), BF16),
+            pltpu.VMEM((2, units // 2, z_.shard), F32),
+            pltpu.VMEM((units, z_.shard), F32),
             pltpu.VMEM((z_.fsdp, units, z_.shard), BF16),
             pltpu.VMEM((rows, z_.head_width), BF16),
             pltpu.VMEM((z_.head_width, rows), BF16),
@@ -1118,7 +1227,9 @@
             pltpu.VMEM((rows, width), BF16),
             pltpu.VMEM((rows, width), BF16),
             pltpu.VMEM((rows, width), BF16),
-            pltpu.VMEM((width, rows), BF16),
+            pltpu.VMEM((rows, width), BF16),
+            pltpu.VMEM((rows, width), F32),
+            pltpu.VMEM((rows, width), F32),
             pltpu.VMEM((rows, width), F32),
             pltpu.VMEM((rows, 128), F32),
             pltpu.VMEM((2, rows // 2, units), F32),
@@ -1126,6 +1237,7 @@
             pltpu.VMEM((rows, units), BF16),
             pltpu.VMEM((units, rows), BF16),
             pltpu.VMEM((2, rows, units), BF16),
+            pltpu.VMEM((2, units, rows), BF16),
             pltpu.VMEM((rows, width), BF16),
             pltpu.VMEM((z_.heads, 4, z_.block, 2 * HD), BF16),
             pltpu.VMEM(down, BF16),
@@ -1137,38 +1249,17 @@
             dma((z_.ctx,)),
             dma((4,)),
             dma((4,)),
-            dma((peers,)),
-            dma((peers,)),
-            dma((peers,)),
-            dma((peers,)),
-            dma((8,)),
+            dma((2, peers)),
+            dma((2, peers)),
+            dma((2, peers)),
+            dma((2, peers)),
+            dma((12,)),
         ],
         compiler_params=pltpu.CompilerParams(
             collective_id=2, has_side_effects=True, vmem_limit_bytes=VMEM_BYTES
         ),
         name="middle",
-    )(tokens, cotangent, gains, heads, wo, wi, wm)
-
-
-def cuts_of(rows, count):
-    unit = rows // 16
-    marks = [16 * (unit * i // count) for i in range(count + 1)]
-    return [(a, b - a) for a, b in zip(marks, marks[1:]) if b > a]
-
-
-def over_rows(start, rows, step, body):
-    whole = rows // step
-
-    def turn(i, carried):
-        body(pl.multiple_of(start + i * step, 16), step)
-        return carried
-
-    if whole > 1:
-        lax.fori_loop(0, whole, turn, 0)
-    elif whole == 1:
-        body(start, step)
-    if rows % step:
-        body(start + whole * step, rows % step)
+    )(tokens, cotangent, gains, heads, wo, wi, wide_weight, down_weight)
 
 
 class Item:
@@ -1298,23 +1389,15 @@
         )
 
     def done_copy(self, item, cut):
-        inner_in, out = self.refs[item.number][5:7]
+        inner_in, mate_out = self.refs[item.number][5:7]
         rows = pl.ds(*item.cuts[cut])
         n = self.numbers[(item.number, cut)]
         return remote(
             inner_in.at[rows],
-            out.at[self.core, rows],
+            mate_out.at[rows],
             self.sems["done_send"].at[n],
             self.sems["done_recv"].at[n],
             self.mate,
-        )
-
-    def keep_copy(self, item, cut):
-        inner_in, out = self.refs[item.number][5:7]
-        rows = pl.ds(*item.cuts[cut])
-        n = self.numbers[(item.number, cut)]
-        return pltpu.make_async_copy(
-            inner_in.at[rows], out.at[self.core, rows], self.sems["keep"].at[n]
         )
 
     def outermost_start(self, item):
@@ -1369,14 +1452,24 @@
             self.out_copy(item, cut).start()
 
         self.done_copy(item, cut).start()
-        self.keep_copy(item, cut).start()
-
-    def line(self, parts):
+
+    def line(self, parts, finish, before):
         for i, (item, cut) in enumerate(parts):
+            if i in before:
+                before[i]()
+            if i >= 2:
+                finish.load(*parts[i - 2])
             self.inward(item, cut)
-            if i:
+            if i >= 1:
                 self.outward(*parts[i - 1])
-        self.outward(*parts[-1])
+            if i >= 2:
+                finish.update(*parts[i - 2])
+        for i in (len(parts) - 2, len(parts) - 1):
+            if i >= 0:
+                finish.load(*parts[i])
+                if i == len(parts) - 1:
+                    self.outward(*parts[i])
+                finish.update(*parts[i])
 
     def settle(self):
         for item in self.items:
@@ -1390,8 +1483,124 @@
                 def outwards(item=item, cut=cut):
                     self.out_copy(item, cut).wait_send()
 
-                self.done_copy(item, cut).wait()
-                self.keep_copy(item, cut).wait()
+                self.done_copy(item, cut).wait_send()
+
+
+def adam_step(weight, gradient, moment, squared, rate_now):
+    first = BETA_FIRST * moment + (1.0 - BETA_FIRST) * gradient
+    second = BETA_SECOND * squared + (1.0 - BETA_SECOND) * gradient * gradient
+    corrected = first / (1.0 - BETA_FIRST**STEP)
+    spread = jnp.sqrt(second / (1.0 - BETA_SECOND**STEP))
+    return (weight - rate_now * (corrected / (spread + ADAM_EPS) + DECAY * weight), first, second)
+
+
+class Finisher:
+    def __init__(self, z_, reducer, states, results, rates, plain_s, pair_s, load_sem, store_sem):
+        self.z_ = z_
+        self.red = reducer
+        self.states = states
+        self.results = results
+        self.rates = rates
+        self.plain_s = plain_s
+        self.pair_s = pair_s
+        self.load_sem = load_sem
+        self.store_sem = store_sem
+        self.stored = None
+
+    def places(self, refs, item, cut, side):
+        first, rows = item.cuts[cut]
+        number = item.number
+        half = self.z_.shard // 2
+        found = []
+        for n in range(3):
+            if number == 3:
+                place = refs[number][n].at[
+                    :,
+                    pl.ds(pl.multiple_of(side * half, half), half),
+                    2 * HD * cut : 2 * HD * (cut + 1),
+                ]
+                slot = self.pair_s
+            else:
+                slot = self.plain_s
+                if number == 1:
+                    place = refs[number][n].at[side, first : first + rows]
+                else:
+                    place = refs[number][n].at[
+                        pl.ds(pl.multiple_of(side * item.rows + first, 16), rows)
+                    ]
+            found.append((n, place, slot, rows))
+        return found
+
+    def slot_view(self, slot, which, n, rows):
+        if slot is self.pair_s:
+            return slot.at[which, n]
+        return slot.at[which, n, 0:rows]
+
+    def copies(self, refs, item, cut, sems, outwards):
+        made = []
+        for which in range(2):
+            side = self.red.core if which == 0 else 1 - self.red.core
+            for n, place, slot, rows in self.places(refs, item, cut, side):
+                view = self.slot_view(slot, which, n, rows)
+                ends = (view, place) if outwards else (place, view)
+                made.append(pltpu.make_async_copy(*ends, sems.at[which, n]))
+        return made
+
+    def settle(self):
+        if self.stored is not None:
+            for copy in self.copies(self.results, *self.stored, self.store_sem, True):
+                copy.wait()
+        self.stored = None
+
+    def load(self, item, cut):
+        if item.number == 4:
+            return
+        self.settle()
+        for copy in self.copies(self.states, item, cut, self.load_sem, False):
+            copy.start()
+
+    def update(self, item, cut):
+        if item.number == 4:
+            self.gain_update()
+            return
+        for copy in self.copies(self.states, item, cut, self.load_sem, False):
+            copy.wait()
+        first, rows = item.cuts[cut]
+        inner_in, mate_out = self.red.refs[item.number][5:7]
+        rate = self.rates[item.number]
+        for which, sums in ((0, inner_in), (1, mate_out)):
+            if which == 1:
+                self.red.done_copy(item, cut).wait_recv()
+
+            def step(start, count, which=which, sums=sums):
+                place = pl.ds(start, count)
+                gradient = sums[pl.ds(first + start, count), :].astype(F32)
+                if item.number == 3:
+                    for kind in range(3):
+                        got = adam_step(
+                            self.pair_s[which, 0, kind, place, :],
+                            gradient[:, 2 * HD * kind : 2 * HD * (kind + 1)],
+                            self.pair_s[which, 1, kind, place, :],
+                            self.pair_s[which, 2, kind, place, :],
+                            rate,
+                        )
+                        for n in range(3):
+                            self.pair_s[which, n, kind, place, :] = got[n]
+                else:
+                    got = adam_step(
+                        self.plain_s[which, 0, place, :],
+                        gradient,
+                        self.plain_s[which, 1, place, :],
+                        self.plain_s[which, 2, place, :],
+                        rate,
+                    )
+                    for n in range(3):
+                        self.plain_s[which, n, place, :] = got[n]
+
+            over_rows(0, rows, 64, step)
+        for copy in self.copies(self.results, item, cut, self.store_sem, True):
+            copy.start()
+        self.stored = (item, cut)
 
 
 def reduce_kernel(
@@ -1405,32 +1614,33 @@
     middle_ref,
     mgrad_ref,
     gain2_ref,
+    gw_ref,
+    gm_ref,
+    gv_ref,
     heads_ref,
     wq_ref,
     g_down,
     g_wide,
     g_attn,
-    out_ref,
-    igrad_ref,
-    o_down,
-    o_wide,
-    o_attn,
-    o_qkv,
-    o_gain,
-    *scratch,
+    *others,
 ):
     down, wide, attn, qkv, gain = items
-    scratch = list(scratch)
+    scratch = list(others)
 
     def take(count):
         taken = scratch[:count]
         del scratch[:count]
         return taken
 
-    heads_s, wq_s, entry_s, grads_s, branch_s, back_s, back_in = take(7)
-    g_qkv, g_gain, gain_acc = take(3)
-    groups = [take(5) for item in items]
-    (a_send, a_recv, y_send, y_recv, local_sem) = take(5)
+    states = [take(3) for n in range(4)]
+    out_ref, igrad_ref = take(2)
+    results = [take(3) for n in range(4)]
+    gain_results = take(3)
+    heads_s, wq_s, entry_s, grads_s, branch_own, branch_s, back_s, back_in = take(8)
+    middle_s, mgrad_s = take(2)
+    g_qkv, g_gain, gain_acc, plain_s, pair_s = take(5)
+    groups = [take(6) for item in items]
+    (a_send, a_recv, y_send, y_recv, local_sem, load_sem, store_sem) = take(7)
     names = (
         "core_send",
         "core_recv",
@@ -1443,15 +1653,13 @@
         "out_send",
         "done_send",
         "done_recv",
-        "keep",
     )
     sems = dict(zip(names, take(len(names))))
     sources = (g_down, g_wide, g_attn, g_qkv, g_gain)
-    outs = (o_down, o_wide, o_attn, o_qkv, o_gain)
-    refs = [
-        (source, *group, out) for source, group, out in zip(sources, groups, outs)
-    ]
+    refs = [(source, *group) for source, group in zip(sources, groups)]
     red = Reducer(z_, items, refs, sems)
+    rates = (FF ** (-0.5), D ** (-0.5), RATE_ATTN, D ** (-0.5))
+    finish = Finisher(z_, red, states, results, rates, plain_s, pair_s, load_sem, store_sem)
     f, c, t = red.f, red.c, red.t
     other = (f, c, 1 - t)
     count = z_.ctx // z_.share
@@ -1477,6 +1685,16 @@
     def back_copy():
         return remote(back_s, back_in, y_send.at[1], y_recv.at[1], other)
 
+    load_wq = pltpu.make_async_copy(wq_ref, wq_s, local_sem.at[1])
+    load_branch = pltpu.make_async_copy(branch_ref, branch_own, local_sem.at[2])
+    load_middle = pltpu.make_async_copy(middle_ref, middle_s, local_sem.at[3])
+    load_mgrad = pltpu.make_async_copy(mgrad_ref, mgrad_s, local_sem.at[4])
+    for item in (down, wide, attn):
+        red.own_copy(item).start()
+    load_wq.start()
+    load_branch.start()
+    load_middle.start()
+    load_mgrad.start()
     greet(
         [(red.ahead(k), c, t) for k in range(1, z_.fsdp)]
         + [(f, lax.rem(c + j, z_.ctx), t) for j in range(1, z_.ctx)]
@@ -1489,9 +1707,6 @@
     own_heads.start()
     for item in (down, wide, attn):
         red.core_copy(item).start()
-        red.own_copy(item).start()
-    load_wq = pltpu.make_async_copy(wq_ref, wq_s, local_sem.at[1])
-    load_wq.start()
 
     for item in (down, wide, attn):
         red.own_copy(item).wait()
@@ -1514,11 +1729,13 @@
     red.outermost_start(down)
 
     branch_copy().wait_recv()
+    load_branch.wait()
+    load_middle.wait()
 
     def output_tile(i, carried):
         rows = pl.ds(pl.multiple_of(i * tile, tile), tile)
-        branch = branch_ref[rows, :].astype(F32) + branch_s[rows, :].astype(F32)
-        out_ref[rows, :] = (middle_ref[rows, :] + branch).astype(BF16)
+        branch = branch_own[rows, :].astype(F32) + branch_s[rows, :].astype(F32)
+        out_ref[rows, :] = (middle_s[rows, :] + branch).astype(BF16)
         return carried
 
     lax.fori_loop(0, z_.rows // tile, output_tile, 0)
@@ -1534,19 +1751,29 @@
         ).wait_recv()
     load_wq.wait()
 
+    lane = lax.broadcasted_iota(jnp.int32, (z_.rows, 2 * HD), 1) < HD
+    lane_half = lax.broadcasted_iota(jnp.int32, (z_.rows // 2, 2 * HD), 1) < HD
+    mid_row = z_.rows // 2
+
     def chunk_grads(p, carried):
-        for i in range(z_.chip_heads):
-            h = p * z_.chip_heads + i
-            pair = heads_s[h, 0:8].reshape(z_.rows, 2 * HD).astype(F32)
-            pair = pair * cos_ref[...] - swap_halves(pair) * sin_ref[...]
-            grads_s[p, :, 2 * HD * i : 2 * HD * (i + 1)] = pair.astype(BF16)
-            value = heads_s[h, 8:12].reshape(z_.rows // 2, 2 * HD).astype(F32)
-            start = z_.chip_heads * 2 * HD + HD * i
-            grads_s[p, 0 : z_.rows // 2, start : start + HD] = value[:, 0:HD].astype(BF16)
-            grads_s[p, z_.rows // 2 :, start : start + HD] = value[:, HD : 2 * HD].astype(BF16)
+        pair = [
+            heads_s[2 * p + i, 0:8].reshape(z_.rows, 2 * HD).astype(F32) for i in range(2)
+        ]
+        query = jnp.where(lane, pair[0], pltpu.roll(pair[1], HD, 1))
+        key = jnp.where(lane, pltpu.roll(pair[0], HD, 1), pair[1])
+        for kind, part in ((0, query), (1, key)):
+            part = part * cos_ref[...] - swap_halves(part) * sin_ref[...]
+            grads_s[p, :, 2 * HD * kind : 2 * HD * (kind + 1)] = part.astype(BF16)
+        value = [
+            heads_s[2 * p + i, 8:12].reshape(mid_row, 2 * HD).astype(F32) for i in range(2)
+        ]
+        early = jnp.where(lane_half, value[0], pltpu.roll(value[1], HD, 1))
+        late = jnp.where(lane_half, pltpu.roll(value[0], HD, 1), value[1])
+        grads_s[p, 0:mid_row, 4 * HD : 6 * HD] = early.astype(BF16)
+        grads_s[p, mid_row : z_.rows, 4 * HD : 6 * HD] = late.astype(BF16)
         return carried
 
-    lax.fori_loop(0, z_.chips, chunk_grads, 0)
+    lax.fori_loop(0, z_.pairs, chunk_grads, 0)
 
     for g in range(z_.fsdp):
         columns = slice(g * z_.shard, (g + 1) * z_.shard)
@@ -1554,7 +1781,7 @@
         def back_tile(i, carried):
             rows = pl.ds(pl.multiple_of(i * tile, tile), tile)
             total = jnp.zeros((tile, z_.shard), F32)
-            for p in range(z_.chips):
+            for p in range(z_.pairs):
                 total = total + lax.dot_general(
                     grads_s[p, rows, :],
                     wq_s[p, g],
@@ -1581,7 +1808,7 @@
                 g_qkv[g, side, rows, :] = grad.astype(BF16)
         return carried
 
-    lax.fori_loop(0, z_.chips, qkv_tile, 0)
+    lax.fori_loop(0, z_.pairs, qkv_tile, 0)
     red.core_copy(qkv).start()
     red.own_copy(qkv).start()
     red.peer_sum(wide)
@@ -1593,56 +1820,91 @@
     red.outermost_start(attn)
 
     parts = [(item, cut) for item in (down, wide, attn) for cut in range(len(item.cuts))]
-    early = len(parts) - 2
-    red.line(parts[:early])
-
-    back_copy().wait_recv()
-    gain_acc[...] = jnp.zeros(gain_acc.shape, F32)
-
-    def input_tile(i, carried):
-        rows = pl.ds(pl.multiple_of(i * tile, tile), tile)
-        normed, scaling = normalize(tok_ref[rows, :].astype(F32))
-        back = back_s[rows, :].astype(F32) + back_in[rows, :].astype(F32)
-        gain_acc[0:1, :] += jnp.sum(back * normed, axis=0, keepdims=True)
-        gains = jnp.concatenate([gain_ref[g, 0:1, :] for g in range(z_.fsdp)], axis=1)
-        igrad_ref[rows, :] = (
-            mgrad_ref[rows, :] + norm_back(back * gains, normed, scaling)
-        ).astype(BF16)
-        return carried
-
-    lax.fori_loop(0, z_.rows // tile, input_tile, 0)
-    top = lax.broadcasted_iota(jnp.int32, (16, z_.shard), 0) == 0
-    for g in range(z_.fsdp):
-        columns = slice(g * z_.shard, (g + 1) * z_.shard)
-        for side, row in ((0, gain_acc[0:1, columns]), (1, gain2_ref[0:1, columns])):
-            g_gain[g, side] = jnp.where(top, row, 0.0).astype(BF16)
-    red.core_copy(gain).start()
-    red.own_copy(gain).start()
-    red.peer_sum(qkv)
-    red.outermost_start(qkv)
-    red.own_copy(gain).wait()
-    red.core_sum(gain)
-    red.peer_start(gain)
-    rest = parts[early:] + [(qkv, cut) for cut in range(len(qkv.cuts))]
-    red.line(rest[:2])
-    red.peer_sum(gain)
-    red.outermost_start(gain)
-    red.line(rest[2:] + [(gain, 0)])
+    def input_part():
+        back_copy().wait_recv()
+        load_mgrad.wait()
+        gain_acc[...] = jnp.zeros(gain_acc.shape, F32)
+
+        def input_tile(i, carried):
+            rows = pl.ds(pl.multiple_of(i * tile, tile), tile)
+            normed, scaling = normalize(tok_ref[rows, :].astype(F32))
+            back = back_s[rows, :].astype(F32) + back_in[rows, :].astype(F32)
+            gain_acc[0:1, :] += jnp.sum(back * normed, axis=0, keepdims=True)
+            gains = jnp.concatenate([gain_ref[g, 0:1, :] for g in range(z_.fsdp)], axis=1)
+            igrad_ref[rows, :] = (
+                mgrad_s[rows, :] + norm_back(back * gains, normed, scaling)
+            ).astype(BF16)
+            return carried
+
+        lax.fori_loop(0, z_.rows // tile, input_tile, 0)
+        top = lax.broadcasted_iota(jnp.int32, (16, z_.shard), 0) == 0
+        for g in range(z_.fsdp):
+            columns = slice(g * z_.shard, (g + 1) * z_.shard)
+            for side, row in ((0, gain_acc[0:1, columns]), (1, gain2_ref[0:1, columns])):
+                g_gain[g, side] = jnp.where(top, row, 0.0).astype(BF16)
+        red.core_copy(gain).start()
+        red.own_copy(gain).start()
+        red.peer_sum(qkv)
+        red.outermost_start(qkv)
+        red.own_copy(gain).wait()
+        red.core_sum(gain)
+        red.peer_start(gain)
+
+    def gain_part():
+        red.peer_sum(gain)
+        red.outermost_start(gain)
+
+    def gain_update():
+        red.done_copy(gain, 0).wait_recv()
+        inner_in, mate_out = red.refs[4][5:7]
+        own_row = inner_in[0:1, :].astype(F32)
+        mate_row = mate_out[0:1, :].astype(F32)
+        first = (red.core == 0).astype(F32)
+        for row, gradient in (
+            (0, own_row * first + mate_row * (1.0 - first)),
+            (1, mate_row * first + own_row * (1.0 - first)),
+        ):
+            place = slice(row, row + 1)
+            got = adam_step(gw_ref[place, :], gradient, gm_ref[place, :], gv_ref[place, :], RATE_GAIN)
+            for n in range(3):
+                gain_results[n][place, :] = got[n]
+
+    finish.gain_update = gain_update
+    parts += [(qkv, cut) for cut in range(len(qkv.cuts))]
+    spot = len(parts) - 2
+    parts.insert(spot, (gain, 0))
+    red.line(parts, finish, {spot - 4: input_part, spot: gain_part})
 
     own_sends = [heads_copy(j) for j in range(1, count)] + [branch_copy(), back_copy()]
     for copy in own_sends:
         copy.wait_send()
     red.settle()
+    finish.settle()
 
 
 def reduce_all(
-    z_, tokens, gains, cosine, sines, branch, middle, middle_grad, gain2, heads, wq, g_down, g_wide, g_attn
+    z_,
+    tokens,
+    gains,
+    cosine,
+    sines,
+    branch,
+    middle,
+    middle_grad,
+    gain2,
+    gain_states,
+    heads,
+    wq,
+    g_down,
+    g_wide,
+    g_attn,
+    states,
 ):
     items = (
         Item(0, z_.units // 2, z_.shard, 2),
-        Item(1, z_.shard, z_.units, 4),
+        Item(1, z_.units, z_.shard, 4),
         Item(2, z_.head_width // 2, z_.shard, 1),
-        Item(3, z_.chips * (z_.shard // 2), z_.chunk, 4),
+        Item(3, z_.pairs * (z_.shard // 2), 6 * HD, z_.pairs),
         Item(4, 16, z_.shard, 1),
     )
     dma = pltpu.SemaphoreType.DMA
@@ -1656,32 +1918,45 @@
             pltpu.VMEM((peers, item.rows, item.columns), BF16),
             pltpu.VMEM((item.rows, item.columns), BF16),
             pltpu.VMEM((item.rows, item.columns), BF16),
+            pltpu.VMEM((item.rows, item.columns), BF16),
         ]
     count = z_.ctx // z_.share
     number = len(items)
+    largest = max(rows for item in items[:3] for first, rows in item.cuts)
+    rows = (z_.rows, z_.width)
+    flat = [array for group in states for array in group]
     return pl.pallas_call(
         functools.partial(reduce_kernel, z_, items),
-        out_shape=(
-            jax.ShapeDtypeStruct((z_.rows, z_.width), BF16),
-            jax.ShapeDtypeStruct((z_.rows, z_.width), BF16),
-        )
-        + tuple(jax.ShapeDtypeStruct((2, item.rows, item.columns), BF16) for item in items),
-        in_specs=[vmem()] * 8 + [anywhere()] * 5,
-        out_specs=tuple([vmem()] * 2 + [anywhere()] * 5),
+        out_shape=tuple(
+            [jax.ShapeDtypeStruct(rows, BF16)] * 2
+            + [jax.ShapeDtypeStruct(array.shape, F32) for array in flat]
+            + [jax.ShapeDtypeStruct(array.shape, F32) for array in gain_states]
+        ),
+        in_specs=[vmem()] * 4
+        + [anywhere()] * 3
+        + [vmem()] * 4
+        + [anywhere()] * 5
+        + [anywhere()] * 12,
+        out_specs=tuple([vmem()] * 2 + [anywhere()] * 12 + [vmem()] * 3),
         scratch_shapes=[
             pltpu.VMEM((z_.heads, 12, z_.block, 2 * HD), BF16),
-            pltpu.VMEM((z_.chips, z_.fsdp, z_.shard, z_.chunk), BF16),
+            pltpu.VMEM((z_.pairs, z_.fsdp, z_.shard, 6 * HD), BF16),
             pltpu.VMEM((z_.fsdp, z_.shard, z_.rows), BF16),
-            pltpu.VMEM((z_.chips, z_.rows, z_.chunk), BF16),
-            pltpu.VMEM((z_.rows, z_.width), BF16),
-            pltpu.VMEM((z_.rows, z_.width), BF16),
-            pltpu.VMEM((z_.rows, z_.width), BF16),
+            pltpu.VMEM((z_.pairs, z_.rows, 6 * HD), BF16),
+            pltpu.VMEM(rows, BF16),
+            pltpu.VMEM(rows, BF16),
+            pltpu.VMEM(rows, BF16),
+            pltpu.VMEM(rows, BF16),
+            pltpu.VMEM(rows, F32),
+            pltpu.VMEM(rows, F32),
             pltpu.VMEM((z_.fsdp, 2, items[3].rows, items[3].columns), BF16),
             pltpu.VMEM((z_.fsdp, 2, 16, z_.shard), BF16),
             pltpu.VMEM((8, z_.width), F32),
+            pltpu.VMEM((2, 3, largest, z_.shard), F32),
+            pltpu.VMEM((2, 3, 3, z_.shard // 2, 2 * HD), F32),
         ]
         + groups
-        + [dma((count,)), dma((count,)), dma((2,)), dma((2,)), dma((2,))]
+        + [dma((count,)), dma((count,)), dma((2,)), dma((2,)), dma((5,)), dma((2, 3)), dma((2, 3))]
         + [
             dma((number,)),
             dma((number,)),
@@ -1689,47 +1964,28 @@
             dma((number, peers)),
             dma((number, peers)),
         ]
-        + [dma((pieces,))] * 7,
+        + [dma((pieces,))] * 6,
         compiler_params=pltpu.CompilerParams(
             collective_id=1, has_side_effects=True, vmem_limit_bytes=VMEM_BYTES
         ),
         name="reduce",
-    )(tokens, gains, cosine, sines, branch, middle, middle_grad, gain2, heads, wq, g_down, g_wide, g_attn)
-
-
-def adam_step(weight, gradient, moment, squared, rate_now):
-    first = BETA_FIRST * moment + (1.0 - BETA_FIRST) * gradient
-    second = BETA_SECOND * squared + (1.0 - BETA_SECOND) * gradient * gradient
-    corrected = first / (1.0 - BETA_FIRST**STEP)
-    spread = jnp.sqrt(second / (1.0 - BETA_SECOND**STEP))
-    return (weight - rate_now * (corrected / (spread + ADAM_EPS) + DECAY * weight), first, second)
-
-
-def update_all(weights, gradients, moments, squares, rates):
-    results = []
-    for weight, gradient, moment, squared, rate_now in zip(
-        weights, gradients, moments, squares, rates
-    ):
-        results.extend(adam_step(weight, gradient, moment, squared, rate_now))
-    return results
-
-
-def by_chip(z_, weight):
-    rows = weight.shape[0]
-    split = weight.reshape(rows, 3, z_.chips, z_.chip_heads, HD)
-    pairs = split[:, 0:2].transpose(2, 0, 3, 1, 4).reshape(z_.chips, rows, -1)
-    values = split[:, 2].transpose(1, 0, 2, 3).reshape(z_.chips, rows, -1)
-    return jnp.concatenate([pairs, values], axis=2)
-
-
-def from_chips(z_, chunked):
-    rows = chunked.shape[1]
-    cut = z_.chip_heads * 2 * HD
-    pairs = chunked[:, :, :cut].reshape(z_.chips, rows, z_.chip_heads, 2, HD)
-    pairs = pairs.transpose(1, 3, 0, 2, 4).reshape(rows, 2, z_.head_width)
-    values = chunked[:, :, cut:].reshape(z_.chips, rows, z_.chip_heads, HD)
-    values = values.transpose(1, 0, 2, 3).reshape(rows, 1, z_.head_width)
-    return jnp.concatenate([pairs, values], axis=1)
+    )(
+        tokens,
+        gains,
+        cosine,
+        sines,
+        branch,
+        middle,
+        middle_grad,
+        gain2,
+        *gain_states,
+        heads,
+        wq,
+        g_down,
+        g_wide,
+        g_attn,
+        *flat,
+    )
 
 
 def on_device(
@@ -1774,9 +2030,9 @@
         gain_rows,
         cosine,
         sines,
-        by_chip(z_, qkv_weight.astype(BF16)),
-        attn_weight.astype(BF16),
-        wide_weight.astype(BF16).transpose(1, 0, 2),
+        qkv_weight.transpose(1, 0, 2),
+        attn_weight,
+        wide_weight.transpose(1, 2, 0),
     )
     attended_packed, attended_turned, lse = attend(z_, endings, packed)
     branch_low, middle, middle_grad, gain_second, grads_packed, down_grad, wide_grad, attn_grad = (
@@ -1787,8 +2043,9 @@
             gains_full,
             attended_packed,
             wo_full,
-            wi_full.reshape(2, z_.width, z_.units),
-            down_weight.astype(BF16),
+            wi_full,
+            wide_weight.transpose(1, 2, 0),
+            down_weight,
         )
     )
     head_grads = attend_back(
@@ -1799,7 +2056,7 @@
         attended_turned,
         lse,
     )
-    output, input_grad, down_sum, wide_sum, attn_sum, qkv_sum, gain_sum = reduce_all(
+    output, input_grad, *updated = reduce_all(
         z_,
         tokens,
         gains_full,
@@ -1809,29 +2066,29 @@
         middle,
         middle_grad,
         gain_second,
+        (norm_gains, gains_mean, gains_square),
         head_grads,
         wq_full,
         down_grad,
         wide_grad,
         attn_grad,
-    )
-    qkv_sum = qkv_sum.reshape(2, z_.chips, z_.shard // 2, z_.chunk).transpose(1, 0, 2, 3)
-    shards = (
-        from_chips(z_, qkv_sum.reshape(z_.chips, z_.shard, z_.chunk)).astype(F32),
-        attn_sum.reshape(z_.head_width, z_.shard).astype(F32),
-        wide_sum.transpose(1, 0, 2).astype(F32),
-        down_sum.reshape(z_.units, z_.shard).astype(F32),
-        gain_sum[:, 0, :].astype(F32),
-    )
-    rates = (D ** (-0.5), RATE_ATTN, D ** (-0.5), FF ** (-0.5), RATE_GAIN)
-    final = update_all(
-        (qkv_weight, attn_weight, wide_weight, down_weight, norm_gains),
-        shards,
-        (qkv_mean, attn_mean, wide_mean, down_mean, gains_mean),
-        (qkv_square, attn_square, wide_square, down_square, gains_square),
-        rates,
-    )
-    return (output, input_grad) + tuple(final)
+        (
+            (down_weight, down_mean, down_square),
+            [array.transpose(1, 2, 0) for array in (wide_weight, wide_mean, wide_square)],
+            (attn_weight, attn_mean, attn_square),
+            [array.transpose(1, 0, 2) for array in (qkv_weight, qkv_mean, qkv_square)],
+        ),
+    )
+    down_new, wide_new, attn_new, qkv_new, gains_new = [updated[n : n + 3] for n in range(0, 15, 3)]
+    return (
+        output,
+        input_grad,
+        *[array.transpose(1, 0, 2) for array in qkv_new],
+        *attn_new,
+        *[array.transpose(2, 0, 1) for array in wide_new],
+        *down_new,
+        *gains_new,
+    )
 
 
 def solution(mesh):

time: 549 us -> 384 us (0.70); the launches traced: 539 us -> 385 us
  Pallas kernels: 405 us -> 346 us
  local copies, waits for them, and re-layouts: 83.1 us -> 33.9 us
  other arithmetic: 49.7 us -> 4.72 us
    pallas_call x1, Pallas kernels: 112 us -> 49.3 us  [project(): pl.pallas_call(functools.partial(project_kernel, z_), out_shape=(jax.Shap...]
    sub x5 -> x0, other arithmetic: 32.6 us -> none  [adam_step(): weight - rate_now * (corrected / (spread + ADAM_EPS) + DECAY * weight)]
    unnamed x40 -> x55, local copies, waits for them, and re-layouts: 60.2 us -> 33.9 us
    convert_element_type x5 -> x0, other arithmetic: 10.4 us -> none  [the longest x1 4.38 us: on_device(): wide_weight.astype(BF16).transpose(1, 0, 2)]
    pallas_call x1, Pallas kernels: 165 us -> 155 us  [reduce_all(): pl.pallas_call(functools.partial(reduce_kernel, z_, items), out_shape=tup...]
    slice x5 -> x0, local copies, waits for them, and re-layouts: 9.08 us -> none  [the longest x2 3.91 us: from_chips(): values = chunked[:, :, cut:].reshape(z_.chips, rows, z_.chip_heads, HD)]
    pallas_call x1, Pallas kernels: 27.6 us -> 34.9 us  [attend_back(): pl.pallas_call(functools.partial(attend_back_kernel, z_, q_tile, k_tile),...]
    reshape x3 -> x0, local copies, waits for them, and re-layouts: 5.88 us -> none  [the longest x1 2.26 us: by_chip(): pairs = split[:, 0:2].transpose(2, 0, 3, 1, 4).reshape(z_.chips, rows, -1)]
where the time goes in v4:
time: 384 us; the launch traced here: 385 us
  Pallas kernels  346 us (90%)
  local copies, waits for them, and re-layouts  33.9 us (9%)
  other arithmetic  4.72 us (1%)
    pallas_call x1, Pallas kernels, reduce_all(): pl.pallas_call(functools.partial(reduce_kernel, z_, items), out_shape=tup...  155 us
    pallas_call x1, Pallas kernels, middle_part(): pl.pallas_call(functools.partial(middle_kernel, z_), out_shape=(jax.Shape...  80.2 us
    pallas_call x1, Pallas kernels, project(): pl.pallas_call(functools.partial(project_kernel, z_), out_shape=(jax.Shap...  49.3 us
    pallas_call x1, Pallas kernels, attend_back(): pl.pallas_call(functools.partial(attend_back_kernel, z_, q_tile, k_tile),...  34.9 us
    unnamed x55, local copies, waits for them, and re-layouts  33.9 us
    pallas_call x1, Pallas kernels, attend(): pl.pallas_call(functools.partial(attend_kernel, z_, q_tile, k_tile), out_...  25.8 us

profile of v4, /device:TPU:0, one launch (start us, length us, event | category | flops | bytes accessed | tf_op | source)
XLA Modules:
  0.0 385.1 jit_solution(14941369161233835805)
XLA Ops:
  0.7 0.9 select_reduce_fusion.1
  1.5 0.2 reduce-window.8
  1.7 0.0 copy-start.9
  1.7 0.7 convert_element_type.15
  2.4 0.1 select_reduce_fusion
  2.5 0.6 pad_convert_fusion.gain_ref
  3.1 1.0 fusion
  4.1 1.3 pad_maximum_fusion
  5.4 49.3 %project.1 = (bf16[12,8,64,128]{3,2,1,0:T(8,128)(2,1)}, bf16[4,2,512,384]{3,2,1,0:T(8,128)(2,1)}, bf16[2,512,512]{2,1,0:T(8,128)(2,1)}, bf16[2,2,656,512]{3,2,1,0:T(8,128)(2,1)}, f32[2,8,512]{2,1,0:T(8,128)}) custom-call(bf16[512,1024]{1,0:T(8,128)(2,1)} %tok_ref.5, f32[8,512]{1,0:T(8,128)} %pad_convert_fusion.gain_ref, ...), custom_call_target="tpu_custom_call" | custom-call | tf_op jit(solution)/shard_map/project/pallas_call | solution.py:423
  54.7 0.0 copy-done.9
  54.7 25.8 %attend.1 = (bf16[4,8,64,128]{3,2,1,0:T(8,128)(2,1)}, f32[64,4096]{1,0:T(8,128)}, f32[8,4096]{1,0:T(8,128)}) custom-call(s32[4]{0:T(128)} %bitcast.38, bf16[12,8,64,128]{3,2,1,0:T(8,128)(2,1)} %get-tuple-element.51.packed_ref), custom_call_target="tpu_custom_call" | custom-call | tf_op jit(solution)/shard_map/attend/pallas_call | solution.py:588
  80.6 80.2 %middle.1 = (bf16[512,1024]{1,0:T(8,128)(2,1)}, f32[512,1024]{1,0:T(8,128)}, f32[512,1024]{1,0:T(8,128)}, f32[8,1024]{1,0:T(8,128)}, bf16[4,8,64,128]{3,2,1,0:T(...) custom-call(bf16[512,1024]{1,0:T(8,128)(2,1)} %tok_ref.5, ...), custom_call_target="tpu_custom_call" | custom-call | tf_op jit(solution)/shard_map/middle/pallas_call | solution.py:1202
  160.8 34.9 %attend_back.1.heads_ref = bf16[12,8,64,128]{3,2,1,0:T(8,128)(2,1)} custom-call(s32[4]{0:T(128)} %bitcast.39, bf16[12,8,64,128]{3,2,1,0:T(8,128)(2,1)} %get-tuple-element.51.packed_ref, bf16[4,8,64,128]{3,2,1,0:T(8,128)(2,1)} %get-tuple-element.59.grad_ref, f32[64,4096]{1,0:T(8,128)} %get-tuple-element.60.outt_ref, f32[8,4096]{1,0:T(8,128)} %get-tuple-element.61.lse_ref), custom_call_target="tpu_custom_call" | custom-call | tf_op jit(solution)/shard_map/attend_back/pallas_call | solution.py:752
  195.7 155.4 %reduce.1 = (bf16[512,1024]{1,0:T(8,128)(2,1)}, bf16[512,1024]{1,0:T(8,128)(2,1)}, f32[1312,512]{1,0:T(8,128)}, f32[1312,512]{1,0:T(8,128)}, f32[1312,512]{1,0:T...) custom-call(bf16[512,1024]{1,0:T(8,128)(2,1)} %tok_ref.5, ...), custom_call_target="tpu_custom_call" | custom-call | tf_op jit(solution)/shard_map/reduce/pallas_call | solution.py:1928
  351.1 0.0 copy-start.2
  351.1 2.4 copy.54
  353.5 2.3 copy.55
  355.8 0.0 copy-done.2
  355.8 0.0 copy-start.1
  355.8 1.7 copy.56
  357.5 1.4 copy-done.1
  358.8 0.0 copy-start.8
  358.8 0.0 slice-start.4
  358.8 1.7 copy.57
  360.5 0.0 copy-done
  360.5 0.0 copy-start.7
  360.5 0.0 slice-start.5
  360.5 0.0 slice-start.2
  360.5 1.7 copy.58
  362.2 0.0 copy-done.8
  362.2 0.0 copy-start.6
  362.2 1.0 copy.59
  363.2 0.8 copy-done.7
  364.0 1.0 copy.60
  365.0 0.0 copy-done.6
  365.0 0.0 slice-start.3
  365.0 1.0 copy.61
  365.9 0.0 slice-done.4
  365.9 0.0 slice-done.5
  365.9 0.0 slice-start
  365.9 2.7 copy.62
  368.7 0.0 slice-done.2
  368.7 0.0 slice-done.3
  368.7 0.0 slice-start.1
  368.7 2.7 copy.63
  371.4 0.9 slice-done
  372.3 0.3 slice-done.1
  372.6 2.7 copy.64
  375.4 1.0 copy-done.5
  376.3 0.0 copy-start.4
  376.3 1.5 copy.65
  377.9 1.2 copy-done.4
  379.1 0.0 copy-start.3
  379.1 1.5 copy.66
  380.6 1.2 copy-done.3
  381.8 0.0 copy-start.12
  381.8 0.0 copy-start.11
  381.8 1.5 copy.67
  383.3 0.0 copy-done.12
  383.3 0.6 copy.68
  383.9 0.0 copy-done.11
  383.9 0.6 copy.69
  384.5 0.0 copy-done.10
  384.5 0.6 copy.70
  (9 shorter events, 0.0 us)
Async XLA Ops:
  1.7 53.0 %copy-start.9 = (s32[4,1]{0,1:T(1,128)}, s32[4,1]{0,1:T(1,128)S(1)}, u32[]{:S(2)}) copy-start(s32[4,1]{0,1:T(1,128)S(1)} %reduce-window.8) | copy-start | bytes 52
  351.1 4.7 %copy-start.2 = (f32[3,512,512]{2,1,0:T(8,128)S(1)}, f32[3,512,512]{2,1,0:T(8,128)}, u32[]{:S(2)}) copy-start(f32[3,512,512]{2,1,0:T(8,128)} %get-tuple-element.68) | copy-start | bytes 9437188
  355.8 3.0 copy-start.1
  355.8 4.7 %copy-start = (f32[3,512,512]{2,1,0:T(8,128)S(1)}, f32[3,512,512]{2,1,0:T(8,128)}, u32[]{:S(2)}) copy-start(f32[3,512,512]{2,1,0:T(8,128)} %get-tuple-element.70) | copy-start | bytes 9437188
  358.8 3.3 copy-start.8
  358.8 7.1 %slice-start.4 = ((s8[5373952]{0:T(1024)(128)(4,1)}), s8[4194304]{0:T(1024)(128)(4,1)S(1)}, s32[]{:S(2)}) async-start(s8[5373952]{0:T(1024)(128)(4,1)} %bitcast.29), calls=%async_computation.4 | async-start | bytes 8388608
  360.5 3.5 copy-start.7
  360.5 5.4 %slice-start.5 = ((s8[5373952]{0:T(1024)(128)(4,1)}), s8[1179648]{0:T(1024)(128)(4,1)S(1)}, s32[]{:S(2)}) async-start(s8[5373952]{0:T(1024)(128)(4,1)} %bitcast.29), calls=%async_computation.5 | async-start | bytes 2359296
  360.5 8.2 %slice-start.2 = ((s8[5373952]{0:T(1024)(128)(4,1)}), s8[4194304]{0:T(1024)(128)(4,1)S(1)}, s32[]{:S(2)}) async-start(s8[5373952]{0:T(1024)(128)(4,1)} %bitcast.26), calls=%async_computation.2 | async-start | bytes 8388608
  362.2 2.8 copy-start.6
  365.0 3.7 slice-start.3
  365.9 6.4 %slice-start = ((s8[5373952]{0:T(1024)(128)(4,1)}), s8[4194304]{0:T(1024)(128)(4,1)S(1)}, s32[]{:S(2)}) async-start(s8[5373952]{0:T(1024)(128)(4,1)} %bitcast.23), calls=%async_computation | async-start | bytes 8388608
  368.7 3.9 %slice-start.1 = ((s8[5373952]{0:T(1024)(128)(4,1)}), s8[1179648]{0:T(1024)(128)(4,1)S(1)}, s32[]{:S(2)}) async-start(s8[5373952]{0:T(1024)(128)(4,1)} %bitcast.23), calls=%async_computation.1 | async-start | bytes 2359296
  372.6 3.7 copy-start.5
  376.3 2.7 copy-start.4
  379.1 2.7 copy-start.3
  381.8 1.5 copy-start.12
  381.8 2.1 copy-start.11
  381.8 2.7 copy-start.10
